TPU v7x, 32 devices: a whole 2x2x4 slice. The times are simulated.
32 devices in a mesh: row: 4 (over z), col: 2 (over x), rep: 4 (over y, core).
Axes of the slice: x: 2, y: 2, z: 4, core: 2. Of those that a mesh axis runs over, the one named last changes fastest.
Arguments:
- tensor_tiles: bfloat16 [64, 4, 128, 128], P(('row', 'col', 'rep')), may hold values from -12 to 12
- tile_pairs: int32 [64], P(('row', 'col', 'rep')), may hold values from 0 to 1, as said below
- tile_counts: int32 [32], P(('row', 'col', 'rep')), may hold values from 1 to 2, as said below
- occupied: bfloat16 [1024, 1024], P(('col', 'rep'), 'row'), as said below
- virtual: bfloat16 [1024, 1024], P(('col', 'rep'), 'row'), as said below
Outputs:
- polar: float32 [4, 4], replicated
- dressed: bfloat16 [1024, 4, 1024], P(('col', 'rep'), None, 'row')
Inputs may be any that keep to these rules, and one draw needn't show every extreme that they name: `tile_pairs`: the 2 entries of one block are distinct: a permutation of its tile pairs. `tile_counts`: some block has all 2 entries live. `occupied`: Symmetric. `virtual`: Symmetric.
All inputs are finite; a program needn't handle non-finite values.
Results may differ from a plain program's by a relative error of at most 0.0049.
Values may be sent and summed in bfloat16 or wider, within the bound.
No kernel may reach another device: no remote copies, remote signals or barrier semaphores. Data moves between devices by JAX's collectives and lax.ppermute only.
A program may use at most 128 MiB of HBM per device.

v0:
```python
import functools

import jax
import jax.numpy as jnp
from jax import lax
from jax.experimental import pallas as pl
from jax.experimental.pallas import tpu as pltpu
from jax.sharding import PartitionSpec as P

PLANE = ("col", "rep")
EVERY = ("row", "col", "rep")
VMEM = pl.BlockSpec(memory_space=pltpu.VMEM)
SMEM = pl.BlockSpec(memory_space=pltpu.SMEM)
ROOM = 48 << 20


def flip(value, axes, mask, count):
    return lax.ppermute(value, axes, [(i, i ^ mask) for i in range(count)])


def after(value, earlier):
    return lax.optimization_barrier((value, earlier))


def gather_row(value, n_row):
    found = {0: value}
    step = n_row // 2
    while step:
        found.update({k ^ step: flip(held, "row", step, n_row) for k, held in list(found.items())})
        step //= 2
    return [found[k] for k in range(n_row)]


def late(n_row):
    return list(range(3, n_row, 2))


def plane_index():
    return lax.axis_index("col") * lax.axis_size("rep") + lax.axis_index("rep")


def place_kernel(nu_tiles, counts_ref, pairs_any, tiles_any, weight_any, column_any, *refs):
    line_ref, bundle_ref, pairs_ref, tiles_ref, sems = refs
    slots, aux, tile, _ = tiles_ref.shape
    cut = line_ref.shape[0] - 1
    copies = [
        pltpu.make_async_copy(source, target, sems.at[i])
        for i, (source, target) in enumerate(
            [
                (tiles_any, tiles_ref),
                (pairs_any, pairs_ref),
                (weight_any, line_ref.at[cut]),
                (column_any, bundle_ref.at[aux - cut]),
            ]
        )
    ]
    for copy in copies:
        copy.start()
    for copy in copies:
        copy.wait()
    for t in range(slots):
        pair = pairs_ref[t]
        rows = pl.ds(pl.multiple_of(pair // nu_tiles * tile, tile), tile)
        cols = pl.ds(pl.multiple_of(pair % nu_tiles * tile, tile), tile)

        @pl.when(t < counts_ref[0])
        def _():
            line_ref[:cut, rows, cols] = tiles_ref[t, :cut]
            bundle_ref[: aux - cut, rows, cols] = tiles_ref[t, cut:]

        @pl.when(t >= counts_ref[0])
        def _():
            line_ref[:cut, rows, cols] = jnp.zeros((cut, tile, tile), line_ref.dtype)
            bundle_ref[: aux - cut, rows, cols] = jnp.zeros((aux - cut, tile, tile), line_ref.dtype)


def place(tile_pairs, tile_counts, tensor_tiles, weight, column):
    slots, aux, tile, _ = tensor_tiles.shape
    mu, nu = weight.shape
    cut = aux // 2
    stays = [
        pltpu.with_memory_space_constraint(value, pltpu.HBM) for value in (tile_pairs, tensor_tiles, weight, column)
    ]
    return pl.pallas_call(
        functools.partial(place_kernel, nu // tile),
        out_shape=[jax.ShapeDtypeStruct((count + 1, mu, nu), weight.dtype) for count in (cut, aux - cut)],
        in_specs=[SMEM] + [pl.BlockSpec(memory_space=pltpu.HBM)] * 4,
        out_specs=[VMEM, VMEM],
        scratch_shapes=[
            pltpu.SMEM(tile_pairs.shape, tile_pairs.dtype),
            pltpu.VMEM(tensor_tiles.shape, tensor_tiles.dtype),
            pltpu.SemaphoreType.DMA((4,)),
        ],
        compiler_params=pltpu.CompilerParams(vmem_limit_bytes=ROOM),
        cost_estimate=pl.CostEstimate(flops=0, bytes_accessed=6 * tensor_tiles.size, transcendentals=0),
        name="place",
    )(tile_counts, *stays)


def dot(left, right):
    return jnp.dot(left, right, preferred_element_type=jnp.float32)


def mix_kernel(n_row, n_plane, *refs):
    lines, bundles = refs[:n_row], refs[n_row : n_row + n_plane]
    half_ref, mixed_ref, both_ref, weight_ref, panel_ref = refs[n_row + n_plane :]
    planes, mu, nu = lines[0].shape
    cut, rest = planes - 1, bundles[0].shape[0] - 1
    row, plane = lax.axis_index("row"), plane_index()
    for k in range(n_plane):
        panel_ref[pl.ds(pl.multiple_of((plane ^ k) * mu, mu), mu), :] = bundles[k][rest]
    for k in range(n_row):
        weight_ref[:, pl.ds(pl.multiple_of((row ^ k) * nu, nu), nu)] = lines[k][cut]
    for p in range(cut):
        total = jnp.zeros((mu, nu), jnp.float32)
        for k in range(n_row):
            at = pl.multiple_of((row ^ k) * nu, nu)
            total += dot(lines[k][p], panel_ref[pl.ds(at, nu), :])
        half_ref[:, p * nu : (p + 1) * nu] = total.astype(half_ref.dtype)
    for p in range(rest):
        total = jnp.zeros((mu, nu), jnp.float32)
        for k in range(n_plane):
            at = pl.multiple_of((plane ^ k) * mu, mu)
            total += dot(weight_ref[:, pl.ds(at, mu)], bundles[k][p])
        mixed_ref[:, p * nu : (p + 1) * nu] = total.astype(mixed_ref.dtype)
        both_ref[:, p * nu : (p + 1) * nu] = total.astype(both_ref.dtype)
        for i, k in enumerate(late(n_row)):
            at = pl.multiple_of((row ^ k) * nu, nu)
            turned = lax.dot_general(
                bundles[0][p], panel_ref[pl.ds(at, nu), :], (((1,), (1,)), ((), ())), preferred_element_type=jnp.float32
            )
            place_at = ((i + 1) * rest + p) * nu
            both_ref[:, place_at : place_at + nu] = turned.astype(both_ref.dtype)


def mix(lines, bundles):
    planes, mu, nu = lines[0].shape
    cut, rest = planes - 1, bundles[0].shape[0] - 1
    n_row, n_plane = len(lines), len(bundles)
    kind = lines[0].dtype
    return pl.pallas_call(
        functools.partial(mix_kernel, n_row, n_plane),
        out_shape=(
            jax.ShapeDtypeStruct((mu, cut * nu), kind),
            jax.ShapeDtypeStruct((mu, rest * nu), kind),
            jax.ShapeDtypeStruct((mu, (1 + len(late(n_row))) * rest * nu), kind),
            jax.ShapeDtypeStruct((mu, n_row * nu), kind),
            jax.ShapeDtypeStruct((n_plane * mu, nu), kind),
        ),
        in_specs=[VMEM] * (n_row + n_plane),
        out_specs=[VMEM] * 5,
        compiler_params=pltpu.CompilerParams(vmem_limit_bytes=ROOM),
        cost_estimate=pl.CostEstimate(
            flops=2 * (cut + rest) * mu * nu * nu * n_row,
            bytes_accessed=4 * n_row * (cut + rest) * mu * nu,
            transcendentals=0,
        ),
        name="mix",
    )(*lines, *bundles)


def share_kernel(n_row, n_plane, weight_ref, panel_ref, line_ref, bundle_ref, near_ref, *refs):
    halves, far = refs[:n_plane], refs[n_plane : n_plane + n_row // 2]
    first_ref, part_ref, share_ref = refs[n_plane + n_row // 2 :]
    cut, mu, nu = first_ref.shape
    rest = part_ref.shape[0]
    aux = cut + rest
    row, plane = lax.axis_index("row"), plane_index()
    known = {2 * i: ref for i, ref in enumerate(far)}
    known[1] = near_ref

    def product(left, right):
        folded = jnp.sum((left.astype(jnp.float32) * right).reshape(mu // 8, 8, nu), axis=0)
        return sum([folded[:, i : i + 128] for i in range(128, nu, 128)], folded[:, :128])

    def store(p, q, value):
        share_ref[p : p + 1, q * 128 : (q + 1) * 128] = jnp.sum(value, axis=0, keepdims=True)

    for q in range(cut):
        total = jnp.zeros((mu, nu), jnp.float32)
        for k in range(n_plane):
            at = pl.multiple_of((plane ^ k) * mu, mu)
            total += dot(weight_ref[:, pl.ds(at, mu)], halves[k][:, q * nu : (q + 1) * nu])
        rounded = total.astype(first_ref.dtype)
        first_ref[q] = rounded
        for p in range(aux):
            value = product(line_ref[p] if p < cut else bundle_ref[p - cut], rounded.astype(jnp.float32))
            store(p, q, value)
            if p >= cut:
                store(q, p, value)
    for q in range(rest):
        total = jnp.zeros((mu, nu), jnp.float32)
        for k, ref in known.items():
            at = pl.multiple_of((row ^ k) * nu, nu)
            total += dot(ref[:, q * nu : (q + 1) * nu], panel_ref[pl.ds(at, nu), :])
        part_ref[q] = total
        for p in range(rest):
            value = product(bundle_ref[p], total)
            for i, k in enumerate(late(n_row)):
                at = ((i + 1) * rest + p) * nu
                other = known[k ^ 1][:, q * nu : (q + 1) * nu]
                value += product(near_ref[:, at : at + nu], other.astype(jnp.float32))
            store(cut + p, cut + q, value)


def share_of(weight, panel, line, bundle, near, halves, far):
    planes, mu, nu = line.shape
    cut, rest = planes - 1, bundle.shape[0] - 1
    n_row, n_plane = 2 * len(far), len(halves)
    return pl.pallas_call(
        functools.partial(share_kernel, n_row, n_plane),
        out_shape=(
            jax.ShapeDtypeStruct((cut, mu, nu), line.dtype),
            jax.ShapeDtypeStruct((rest, mu, nu), jnp.float32),
            jax.ShapeDtypeStruct((cut + rest, (cut + rest) * 128), jnp.float32),
        ),
        in_specs=[VMEM] * (5 + n_plane + len(far)),
        out_specs=[VMEM] * 3,
        compiler_params=pltpu.CompilerParams(vmem_limit_bytes=ROOM),
        cost_estimate=pl.CostEstimate(
            flops=2 * (cut + rest) * mu * mu * nu * n_plane,
            bytes_accessed=4 * n_plane * (cut + rest) * mu * nu,
            transcendentals=0,
        ),
        name="polar_share",
    )(weight, panel, line, bundle, near, *halves, *far)


def dress_kernel(n_row, panel_ref, first_ref, part_ref, *refs):
    blocks, out_ref = refs[:-1], refs[-1]
    cut, _, nu = first_ref.shape
    row = lax.axis_index("row")
    for q in range(cut):
        out_ref[:, q, :] = first_ref[q]
    for q in range(part_ref.shape[0]):
        total = part_ref[q]
        for k, ref in zip(late(n_row), blocks):
            at = pl.multiple_of((row ^ k) * nu, nu)
            total += dot(ref[:, q * nu : (q + 1) * nu], panel_ref[pl.ds(at, nu), :])
        out_ref[:, cut + q, :] = total.astype(out_ref.dtype)


def dress(panel, first, part, blocks, n_row):
    cut, mu, nu = first.shape
    aux = cut + part.shape[0]
    return pl.pallas_call(
        functools.partial(dress_kernel, n_row),
        out_shape=jax.ShapeDtypeStruct((mu, aux, nu), first.dtype),
        in_specs=[VMEM] * (3 + len(blocks)),
        out_specs=VMEM,
        compiler_params=pltpu.CompilerParams(vmem_limit_bytes=ROOM),
        cost_estimate=pl.CostEstimate(flops=2 * mu * nu * nu * aux, bytes_accessed=8 * mu * aux * nu, transcendentals=0),
        name="dress",
    )(panel, first, part, *blocks)


def finish_kernel(total_ao, first_ref, second_ref, out_ref):
    aux = out_ref.shape[0]
    for q in range(aux):
        lanes = pl.ds(q * 128, 128)
        share = first_ref[:, lanes] + second_ref[:, lanes]
        out_ref[:, q : q + 1] = jnp.sum(share, axis=1, keepdims=True) / total_ao


def finish(first, second, total_ao):
    aux = first.shape[0]
    return pl.pallas_call(
        functools.partial(finish_kernel, total_ao),
        out_shape=jax.ShapeDtypeStruct((aux, aux), jnp.float32),
        in_specs=[VMEM, VMEM],
        out_specs=VMEM,
        compiler_params=pltpu.CompilerParams(vmem_limit_bytes=ROOM),
        name="finish",
    )(first, second)


def on_device(tensor_tiles, tile_pairs, tile_counts, occupied, virtual):
    aux = tensor_tiles.shape[1]
    n_row, n_plane = lax.axis_size("row"), lax.axis_size("col") * lax.axis_size("rep")
    near = list(range(2, n_plane, 2))
    sibling = lambda value: flip(value, PLANE, 1, n_plane)

    def gather_plane(value):
        values = [value] + [flip(value, PLANE, k, n_plane) for k in near]
        return [held for value in values for held in (value, sibling(value))]

    line, bundle = place(tile_pairs, tile_counts, tensor_tiles, occupied, virtual)
    half, mixed, both, weight, panel = mix(gather_row(line, n_row), gather_plane(bundle))
    far = {0: mixed}
    step = n_row // 2
    while step > 1:
        far.update({k ^ step: flip(held, "row", step, n_row) for k, held in list(far.items())})
        step //= 2
    beside = flip(both, "row", 1, n_row)
    blocks = [flip(far[k ^ 1], "row", 1, n_row) for k in late(n_row)]
    first, part, share = share_of(
        weight, panel, line, bundle, beside, gather_plane(half), [far[k] for k in range(0, n_row, 2)]
    )
    step = 1
    while step < n_plane:
        share = share + flip(share, PLANE, step, n_plane)
        step *= 2
    step = 1
    while 2 * step < n_row:
        share = share + flip(share, "row", step, n_row)
        step *= 2
    last, dressed = after(flip(share, "row", step, n_row), dress(panel, first, part, blocks, n_row))
    polar = finish(share, last, weight.shape[1])
    return polar, dressed


def solution(mesh):
    return jax.shard_map(
        on_device,
        mesh=mesh,
        in_specs=(P(EVERY, None, None, None), P(EVERY), P(EVERY), P(PLANE, "row"), P(PLANE, "row")),
        out_specs=(P(), P(PLANE, None, "row")),
        check_vma=False,
    )
```

profile of v0, /device:TPU:0, one launch (start us, length us, event | category | flops | bytes accessed | tf_op | source)
XLA Modules:
  0.0 56.1 jit_solution(3649030611100950309)
XLA Ops:
  1.3 1.1 %place.1 = (bf16[3,128,256]{2,1,0:T(8,128)(2,1)S(1)}, bf16[3,128,256]{2,1,0:T(8,128)(2,1)S(1)}) custom-call(s32[1]{0:T(128)S(6)} %copy.7.counts_ref, s32[2]{0:T(128)} %pairs_any.1, bf16[2,4,128,128]{3,2,1,0:T(8,128)(2,1)} %tiles_any.1, bf16[128,256]{1,0:T(8,128)(2,1)} %weight_any.1, bf16[128,256]{1,0:T(8,128)(2,1)} %column_any.1), custom_call_target="tpu_custom_call" | custom-call | bytes 786432 | tf_op jit(solution)/shard_map/place/pallas_call | solution.py:84
  2.4 4.1 %collective-permute-start.1 = (bf16[3,128,256]{2,1,0:T(8,128)(2,1)S(1)}, bf16[3,128,256]{2,1,0:T(8,128)(2,1)S(1)}, u32[]{:S(2)}, u32[]{:S(2)}) collective-permute-start(bf16[3,128,256]{2,1,0:T(8,128)(2,1)S(1)} %get-tuple-element.14.refs_0_.line_ref), channel_id=1, source_target_pairs={{0,16},{8,24},{16,0},{24,8},{1,17},{9,25},{17,1},{25,9},{2,18},{10... | collective-permute-start | bytes 589832 | tf_op jit(solution)/shard_map/ppermute | solution.py:18
  6.5 1.6 %collective-permute-start = (bf16[3,128,256]{2,1,0:T(8,128)(2,1)S(1)}, bf16[3,128,256]{2,1,0:T(8,128)(2,1)S(1)}, u32[]{:S(2)}, u32[]{:S(2)}) collective-permute-start(bf16[3,128,256]{2,1,0:T(8,128)(2,1)S(1)} %get-tuple-element.14.refs_0_.line_ref), channel_id=1, source_target_pairs={{0,8},{8,0},{16,24},{24,16},{1,9},{9,1},{17,25},{25,17},{2,10},{10... | collective-permute-start | bytes 589832 | tf_op jit(solution)/shard_map/ppermute | solution.py:18
  8.0 2.4 %collective-permute-start.8 = (bf16[3,128,256]{2,1,0:T(8,128)(2,1)S(1)}, bf16[3,128,256]{2,1,0:T(8,128)(2,1)S(1)}, u32[]{:S(2)}, u32[]{:S(2)}) collective-permute-start(bf16[3,128,256]{2,1,0:T(8,128)(2,1)S(1)} %get-tuple-element.15.refs_4_.bundle_ref), channel_id=1, source_target_pairs={{0,6},{1,7},{2,4},{3,5},{4,2},{5,3},{6,0},{7,1},{8,14},{9,15},{10,... | collective-permute-start | bytes 589832 | tf_op jit(solution)/shard_map/ppermute | solution.py:18
  11.5 4.2 %collective-permute-done.1.refs_2_ = bf16[3,128,256]{2,1,0:T(8,128)(2,1)S(1)} collective-permute-done((bf16[3,128,256]{2,1,0:T(8,128)(2,1)S(1)}, bf16[3,128,256]{2,1,0:T(8,128)(2,1)S(1)}, u32[]{:S(2)}, u32[]{:S(2)}) %collective-permute-start.1) | collective-permute-done | bytes 196640 | tf_op jit(solution)/shard_map/ppermute | solution.py:18
  15.9 1.5 %collective-permute-start.2 = (bf16[3,128,256]{2,1,0:T(8,128)(2,1)S(1)}, bf16[3,128,256]{2,1,0:T(8,128)(2,1)S(1)}, u32[]{:S(2)}, u32[]{:S(2)}) collective-permute-start(bf16[3,128,256]{2,1,0:T(8,128)(2,1)S(1)} %collective-permute-done.1.refs_2_), channel_id=1, source_target_pairs={{0,8},{8,0},{16,24},{24,16},{1,9},{9,1},{17,25},{25,17},{2,10},{10... | collective-permute-start | bytes 589832 | tf_op jit(solution)/shard_map/ppermute | solution.py:18
  17.4 2.0 %collective-permute-done.6.refs_8_ = bf16[3,128,256]{2,1,0:T(8,128)(2,1)S(1)} collective-permute-done((bf16[3,128,256]{2,1,0:T(8,128)(2,1)S(1)}, bf16[3,128,256]{2,1,0:T(8,128)(2,1)S(1)}, u32[]{:S(2)}, u32[]{:S(2)}) %collective-permute-start.6) | collective-permute-done | bytes 196640 | tf_op jit(solution)/shard_map/ppermute | solution.py:18
  19.8 3.2 %collective-permute-done.2.refs_3_ = bf16[3,128,256]{2,1,0:T(8,128)(2,1)S(1)} collective-permute-done((bf16[3,128,256]{2,1,0:T(8,128)(2,1)S(1)}, bf16[3,128,256]{2,1,0:T(8,128)(2,1)S(1)}, u32[]{:S(2)}, u32[]{:S(2)}) %collective-permute-start.2) | collective-permute-done | bytes 196640 | tf_op jit(solution)/shard_map/ppermute | solution.py:18
  23.7 2.3 %collective-permute-start.18 = (bf16[128,512]{1,0:T(8,128)(2,1)S(1)}, bf16[128,512]{1,0:T(8,128)(2,1)S(1)}, u32[]{:S(2)}, u32[]{:S(2)}) collective-permute-start(bf16[128,512]{1,0:T(8,128)(2,1)S(1)} %get-tuple-element.20.refs_8_), channel_id=1, source_target_pairs={{0,16},{8,24},{16,0},{24,8},{1,17},{9,25},{17,1},{25,9},{2,18},{10... | collective-permute-start | bytes 393224 | tf_op jit(solution)/shard_map/ppermute | solution.py:18
  26.1 2.5 %collective-permute-start.16 = (bf16[128,512]{1,0:T(8,128)(2,1)S(1)}, bf16[128,512]{1,0:T(8,128)(2,1)S(1)}, u32[]{:S(2)}, u32[]{:S(2)}) collective-permute-start(bf16[128,512]{1,0:T(8,128)(2,1)S(1)} %get-tuple-element.19.refs_0_), channel_id=1, source_target_pairs={{0,6},{1,7},{2,4},{3,5},{4,2},{5,3},{6,0},{7,1},{8,14},{9,15},{10,... | collective-permute-start | bytes 393224 | tf_op jit(solution)/shard_map/ppermute | solution.py:18
  29.5 1.7 %collective-permute-start.10 = (bf16[128,1024]{1,0:T(8,128)(2,1)S(1)}, bf16[128,1024]{1,0:T(8,128)(2,1)S(1)}, u32[]{:S(2)}, u32[]{:S(2)}) collective-permute-start(bf16[128,1024]{1,0:T(8,128)(2,1)S(1)} %get-tuple-element.18), channel_id=1, source_target_pairs={{0,8},{8,0},{16,24},{24,16},{1,9},{9,1},{17,25},{25,17},{2,10},{10... | collective-permute-start | bytes 786440 | tf_op jit(solution)/shard_map/ppermute | solution.py:18
  31.3 1.3 %collective-permute-done.18.refs_9_ = bf16[128,512]{1,0:T(8,128)(2,1)S(1)} collective-permute-done((bf16[128,512]{1,0:T(8,128)(2,1)S(1)}, bf16[128,512]{1,0:T(8,128)(2,1)S(1)}, u32[]{:S(2)}, u32[]{:S(2)}) %collective-permute-start.18) | collective-permute-done | bytes 131104 | tf_op jit(solution)/shard_map/ppermute | solution.py:18
  33.4 1.5 %collective-permute-done.14.refs_4_ = bf16[128,512]{1,0:T(8,128)(2,1)S(1)} collective-permute-done((bf16[128,512]{1,0:T(8,128)(2,1)S(1)}, bf16[128,512]{1,0:T(8,128)(2,1)S(1)}, u32[]{:S(2)}, u32[]{:S(2)}) %collective-permute-start.14) | collective-permute-done | bytes 131104 | tf_op jit(solution)/shard_map/ppermute | solution.py:18
  35.4 1.5 %collective-permute-start.24 = (bf16[128,512]{1,0:T(8,128)(2,1)S(1)}, bf16[128,512]{1,0:T(8,128)(2,1)S(1)}, u32[]{:S(2)}, u32[]{:S(2)}) collective-permute-start(bf16[128,512]{1,0:T(8,128)(2,1)S(1)} %collective-permute-done.18.refs_9_), channel_id=1, source_target_pairs={{0,8},{8,0},{16,24},{24,16},{1,9},{9,1},{17,25},{25,17},{2,10},{10... | collective-permute-start | bytes 393224 | tf_op jit(solution)/shard_map/ppermute | solution.py:18
  36.9 1.1 %collective-permute-done.10.near_ref = bf16[128,1024]{1,0:T(8,128)(2,1)S(1)} collective-permute-done((bf16[128,1024]{1,0:T(8,128)(2,1)S(1)}, bf16[128,1024]{1,0:T(8,128)(2,1)S(1)}, u32[]{:S(2)}, u32[]{:S(2)}) %collective-permute-start.10) | collective-permute-done | bytes 262176 | tf_op jit(solution)/shard_map/ppermute | solution.py:18
  38.7 1.2 %collective-permute-done.19 = f32[4,512]{1,0:T(4,128)S(1)} collective-permute-done((f32[4,512]{1,0:T(4,128)S(1)}, f32[4,512]{1,0:T(4,128)S(1)}, u32[]{:S(2)}, u32[]{:S(2)}) %collective-permute-start.19) | collective-permute-done | bytes 8224 | tf_op jit(solution)/shard_map/ppermute | solution.py:18
  39.9 1.7 %collective-permute-start.20 = (f32[4,512]{1,0:T(4,128)S(1)}, f32[4,512]{1,0:T(4,128)S(1)}, u32[]{:S(2)}, u32[]{:S(2)}) collective-permute-start(f32[4,512]{1,0:T(4,128)S(1)} %add.12), channel_id=1, source_target_pairs={{0,2},{1,3},{2,0},{3,1},{4,6},{5,7},{6,4},{7,5},{8,10},{9,11},{10,... | collective-permute-start | bytes 24584 | tf_op jit(solution)/shard_map/ppermute | solution.py:18
  41.6 2.0 %collective-permute-done.20 = f32[4,512]{1,0:T(4,128)S(1)} collective-permute-done((f32[4,512]{1,0:T(4,128)S(1)}, f32[4,512]{1,0:T(4,128)S(1)}, u32[]{:S(2)}, u32[]{:S(2)}) %collective-permute-start.20) | collective-permute-done | bytes 8224 | tf_op jit(solution)/shard_map/ppermute | solution.py:18
  43.6 1.5 %collective-permute-start.21 = (f32[4,512]{1,0:T(4,128)S(1)}, f32[4,512]{1,0:T(4,128)S(1)}, u32[]{:S(2)}, u32[]{:S(2)}) collective-permute-start(f32[4,512]{1,0:T(4,128)S(1)} %add.13), channel_id=1, source_target_pairs={{0,4},{1,5},{2,6},{3,7},{4,0},{5,1},{6,2},{7,3},{8,12},{9,13},{10,... | collective-permute-start | bytes 24584 | tf_op jit(solution)/shard_map/ppermute | solution.py:18
  45.1 2.1 %collective-permute-done.21 = f32[4,512]{1,0:T(4,128)S(1)} collective-permute-done((f32[4,512]{1,0:T(4,128)S(1)}, f32[4,512]{1,0:T(4,128)S(1)}, u32[]{:S(2)}, u32[]{:S(2)}) %collective-permute-start.21) | collective-permute-done | bytes 8224 | tf_op jit(solution)/shard_map/ppermute | solution.py:18
  47.2 3.6 %collective-permute-done.22 = f32[4,512]{1,0:T(4,128)S(1)} collective-permute-done((f32[4,512]{1,0:T(4,128)S(1)}, f32[4,512]{1,0:T(4,128)S(1)}, u32[]{:S(2)}, u32[]{:S(2)}) %collective-permute-start.22) | collective-permute-done | bytes 8224 | tf_op jit(solution)/shard_map/ppermute | solution.py:18
  50.9 1.4 %collective-permute-start.23 = (f32[4,512]{1,0:T(4,128)S(1)}, f32[4,512]{1,0:T(4,128)S(1)}, u32[]{:S(2)}, u32[]{:S(2)}) collective-permute-start(f32[4,512]{1,0:T(4,128)S(1)} %add.15.first_ref), channel_id=1, source_target_pairs={{0,16},{8,24},{16,0},{24,8},{1,17},{9,25},{17,1},{25,9},{2,18},{10... | collective-permute-start | bytes 24584 | tf_op jit(solution)/shard_map/ppermute | solution.py:18
  52.3 1.3 %dress.1 = bf16[128,4,256]{2,1,0:T(4,128)(2,1)} custom-call(bf16[1024,256]{1,0:T(8,128)(2,1)S(1)} %get-tuple-element.17.panel_ref, bf16[2,128,256]{2,1,0:T(8,128)(2,1)S(1)} %get-tuple-element.22.first_ref, f32[2,128,256]{2,1,0:T(8,128)S(1)} %get-tuple-element.23.part_ref, bf16[128,512]{1,0:T(8,128)(2,1)S(1)} %collective-permute-done.24.refs_0_), custom_call_target="tpu_custom_call" | custom-call | flops 67108864 | bytes 1048576 | tf_op jit(solution)/shard_map/dress/pallas_call | solution.py:246
  53.6 1.9 %collective-permute-done.23.second_ref = f32[4,512]{1,0:T(4,128)S(1)} collective-permute-done((f32[4,512]{1,0:T(4,128)S(1)}, f32[4,512]{1,0:T(4,128)S(1)}, u32[]{:S(2)}, u32[]{:S(2)}) %collective-permute-start.23) | collective-permute-done | bytes 8224 | tf_op jit(solution)/shard_map/ppermute | solution.py:18
  (35 shorter events, 6.2 us)
Async XLA Ops:
  2.4 13.3 %collective-permute-start.1 = (bf16[3,128,256]{2,1,0:T(8,128)(2,1)S(1)}, bf16[3,128,256]{2,1,0:T(8,128)(2,1)S(1)}, u32[]{:S(2)}, u32[]{:S(2)}) collective-permute-start(bf16[3,128,256]{2,1,0:T(8,128)(2,1)S(1)} %get-tuple-element.14.refs_0_.line_ref), channel_id=1, source_target_pairs={{0,16},{8,24},{16,0},{24,8},{1,17},{9,25},{17,1},{25,9},{2,18},{10... | collective-permute-start | bytes 589832 | tf_op jit(solution)/shard_map/ppermute | solution.py:18
  6.5 9.4 %collective-permute-start = (bf16[3,128,256]{2,1,0:T(8,128)(2,1)S(1)}, bf16[3,128,256]{2,1,0:T(8,128)(2,1)S(1)}, u32[]{:S(2)}, u32[]{:S(2)}) collective-permute-start(bf16[3,128,256]{2,1,0:T(8,128)(2,1)S(1)} %get-tuple-element.14.refs_0_.line_ref), channel_id=1, source_target_pairs={{0,8},{8,0},{16,24},{24,16},{1,9},{9,1},{17,25},{25,17},{2,10},{10... | collective-permute-start | bytes 589832 | tf_op jit(solution)/shard_map/ppermute | solution.py:18
  8.0 9.3 %collective-permute-start.8 = (bf16[3,128,256]{2,1,0:T(8,128)(2,1)S(1)}, bf16[3,128,256]{2,1,0:T(8,128)(2,1)S(1)}, u32[]{:S(2)}, u32[]{:S(2)}) collective-permute-start(bf16[3,128,256]{2,1,0:T(8,128)(2,1)S(1)} %get-tuple-element.15.refs_4_.bundle_ref), channel_id=1, source_target_pairs={{0,6},{1,7},{2,4},{3,5},{4,2},{5,3},{6,0},{7,1},{8,14},{9,15},{10,... | collective-permute-start | bytes 589832 | tf_op jit(solution)/shard_map/ppermute | solution.py:18
  10.5 8.8 %collective-permute-start.6 = (bf16[3,128,256]{2,1,0:T(8,128)(2,1)S(1)}, bf16[3,128,256]{2,1,0:T(8,128)(2,1)S(1)}, u32[]{:S(2)}, u32[]{:S(2)}) collective-permute-start(bf16[3,128,256]{2,1,0:T(8,128)(2,1)S(1)} %get-tuple-element.15.refs_4_.bundle_ref), channel_id=1, source_target_pairs={{0,4},{1,5},{2,6},{3,7},{4,0},{5,1},{6,2},{7,3},{8,12},{9,13},{10,... | collective-permute-start | bytes 589832 | tf_op jit(solution)/shard_map/ppermute | solution.py:18
  11.0 8.3 %collective-permute-start.4 = (bf16[3,128,256]{2,1,0:T(8,128)(2,1)S(1)}, bf16[3,128,256]{2,1,0:T(8,128)(2,1)S(1)}, u32[]{:S(2)}, u32[]{:S(2)}) collective-permute-start(bf16[3,128,256]{2,1,0:T(8,128)(2,1)S(1)} %get-tuple-element.15.refs_4_.bundle_ref), channel_id=1, source_target_pairs={{0,2},{1,3},{2,0},{3,1},{4,6},{5,7},{6,4},{7,5},{8,10},{9,11},{10,... | collective-permute-start | bytes 589832 | tf_op jit(solution)/shard_map/ppermute | solution.py:18
  15.7 4.2 %collective-permute-start.3 = (bf16[3,128,256]{2,1,0:T(8,128)(2,1)S(1)}, bf16[3,128,256]{2,1,0:T(8,128)(2,1)S(1)}, u32[]{:S(2)}, u32[]{:S(2)}) collective-permute-start(bf16[3,128,256]{2,1,0:T(8,128)(2,1)S(1)} %get-tuple-element.15.refs_4_.bundle_ref), channel_id=1, source_target_pairs={{0,1},{1,0},{2,3},{3,2},{4,5},{5,4},{6,7},{7,6},{8,9},{9,8},{10,11... | collective-permute-start | bytes 589832 | tf_op jit(solution)/shard_map/ppermute | solution.py:18
  15.9 7.1 %collective-permute-start.2 = (bf16[3,128,256]{2,1,0:T(8,128)(2,1)S(1)}, bf16[3,128,256]{2,1,0:T(8,128)(2,1)S(1)}, u32[]{:S(2)}, u32[]{:S(2)}) collective-permute-start(bf16[3,128,256]{2,1,0:T(8,128)(2,1)S(1)} %collective-permute-done.1.refs_2_), channel_id=1, source_target_pairs={{0,8},{8,0},{16,24},{24,16},{1,9},{9,1},{17,25},{25,17},{2,10},{10... | collective-permute-start | bytes 589832 | tf_op jit(solution)/shard_map/ppermute | solution.py:18
  17.4 5.6 %collective-permute-start.9 = (bf16[3,128,256]{2,1,0:T(8,128)(2,1)S(1)}, bf16[3,128,256]{2,1,0:T(8,128)(2,1)S(1)}, u32[]{:S(2)}, u32[]{:S(2)}) collective-permute-start(bf16[3,128,256]{2,1,0:T(8,128)(2,1)S(1)} %collective-permute-done.8.refs_10_), channel_id=1, source_target_pairs={{0,1},{1,0},{2,3},{3,2},{4,5},{5,4},{6,7},{7,6},{8,9},{9,8},{10,11... | collective-permute-start | bytes 589832 | tf_op jit(solution)/shard_map/ppermute | solution.py:18
  19.3 3.7 %collective-permute-start.7 = (bf16[3,128,256]{2,1,0:T(8,128)(2,1)S(1)}, bf16[3,128,256]{2,1,0:T(8,128)(2,1)S(1)}, u32[]{:S(2)}, u32[]{:S(2)}) collective-permute-start(bf16[3,128,256]{2,1,0:T(8,128)(2,1)S(1)} %collective-permute-done.6.refs_8_), channel_id=1, source_target_pairs={{0,1},{1,0},{2,3},{3,2},{4,5},{5,4},{6,7},{7,6},{8,9},{9,8},{10,11... | collective-permute-start | bytes 589832 | tf_op jit(solution)/shard_map/ppermute | solution.py:18
  19.3 3.7 %collective-permute-start.5 = (bf16[3,128,256]{2,1,0:T(8,128)(2,1)S(1)}, bf16[3,128,256]{2,1,0:T(8,128)(2,1)S(1)}, u32[]{:S(2)}, u32[]{:S(2)}) collective-permute-start(bf16[3,128,256]{2,1,0:T(8,128)(2,1)S(1)} %collective-permute-done.4.refs_6_), channel_id=1, source_target_pairs={{0,1},{1,0},{2,3},{3,2},{4,5},{5,4},{6,7},{7,6},{8,9},{9,8},{10,11... | collective-permute-start | bytes 589832 | tf_op jit(solution)/shard_map/ppermute | solution.py:18
  23.7 8.8 %collective-permute-start.18 = (bf16[128,512]{1,0:T(8,128)(2,1)S(1)}, bf16[128,512]{1,0:T(8,128)(2,1)S(1)}, u32[]{:S(2)}, u32[]{:S(2)}) collective-permute-start(bf16[128,512]{1,0:T(8,128)(2,1)S(1)} %get-tuple-element.20.refs_8_), channel_id=1, source_target_pairs={{0,16},{8,24},{16,0},{24,8},{1,17},{9,25},{17,1},{25,9},{2,18},{10... | collective-permute-start | bytes 393224 | tf_op jit(solution)/shard_map/ppermute | solution.py:18
  26.1 7.3 %collective-permute-start.16 = (bf16[128,512]{1,0:T(8,128)(2,1)S(1)}, bf16[128,512]{1,0:T(8,128)(2,1)S(1)}, u32[]{:S(2)}, u32[]{:S(2)}) collective-permute-start(bf16[128,512]{1,0:T(8,128)(2,1)S(1)} %get-tuple-element.19.refs_0_), channel_id=1, source_target_pairs={{0,6},{1,7},{2,4},{3,5},{4,2},{5,3},{6,0},{7,1},{8,14},{9,15},{10,... | collective-permute-start | bytes 393224 | tf_op jit(solution)/shard_map/ppermute | solution.py:18
  28.5 6.4 %collective-permute-start.14 = (bf16[128,512]{1,0:T(8,128)(2,1)S(1)}, bf16[128,512]{1,0:T(8,128)(2,1)S(1)}, u32[]{:S(2)}, u32[]{:S(2)}) collective-permute-start(bf16[128,512]{1,0:T(8,128)(2,1)S(1)} %get-tuple-element.19.refs_0_), channel_id=1, source_target_pairs={{0,4},{1,5},{2,6},{3,7},{4,0},{5,1},{6,2},{7,3},{8,12},{9,13},{10,... | collective-permute-start | bytes 393224 | tf_op jit(solution)/shard_map/ppermute | solution.py:18
  29.0 5.8 %collective-permute-start.12 = (bf16[128,512]{1,0:T(8,128)(2,1)S(1)}, bf16[128,512]{1,0:T(8,128)(2,1)S(1)}, u32[]{:S(2)}, u32[]{:S(2)}) collective-permute-start(bf16[128,512]{1,0:T(8,128)(2,1)S(1)} %get-tuple-element.19.refs_0_), channel_id=1, source_target_pairs={{0,2},{1,3},{2,0},{3,1},{4,6},{5,7},{6,4},{7,5},{8,10},{9,11},{10,... | collective-permute-start | bytes 393224 | tf_op jit(solution)/shard_map/ppermute | solution.py:18
  29.5 8.5 %collective-permute-start.10 = (bf16[128,1024]{1,0:T(8,128)(2,1)S(1)}, bf16[128,1024]{1,0:T(8,128)(2,1)S(1)}, u32[]{:S(2)}, u32[]{:S(2)}) collective-permute-start(bf16[128,1024]{1,0:T(8,128)(2,1)S(1)} %get-tuple-element.18), channel_id=1, source_target_pairs={{0,8},{8,0},{16,24},{24,16},{1,9},{9,1},{17,25},{25,17},{2,10},{10... | collective-permute-start | bytes 786440 | tf_op jit(solution)/shard_map/ppermute | solution.py:18
  32.6 2.8 %collective-permute-start.11 = (bf16[128,512]{1,0:T(8,128)(2,1)S(1)}, bf16[128,512]{1,0:T(8,128)(2,1)S(1)}, u32[]{:S(2)}, u32[]{:S(2)}) collective-permute-start(bf16[128,512]{1,0:T(8,128)(2,1)S(1)} %get-tuple-element.19.refs_0_), channel_id=1, source_target_pairs={{0,1},{1,0},{2,3},{3,2},{4,5},{5,4},{6,7},{7,6},{8,9},{9,8},{10,11... | collective-permute-start | bytes 393224 | tf_op jit(solution)/shard_map/ppermute | solution.py:18
  33.4 3.6 %collective-permute-start.17 = (bf16[128,512]{1,0:T(8,128)(2,1)S(1)}, bf16[128,512]{1,0:T(8,128)(2,1)S(1)}, u32[]{:S(2)}, u32[]{:S(2)}) collective-permute-start(bf16[128,512]{1,0:T(8,128)(2,1)S(1)} %collective-permute-done.16.refs_6_), channel_id=1, source_target_pairs={{0,1},{1,0},{2,3},{3,2},{4,5},{5,4},{6,7},{7,6},{8,9},{9,8},{10,11... | collective-permute-start | bytes 393224 | tf_op jit(solution)/shard_map/ppermute | solution.py:18
  34.9 2.1 %collective-permute-start.15 = (bf16[128,512]{1,0:T(8,128)(2,1)S(1)}, bf16[128,512]{1,0:T(8,128)(2,1)S(1)}, u32[]{:S(2)}, u32[]{:S(2)}) collective-permute-start(bf16[128,512]{1,0:T(8,128)(2,1)S(1)} %collective-permute-done.14.refs_4_), channel_id=1, source_target_pairs={{0,1},{1,0},{2,3},{3,2},{4,5},{5,4},{6,7},{7,6},{8,9},{9,8},{10,11... | collective-permute-start | bytes 393224 | tf_op jit(solution)/shard_map/ppermute | solution.py:18
  34.9 2.1 %collective-permute-start.13 = (bf16[128,512]{1,0:T(8,128)(2,1)S(1)}, bf16[128,512]{1,0:T(8,128)(2,1)S(1)}, u32[]{:S(2)}, u32[]{:S(2)}) collective-permute-start(bf16[128,512]{1,0:T(8,128)(2,1)S(1)} %collective-permute-done.12.refs_2_), channel_id=1, source_target_pairs={{0,1},{1,0},{2,3},{3,2},{4,5},{5,4},{6,7},{7,6},{8,9},{9,8},{10,11... | collective-permute-start | bytes 393224 | tf_op jit(solution)/shard_map/ppermute | solution.py:18
  35.4 16.9 %collective-permute-start.24 = (bf16[128,512]{1,0:T(8,128)(2,1)S(1)}, bf16[128,512]{1,0:T(8,128)(2,1)S(1)}, u32[]{:S(2)}, u32[]{:S(2)}) collective-permute-start(bf16[128,512]{1,0:T(8,128)(2,1)S(1)} %collective-permute-done.18.refs_9_), channel_id=1, source_target_pairs={{0,8},{8,0},{16,24},{24,16},{1,9},{9,1},{17,25},{25,17},{2,10},{10... | collective-permute-start | bytes 393224 | tf_op jit(solution)/shard_map/ppermute | solution.py:18
  39.9 3.7 %collective-permute-start.20 = (f32[4,512]{1,0:T(4,128)S(1)}, f32[4,512]{1,0:T(4,128)S(1)}, u32[]{:S(2)}, u32[]{:S(2)}) collective-permute-start(f32[4,512]{1,0:T(4,128)S(1)} %add.12), channel_id=1, source_target_pairs={{0,2},{1,3},{2,0},{3,1},{4,6},{5,7},{6,4},{7,5},{8,10},{9,11},{10,... | collective-permute-start | bytes 24584 | tf_op jit(solution)/shard_map/ppermute | solution.py:18
  43.6 3.7 %collective-permute-start.21 = (f32[4,512]{1,0:T(4,128)S(1)}, f32[4,512]{1,0:T(4,128)S(1)}, u32[]{:S(2)}, u32[]{:S(2)}) collective-permute-start(f32[4,512]{1,0:T(4,128)S(1)} %add.13), channel_id=1, source_target_pairs={{0,4},{1,5},{2,6},{3,7},{4,0},{5,1},{6,2},{7,3},{8,12},{9,13},{10,... | collective-permute-start | bytes 24584 | tf_op jit(solution)/shard_map/ppermute | solution.py:18
  47.2 3.7 %collective-permute-start.22 = (f32[4,512]{1,0:T(4,128)S(1)}, f32[4,512]{1,0:T(4,128)S(1)}, u32[]{:S(2)}, u32[]{:S(2)}) collective-permute-start(f32[4,512]{1,0:T(4,128)S(1)} %add.14), channel_id=1, source_target_pairs={{0,8},{8,0},{16,24},{24,16},{1,9},{9,1},{17,25},{25,17},{2,10},{10... | collective-permute-start | bytes 24584 | tf_op jit(solution)/shard_map/ppermute | solution.py:18
  50.9 4.6 %collective-permute-start.23 = (f32[4,512]{1,0:T(4,128)S(1)}, f32[4,512]{1,0:T(4,128)S(1)}, u32[]{:S(2)}, u32[]{:S(2)}) collective-permute-start(f32[4,512]{1,0:T(4,128)S(1)} %add.15.first_ref), channel_id=1, source_target_pairs={{0,16},{8,24},{16,0},{24,8},{1,17},{9,25},{17,1},{25,9},{2,18},{10... | collective-permute-start | bytes 24584 | tf_op jit(solution)/shard_map/ppermute | solution.py:18
  (1 other events, 1.2 us)
where the time goes:
time: 56.3 us; the launch traced here: 56.1 us
  starting transfers between devices  25.5 us (45%)
  waiting for transfers between devices  24.9 us (44%)
  Pallas kernels  4.32 us (8%)
  between operations  1.34 us (2%)
    ppermute x25, starting transfers between devices, flip(): return lax.ppermute(value, axes, [(i, i ^ mask) for i in range(count)])  25.5 us
    ppermute x25, waiting for transfers between devices, flip(): return lax.ppermute(value, axes, [(i, i ^ mask) for i in range(count)])  24.9 us
    pallas_call x1, Pallas kernels, dress(): pl.pallas_call(functools.partial(dress_kernel, n_row), out_shape=jax.Shap...  1.29 us
  transfers between devices with their start and end apart: 25, of which 13 were waited for; matrix products, arithmetic and copies ran while one was open for 0% of the time, Pallas kernels for 3%

commit v1 on v0

--- a/solution.py
+++ b/solution.py
@@ -173,8 +173,12 @@
         folded = jnp.sum((left.astype(jnp.float32) * right).reshape(mu // 8, 8, nu), axis=0)
         return sum([folded[:, i : i + 128] for i in range(128, nu, 128)], folded[:, :128])
 
+    lanes = lax.broadcasted_iota(jnp.int32, share_ref.shape[1:], 1)
+    shares = [jnp.zeros(share_ref.shape[1:], jnp.float32)]
+
     def store(p, q, value):
-        share_ref[p : p + 1, q * 128 : (q + 1) * 128] = jnp.sum(value, axis=0, keepdims=True)
+        total = jnp.sum(jnp.sum(value, axis=0, keepdims=True), axis=1, keepdims=True)
+        shares[0] = jnp.where(lanes == p * aux + q, total, shares[0])
 
     for q in range(cut):
         total = jnp.zeros((mu, nu), jnp.float32)
@@ -201,6 +205,8 @@
                 other = known[k ^ 1][:, q * nu : (q + 1) * nu]
                 value += product(near_ref[:, at : at + nu], other.astype(jnp.float32))
             store(cut + p, cut + q, value)
+    for i in range(share_ref.shape[0]):
+        share_ref[i] = shares[0]
 
 
 def share_of(weight, panel, line, bundle, near, halves, far):
@@ -212,7 +218,7 @@
         out_shape=(
             jax.ShapeDtypeStruct((cut, mu, nu), line.dtype),
             jax.ShapeDtypeStruct((rest, mu, nu), jnp.float32),
-            jax.ShapeDtypeStruct((cut + rest, (cut + rest) * 128), jnp.float32),
+            jax.ShapeDtypeStruct((n_row * n_plane, 1, 128), jnp.float32),
         ),
         in_specs=[VMEM] * (5 + n_plane + len(far)),
         out_specs=[VMEM] * 3,
@@ -226,8 +232,8 @@
     )(weight, panel, line, bundle, near, *halves, *far)
 
 
-def dress_kernel(n_row, panel_ref, first_ref, part_ref, *refs):
-    blocks, out_ref = refs[:-1], refs[-1]
+def dress_kernel(n_row, panel_ref, first_ref, part_ref, shares_ref, *refs):
+    blocks, (out_ref, polar_ref) = refs[:-2], refs[-2:]
     cut, _, nu = first_ref.shape
     row = lax.axis_index("row")
     for q in range(cut):
@@ -238,40 +244,27 @@
             at = pl.multiple_of((row ^ k) * nu, nu)
             total += dot(ref[:, q * nu : (q + 1) * nu], panel_ref[pl.ds(at, nu), :])
         out_ref[:, cut + q, :] = total.astype(out_ref.dtype)
-
-
-def dress(panel, first, part, blocks, n_row):
+    aux = polar_ref.shape[0]
+    polar = jnp.sum(shares_ref[...], axis=0) / panel_ref.shape[0]
+    for p in range(aux):
+        polar_ref[p : p + 1, :] = polar[:, p * aux : (p + 1) * aux]
+
+
+def dress(panel, first, part, shares, blocks, n_row):
     cut, mu, nu = first.shape
     aux = cut + part.shape[0]
     return pl.pallas_call(
         functools.partial(dress_kernel, n_row),
-        out_shape=jax.ShapeDtypeStruct((mu, aux, nu), first.dtype),
-        in_specs=[VMEM] * (3 + len(blocks)),
-        out_specs=VMEM,
+        out_shape=(
+            jax.ShapeDtypeStruct((mu, aux, nu), first.dtype),
+            jax.ShapeDtypeStruct((aux, aux), jnp.float32),
+        ),
+        in_specs=[VMEM] * (4 + len(blocks)),
+        out_specs=(VMEM, VMEM),
         compiler_params=pltpu.CompilerParams(vmem_limit_bytes=ROOM),
         cost_estimate=pl.CostEstimate(flops=2 * mu * nu * nu * aux, bytes_accessed=8 * mu * aux * nu, transcendentals=0),
         name="dress",
-    )(panel, first, part, *blocks)
-
-
-def finish_kernel(total_ao, first_ref, second_ref, out_ref):
-    aux = out_ref.shape[0]
-    for q in range(aux):
-        lanes = pl.ds(q * 128, 128)
-        share = first_ref[:, lanes] + second_ref[:, lanes]
-        out_ref[:, q : q + 1] = jnp.sum(share, axis=1, keepdims=True) / total_ao
-
-
-def finish(first, second, total_ao):
-    aux = first.shape[0]
-    return pl.pallas_call(
-        functools.partial(finish_kernel, total_ao),
-        out_shape=jax.ShapeDtypeStruct((aux, aux), jnp.float32),
-        in_specs=[VMEM, VMEM],
-        out_specs=VMEM,
-        compiler_params=pltpu.CompilerParams(vmem_limit_bytes=ROOM),
-        name="finish",
-    )(first, second)
+    )(panel, first, part, shares, *blocks)
 
 
 def on_device(tensor_tiles, tile_pairs, tile_counts, occupied, virtual):
@@ -292,20 +285,12 @@
         far.update({k ^ step: flip(held, "row", step, n_row) for k, held in list(far.items())})
         step //= 2
     beside = flip(both, "row", 1, n_row)
-    blocks = [flip(far[k ^ 1], "row", 1, n_row) for k in late(n_row)]
+    sources, beside = after([far[k ^ 1] for k in late(n_row)], beside)
+    blocks = [flip(held, "row", 1, n_row) for held in sources]
     first, part, share = share_of(
         weight, panel, line, bundle, beside, gather_plane(half), [far[k] for k in range(0, n_row, 2)]
     )
-    step = 1
-    while step < n_plane:
-        share = share + flip(share, PLANE, step, n_plane)
-        step *= 2
-    step = 1
-    while 2 * step < n_row:
-        share = share + flip(share, "row", step, n_row)
-        step *= 2
-    last, dressed = after(flip(share, "row", step, n_row), dress(panel, first, part, blocks, n_row))
-    polar = finish(share, last, weight.shape[1])
+    dressed, polar = dress(panel, first, part, lax.all_to_all(share, EVERY, 0, 0), blocks, n_row)
     return polar, dressed
 
 

time: 56.3 us -> 50.4 us (0.90)
  waiting for transfers between devices: 24.9 us -> 14.4 us
  blocking collectives: 0 us -> 10.2 us
  starting transfers between devices: 25.5 us -> 20.6 us
  Pallas kernels: 4.32 us -> 3.75 us
    ppermute x25 -> x20, waiting for transfers between devices: 24.9 us -> 14.4 us  [flip(): return lax.ppermute(value, axes, [(i, i ^ mask) for i in range(count)])]
    all_to_all x0 -> x1, blocking collectives: none -> 10.2 us  [on_device(): lax.all_to_all(share, EVERY, 0, 0)]
    ppermute x25 -> x20, starting transfers between devices: 25.5 us -> 20.6 us  [flip(): return lax.ppermute(value, axes, [(i, i ^ mask) for i in range(count)])]
    pallas_call x2 -> x1, Pallas kernels: 1.95 us -> 1.29 us  [dress(): pl.pallas_call(functools.partial(dress_kernel, n_row), out_shape=(jax.Sha...]
  transfers between devices with their start and end apart: 25 -> 20, of which waited for: 13 -> 8; matrix products, arithmetic and copies ran while one was open for 0% -> 0% of each run, Pallas kernels for 3% -> 1%
where the time goes in v1:
time: 50.4 us; the launch traced here: 50.2 us
  starting transfers between devices  20.6 us (41%)
  waiting for transfers between devices  14.4 us (29%)
  blocking collectives  10.2 us (20%)
  Pallas kernels  3.75 us (7%)
  between operations  1.33 us (3%)
    ppermute x20, starting transfers between devices, flip(): return lax.ppermute(value, axes, [(i, i ^ mask) for i in range(count)])  20.6 us
    ppermute x20, waiting for transfers between devices, flip(): return lax.ppermute(value, axes, [(i, i ^ mask) for i in range(count)])  14.4 us
    all_to_all x1, blocking collectives, on_device(): lax.all_to_all(share, EVERY, 0, 0)  10.2 us
    pallas_call x1, Pallas kernels, dress(): pl.pallas_call(functools.partial(dress_kernel, n_row), out_shape=(jax.Sha...  1.29 us
    pallas_call x1, Pallas kernels, place(): pl.pallas_call(functools.partial(place_kernel, nu // tile), out_shape=[ja...  1.07 us
  transfers between devices with their start and end apart: 20, of which 8 were waited for; matrix products, arithmetic and copies ran while one was open for 0% of the time, Pallas kernels for 1%

profile of v1, /device:TPU:0, one launch (start us, length us, event | category | flops | bytes accessed | tf_op | source)
XLA Modules:
  0.0 50.2 jit_solution(2603081333451352495)
XLA Ops:
  1.3 1.1 %place.1 = (bf16[3,128,256]{2,1,0:T(8,128)(2,1)S(1)}, bf16[3,128,256]{2,1,0:T(8,128)(2,1)S(1)}) custom-call(s32[1]{0:T(128)S(6)} %copy.7.counts_ref, s32[2]{0:T(128)} %pairs_any.1, bf16[2,4,128,128]{3,2,1,0:T(8,128)(2,1)} %tiles_any.1, bf16[128,256]{1,0:T(8,128)(2,1)} %weight_any.1, bf16[128,256]{1,0:T(8,128)(2,1)} %column_any.1), custom_call_target="tpu_custom_call" | custom-call | bytes 786432 | tf_op jit(solution)/shard_map/place/pallas_call | solution.py:84
  2.4 4.1 %collective-permute-start.1 = (bf16[3,128,256]{2,1,0:T(8,128)(2,1)S(1)}, bf16[3,128,256]{2,1,0:T(8,128)(2,1)S(1)}, u32[]{:S(2)}, u32[]{:S(2)}) collective-permute-start(bf16[3,128,256]{2,1,0:T(8,128)(2,1)S(1)} %get-tuple-element.16.refs_0_.line_ref), channel_id=1, source_target_pairs={{0,16},{8,24},{16,0},{24,8},{1,17},{9,25},{17,1},{25,9},{2,18},{10... | collective-permute-start | bytes 589832 | tf_op jit(solution)/shard_map/ppermute | solution.py:18
  6.5 1.6 %collective-permute-start = (bf16[3,128,256]{2,1,0:T(8,128)(2,1)S(1)}, bf16[3,128,256]{2,1,0:T(8,128)(2,1)S(1)}, u32[]{:S(2)}, u32[]{:S(2)}) collective-permute-start(bf16[3,128,256]{2,1,0:T(8,128)(2,1)S(1)} %get-tuple-element.16.refs_0_.line_ref), channel_id=1, source_target_pairs={{0,8},{8,0},{16,24},{24,16},{1,9},{9,1},{17,25},{25,17},{2,10},{10... | collective-permute-start | bytes 589832 | tf_op jit(solution)/shard_map/ppermute | solution.py:18
  8.0 2.4 %collective-permute-start.8 = (bf16[3,128,256]{2,1,0:T(8,128)(2,1)S(1)}, bf16[3,128,256]{2,1,0:T(8,128)(2,1)S(1)}, u32[]{:S(2)}, u32[]{:S(2)}) collective-permute-start(bf16[3,128,256]{2,1,0:T(8,128)(2,1)S(1)} %get-tuple-element.17.refs_4_.bundle_ref), channel_id=1, source_target_pairs={{0,6},{1,7},{2,4},{3,5},{4,2},{5,3},{6,0},{7,1},{8,14},{9,15},{10,... | collective-permute-start | bytes 589832 | tf_op jit(solution)/shard_map/ppermute | solution.py:18
  10.5 0.5 %collective-permute-start.6 = (bf16[3,128,256]{2,1,0:T(8,128)(2,1)S(1)}, bf16[3,128,256]{2,1,0:T(8,128)(2,1)S(1)}, u32[]{:S(2)}, u32[]{:S(2)}) collective-permute-start(bf16[3,128,256]{2,1,0:T(8,128)(2,1)S(1)} %get-tuple-element.17.refs_4_.bundle_ref), channel_id=1, source_target_pairs={{0,4},{1,5},{2,6},{3,7},{4,0},{5,1},{6,2},{7,3},{8,12},{9,13},{10,... | collective-permute-start | bytes 589832 | tf_op jit(solution)/shard_map/ppermute | solution.py:18
  11.0 0.5 %collective-permute-start.4 = (bf16[3,128,256]{2,1,0:T(8,128)(2,1)S(1)}, bf16[3,128,256]{2,1,0:T(8,128)(2,1)S(1)}, u32[]{:S(2)}, u32[]{:S(2)}) collective-permute-start(bf16[3,128,256]{2,1,0:T(8,128)(2,1)S(1)} %get-tuple-element.17.refs_4_.bundle_ref), channel_id=1, source_target_pairs={{0,2},{1,3},{2,0},{3,1},{4,6},{5,7},{6,4},{7,5},{8,10},{9,11},{10,... | collective-permute-start | bytes 589832 | tf_op jit(solution)/shard_map/ppermute | solution.py:18
  11.5 4.2 %collective-permute-done.1.refs_2_ = bf16[3,128,256]{2,1,0:T(8,128)(2,1)S(1)} collective-permute-done((bf16[3,128,256]{2,1,0:T(8,128)(2,1)S(1)}, bf16[3,128,256]{2,1,0:T(8,128)(2,1)S(1)}, u32[]{:S(2)}, u32[]{:S(2)}) %collective-permute-start.1) | collective-permute-done | bytes 196640 | tf_op jit(solution)/shard_map/ppermute | solution.py:18
  15.9 1.5 %collective-permute-start.2 = (bf16[3,128,256]{2,1,0:T(8,128)(2,1)S(1)}, bf16[3,128,256]{2,1,0:T(8,128)(2,1)S(1)}, u32[]{:S(2)}, u32[]{:S(2)}) collective-permute-start(bf16[3,128,256]{2,1,0:T(8,128)(2,1)S(1)} %collective-permute-done.1.refs_2_), channel_id=1, source_target_pairs={{0,8},{8,0},{16,24},{24,16},{1,9},{9,1},{17,25},{25,17},{2,10},{10... | collective-permute-start | bytes 589832 | tf_op jit(solution)/shard_map/ppermute | solution.py:18
  17.4 2.0 %collective-permute-done.6.refs_8_ = bf16[3,128,256]{2,1,0:T(8,128)(2,1)S(1)} collective-permute-done((bf16[3,128,256]{2,1,0:T(8,128)(2,1)S(1)}, bf16[3,128,256]{2,1,0:T(8,128)(2,1)S(1)}, u32[]{:S(2)}, u32[]{:S(2)}) %collective-permute-start.6) | collective-permute-done | bytes 196640 | tf_op jit(solution)/shard_map/ppermute | solution.py:18
  19.3 0.5 %collective-permute-start.5 = (bf16[3,128,256]{2,1,0:T(8,128)(2,1)S(1)}, bf16[3,128,256]{2,1,0:T(8,128)(2,1)S(1)}, u32[]{:S(2)}, u32[]{:S(2)}) collective-permute-start(bf16[3,128,256]{2,1,0:T(8,128)(2,1)S(1)} %collective-permute-done.4.refs_6_), channel_id=1, source_target_pairs={{0,1},{1,0},{2,3},{3,2},{4,5},{5,4},{6,7},{7,6},{8,9},{9,8},{10,11... | collective-permute-start | bytes 589832 | tf_op jit(solution)/shard_map/ppermute | solution.py:18
  19.8 3.2 %collective-permute-done.2.refs_3_ = bf16[3,128,256]{2,1,0:T(8,128)(2,1)S(1)} collective-permute-done((bf16[3,128,256]{2,1,0:T(8,128)(2,1)S(1)}, bf16[3,128,256]{2,1,0:T(8,128)(2,1)S(1)}, u32[]{:S(2)}, u32[]{:S(2)}) %collective-permute-start.2) | collective-permute-done | bytes 196640 | tf_op jit(solution)/shard_map/ppermute | solution.py:18
  23.0 0.7 %mix.1 = (bf16[128,512]{1,0:T(8,128)(2,1)S(1)}, bf16[128,512]{1,0:T(8,128)(2,1)S(1)}, bf16[128,1024]{1,0:T(8,128)(2,1)S(1)}, bf16[128,1024]{1,0:T(8,128)(2,1)S(1)}, bf16[1024,256]{1,0:T(8,128)(2,1)S(1)}) custom-call(bf16[3,128,256]{2,1,0:T(8,128)(2,1)S(1)} %get-tuple-element.16.refs_0_.line_ref, bf16[3,128,256]{2,1,0:T(8,128)(2,1)S(1)} %collective-permute-done.refs_1_, ...), custom_call_target="tpu_custom_call" | custom-call | flops 268435456 | bytes 2097152 | tf_op jit(solution)/shard_map/mix/pallas_call | solution.py:141
  23.7 0.7 %collective-permute-start.11 = (bf16[128,1024]{1,0:T(8,128)(2,1)S(1)}, bf16[128,1024]{1,0:T(8,128)(2,1)S(1)}, u32[]{:S(2)}, u32[]{:S(2)}) collective-permute-start(bf16[128,1024]{1,0:T(8,128)(2,1)S(1)} %get-tuple-element.21), channel_id=1, source_target_pairs={{0,8},{8,0},{16,24},{24,16},{1,9},{9,1},{17,25},{25,17},{2,10},{10... | collective-permute-start | bytes 786440 | tf_op jit(solution)/shard_map/ppermute | solution.py:18
  24.4 3.4 %collective-permute-start.10 = (bf16[128,512]{1,0:T(8,128)(2,1)S(1)}, bf16[128,512]{1,0:T(8,128)(2,1)S(1)}, u32[]{:S(2)}, u32[]{:S(2)}) collective-permute-start(bf16[128,512]{1,0:T(8,128)(2,1)S(1)} %get-tuple-element.20.refs_8_), channel_id=1, source_target_pairs={{0,16},{8,24},{16,0},{24,8},{1,17},{9,25},{17,1},{25,9},{2,18},{10... | collective-permute-start | bytes 393224 | tf_op jit(solution)/shard_map/ppermute | solution.py:18
  27.8 2.4 %collective-permute-start.17 = (bf16[128,512]{1,0:T(8,128)(2,1)S(1)}, bf16[128,512]{1,0:T(8,128)(2,1)S(1)}, u32[]{:S(2)}, u32[]{:S(2)}) collective-permute-start(bf16[128,512]{1,0:T(8,128)(2,1)S(1)} %get-tuple-element.23.refs_0_), channel_id=1, source_target_pairs={{0,6},{1,7},{2,4},{3,5},{4,2},{5,3},{6,0},{7,1},{8,14},{9,15},{10,... | collective-permute-start | bytes 393224 | tf_op jit(solution)/shard_map/ppermute | solution.py:18
  30.2 0.5 %collective-permute-start.15 = (bf16[128,512]{1,0:T(8,128)(2,1)S(1)}, bf16[128,512]{1,0:T(8,128)(2,1)S(1)}, u32[]{:S(2)}, u32[]{:S(2)}) collective-permute-start(bf16[128,512]{1,0:T(8,128)(2,1)S(1)} %get-tuple-element.23.refs_0_), channel_id=1, source_target_pairs={{0,4},{1,5},{2,6},{3,7},{4,0},{5,1},{6,2},{7,3},{8,12},{9,13},{10,... | collective-permute-start | bytes 393224 | tf_op jit(solution)/shard_map/ppermute | solution.py:18
  30.8 0.5 %collective-permute-start.13 = (bf16[128,512]{1,0:T(8,128)(2,1)S(1)}, bf16[128,512]{1,0:T(8,128)(2,1)S(1)}, u32[]{:S(2)}, u32[]{:S(2)}) collective-permute-start(bf16[128,512]{1,0:T(8,128)(2,1)S(1)} %get-tuple-element.23.refs_0_), channel_id=1, source_target_pairs={{0,2},{1,3},{2,0},{3,1},{4,6},{5,7},{6,4},{7,5},{8,10},{9,11},{10,... | collective-permute-start | bytes 393224 | tf_op jit(solution)/shard_map/ppermute | solution.py:18
  31.3 0.8 %collective-permute-done.10.refs_9_ = bf16[128,512]{1,0:T(8,128)(2,1)S(1)} collective-permute-done((bf16[128,512]{1,0:T(8,128)(2,1)S(1)}, bf16[128,512]{1,0:T(8,128)(2,1)S(1)}, u32[]{:S(2)}, u32[]{:S(2)}) %collective-permute-start.10) | collective-permute-done | bytes 131104 | tf_op jit(solution)/shard_map/ppermute | solution.py:18
  32.1 2.6 %collective-permute-done.17.refs_6_ = bf16[128,512]{1,0:T(8,128)(2,1)S(1)} collective-permute-done((bf16[128,512]{1,0:T(8,128)(2,1)S(1)}, bf16[128,512]{1,0:T(8,128)(2,1)S(1)}, u32[]{:S(2)}, u32[]{:S(2)}) %collective-permute-start.17) | collective-permute-done | bytes 131104 | tf_op jit(solution)/shard_map/ppermute | solution.py:18
  34.8 1.3 %collective-permute-done.15.refs_4_ = bf16[128,512]{1,0:T(8,128)(2,1)S(1)} collective-permute-done((bf16[128,512]{1,0:T(8,128)(2,1)S(1)}, bf16[128,512]{1,0:T(8,128)(2,1)S(1)}, u32[]{:S(2)}, u32[]{:S(2)}) %collective-permute-start.15) | collective-permute-done | bytes 131104 | tf_op jit(solution)/shard_map/ppermute | solution.py:18
  36.6 1.4 %collective-permute-start.19 = (bf16[128,512]{1,0:T(8,128)(2,1)S(1)}, bf16[128,512]{1,0:T(8,128)(2,1)S(1)}, u32[]{:S(2)}, u32[]{:S(2)}) collective-permute-start(bf16[128,512]{1,0:T(8,128)(2,1)S(1)} %collective-permute-done.10.refs_9_), channel_id=1, source_target_pairs={{0,8},{8,0},{16,24},{24,16},{1,9},{9,1},{17,25},{25,17},{2,10},{10... | collective-permute-start | bytes 393224 | tf_op jit(solution)/shard_map/ppermute | solution.py:18
  38.1 0.7 %polar_share.1 = (bf16[2,128,256]{2,1,0:T(8,128)(2,1)S(1)}, f32[2,128,256]{2,1,0:T(8,128)S(1)}, f32[32,1,128]{2,1,0:T(1,128)S(1)}) custom-call(bf16[128,1024]{1,0:T(8,128)(2,1)S(1)} %get-tuple-element.19.weight_ref, bf16[1024,256]{1,0:T(8,128)(2,1)S(1)} %get-tuple-element.18.panel_ref, bf16[3,128,256]{2,1,0:T(8,128)(2,1)S(1)} %get-tuple-element.16.refs_0_.line_ref, ...), custom_call_target="tpu_custom_call" | custom-call | flops 268435456 | bytes 4194304 | tf_op jit(solution)/shard_map/polar_share/pallas_call | solution.py:216
  38.7 10.2 %all_to_all.5.shares_ref = f32[32,1,128]{2,1,0:T(1,128)S(1)} all-to-all(f32[32,1,128]{2,1,0:T(1,128)S(1)} %get-tuple-element.26), channel_id=1, replica_groups=mesh['row'=4,'col'=2,'rep'=4] {'row','col','rep'}, dimensions={0} | all-to-all | bytes 32768 | tf_op jit(solution)/shard_map/all_to_all | solution.py:293
  48.9 1.3 %dress.1 = (bf16[128,4,256]{2,1,0:T(4,128)(2,1)}, f32[4,4]{1,0:T(4,128)}) custom-call(bf16[1024,256]{1,0:T(8,128)(2,1)S(1)} %get-tuple-element.18.panel_ref, bf16[2,128,256]{2,1,0:T(8,128)(2,1)S(1)} %get-tuple-element.24.first_ref, f32[2,128,256]{2,1,0:T(8,128)S(1)} %get-tuple-element.25.part_ref, f32[32,1,128]{2,1,0:T(1,128)S(1)} %all_to_all.5.shares_ref, ...), custom_call_target="tpu_custom_call" | custom-call | flops 67108864 | bytes 1048576 | tf_op jit(solution)/shard_map/dress/pallas_call | solution.py:256
  (21 shorter events, 0.8 us)
Async XLA Ops:
  2.4 13.3 %collective-permute-start.1 = (bf16[3,128,256]{2,1,0:T(8,128)(2,1)S(1)}, bf16[3,128,256]{2,1,0:T(8,128)(2,1)S(1)}, u32[]{:S(2)}, u32[]{:S(2)}) collective-permute-start(bf16[3,128,256]{2,1,0:T(8,128)(2,1)S(1)} %get-tuple-element.16.refs_0_.line_ref), channel_id=1, source_target_pairs={{0,16},{8,24},{16,0},{24,8},{1,17},{9,25},{17,1},{25,9},{2,18},{10... | collective-permute-start | bytes 589832 | tf_op jit(solution)/shard_map/ppermute | solution.py:18
  6.5 9.4 %collective-permute-start = (bf16[3,128,256]{2,1,0:T(8,128)(2,1)S(1)}, bf16[3,128,256]{2,1,0:T(8,128)(2,1)S(1)}, u32[]{:S(2)}, u32[]{:S(2)}) collective-permute-start(bf16[3,128,256]{2,1,0:T(8,128)(2,1)S(1)} %get-tuple-element.16.refs_0_.line_ref), channel_id=1, source_target_pairs={{0,8},{8,0},{16,24},{24,16},{1,9},{9,1},{17,25},{25,17},{2,10},{10... | collective-permute-start | bytes 589832 | tf_op jit(solution)/shard_map/ppermute | solution.py:18
  8.0 9.3 %collective-permute-start.8 = (bf16[3,128,256]{2,1,0:T(8,128)(2,1)S(1)}, bf16[3,128,256]{2,1,0:T(8,128)(2,1)S(1)}, u32[]{:S(2)}, u32[]{:S(2)}) collective-permute-start(bf16[3,128,256]{2,1,0:T(8,128)(2,1)S(1)} %get-tuple-element.17.refs_4_.bundle_ref), channel_id=1, source_target_pairs={{0,6},{1,7},{2,4},{3,5},{4,2},{5,3},{6,0},{7,1},{8,14},{9,15},{10,... | collective-permute-start | bytes 589832 | tf_op jit(solution)/shard_map/ppermute | solution.py:18
  10.5 8.8 %collective-permute-start.6 = (bf16[3,128,256]{2,1,0:T(8,128)(2,1)S(1)}, bf16[3,128,256]{2,1,0:T(8,128)(2,1)S(1)}, u32[]{:S(2)}, u32[]{:S(2)}) collective-permute-start(bf16[3,128,256]{2,1,0:T(8,128)(2,1)S(1)} %get-tuple-element.17.refs_4_.bundle_ref), channel_id=1, source_target_pairs={{0,4},{1,5},{2,6},{3,7},{4,0},{5,1},{6,2},{7,3},{8,12},{9,13},{10,... | collective-permute-start | bytes 589832 | tf_op jit(solution)/shard_map/ppermute | solution.py:18
  11.0 8.3 %collective-permute-start.4 = (bf16[3,128,256]{2,1,0:T(8,128)(2,1)S(1)}, bf16[3,128,256]{2,1,0:T(8,128)(2,1)S(1)}, u32[]{:S(2)}, u32[]{:S(2)}) collective-permute-start(bf16[3,128,256]{2,1,0:T(8,128)(2,1)S(1)} %get-tuple-element.17.refs_4_.bundle_ref), channel_id=1, source_target_pairs={{0,2},{1,3},{2,0},{3,1},{4,6},{5,7},{6,4},{7,5},{8,10},{9,11},{10,... | collective-permute-start | bytes 589832 | tf_op jit(solution)/shard_map/ppermute | solution.py:18
  15.7 4.2 %collective-permute-start.3 = (bf16[3,128,256]{2,1,0:T(8,128)(2,1)S(1)}, bf16[3,128,256]{2,1,0:T(8,128)(2,1)S(1)}, u32[]{:S(2)}, u32[]{:S(2)}) collective-permute-start(bf16[3,128,256]{2,1,0:T(8,128)(2,1)S(1)} %get-tuple-element.17.refs_4_.bundle_ref), channel_id=1, source_target_pairs={{0,1},{1,0},{2,3},{3,2},{4,5},{5,4},{6,7},{7,6},{8,9},{9,8},{10,11... | collective-permute-start | bytes 589832 | tf_op jit(solution)/shard_map/ppermute | solution.py:18
  15.9 7.1 %collective-permute-start.2 = (bf16[3,128,256]{2,1,0:T(8,128)(2,1)S(1)}, bf16[3,128,256]{2,1,0:T(8,128)(2,1)S(1)}, u32[]{:S(2)}, u32[]{:S(2)}) collective-permute-start(bf16[3,128,256]{2,1,0:T(8,128)(2,1)S(1)} %collective-permute-done.1.refs_2_), channel_id=1, source_target_pairs={{0,8},{8,0},{16,24},{24,16},{1,9},{9,1},{17,25},{25,17},{2,10},{10... | collective-permute-start | bytes 589832 | tf_op jit(solution)/shard_map/ppermute | solution.py:18
  17.4 5.6 %collective-permute-start.9 = (bf16[3,128,256]{2,1,0:T(8,128)(2,1)S(1)}, bf16[3,128,256]{2,1,0:T(8,128)(2,1)S(1)}, u32[]{:S(2)}, u32[]{:S(2)}) collective-permute-start(bf16[3,128,256]{2,1,0:T(8,128)(2,1)S(1)} %collective-permute-done.8.refs_10_), channel_id=1, source_target_pairs={{0,1},{1,0},{2,3},{3,2},{4,5},{5,4},{6,7},{7,6},{8,9},{9,8},{10,11... | collective-permute-start | bytes 589832 | tf_op jit(solution)/shard_map/ppermute | solution.py:18
  19.3 3.7 %collective-permute-start.7 = (bf16[3,128,256]{2,1,0:T(8,128)(2,1)S(1)}, bf16[3,128,256]{2,1,0:T(8,128)(2,1)S(1)}, u32[]{:S(2)}, u32[]{:S(2)}) collective-permute-start(bf16[3,128,256]{2,1,0:T(8,128)(2,1)S(1)} %collective-permute-done.6.refs_8_), channel_id=1, source_target_pairs={{0,1},{1,0},{2,3},{3,2},{4,5},{5,4},{6,7},{7,6},{8,9},{9,8},{10,11... | collective-permute-start | bytes 589832 | tf_op jit(solution)/shard_map/ppermute | solution.py:18
  19.3 3.7 %collective-permute-start.5 = (bf16[3,128,256]{2,1,0:T(8,128)(2,1)S(1)}, bf16[3,128,256]{2,1,0:T(8,128)(2,1)S(1)}, u32[]{:S(2)}, u32[]{:S(2)}) collective-permute-start(bf16[3,128,256]{2,1,0:T(8,128)(2,1)S(1)} %collective-permute-done.4.refs_6_), channel_id=1, source_target_pairs={{0,1},{1,0},{2,3},{3,2},{4,5},{5,4},{6,7},{7,6},{8,9},{9,8},{10,11... | collective-permute-start | bytes 589832 | tf_op jit(solution)/shard_map/ppermute | solution.py:18
  23.7 12.9 %collective-permute-start.11 = (bf16[128,1024]{1,0:T(8,128)(2,1)S(1)}, bf16[128,1024]{1,0:T(8,128)(2,1)S(1)}, u32[]{:S(2)}, u32[]{:S(2)}) collective-permute-start(bf16[128,1024]{1,0:T(8,128)(2,1)S(1)} %get-tuple-element.21), channel_id=1, source_target_pairs={{0,8},{8,0},{16,24},{24,16},{1,9},{9,1},{17,25},{25,17},{2,10},{10... | collective-permute-start | bytes 786440 | tf_op jit(solution)/shard_map/ppermute | solution.py:18
  24.4 7.7 %collective-permute-start.10 = (bf16[128,512]{1,0:T(8,128)(2,1)S(1)}, bf16[128,512]{1,0:T(8,128)(2,1)S(1)}, u32[]{:S(2)}, u32[]{:S(2)}) collective-permute-start(bf16[128,512]{1,0:T(8,128)(2,1)S(1)} %get-tuple-element.20.refs_8_), channel_id=1, source_target_pairs={{0,16},{8,24},{16,0},{24,8},{1,17},{9,25},{17,1},{25,9},{2,18},{10... | collective-permute-start | bytes 393224 | tf_op jit(solution)/shard_map/ppermute | solution.py:18
  27.8 7.0 %collective-permute-start.17 = (bf16[128,512]{1,0:T(8,128)(2,1)S(1)}, bf16[128,512]{1,0:T(8,128)(2,1)S(1)}, u32[]{:S(2)}, u32[]{:S(2)}) collective-permute-start(bf16[128,512]{1,0:T(8,128)(2,1)S(1)} %get-tuple-element.23.refs_0_), channel_id=1, source_target_pairs={{0,6},{1,7},{2,4},{3,5},{4,2},{5,3},{6,0},{7,1},{8,14},{9,15},{10,... | collective-permute-start | bytes 393224 | tf_op jit(solution)/shard_map/ppermute | solution.py:18
  30.2 5.9 %collective-permute-start.15 = (bf16[128,512]{1,0:T(8,128)(2,1)S(1)}, bf16[128,512]{1,0:T(8,128)(2,1)S(1)}, u32[]{:S(2)}, u32[]{:S(2)}) collective-permute-start(bf16[128,512]{1,0:T(8,128)(2,1)S(1)} %get-tuple-element.23.refs_0_), channel_id=1, source_target_pairs={{0,4},{1,5},{2,6},{3,7},{4,0},{5,1},{6,2},{7,3},{8,12},{9,13},{10,... | collective-permute-start | bytes 393224 | tf_op jit(solution)/shard_map/ppermute | solution.py:18
  30.8 5.4 %collective-permute-start.13 = (bf16[128,512]{1,0:T(8,128)(2,1)S(1)}, bf16[128,512]{1,0:T(8,128)(2,1)S(1)}, u32[]{:S(2)}, u32[]{:S(2)}) collective-permute-start(bf16[128,512]{1,0:T(8,128)(2,1)S(1)} %get-tuple-element.23.refs_0_), channel_id=1, source_target_pairs={{0,2},{1,3},{2,0},{3,1},{4,6},{5,7},{6,4},{7,5},{8,10},{9,11},{10,... | collective-permute-start | bytes 393224 | tf_op jit(solution)/shard_map/ppermute | solution.py:18
  32.1 5.9 %collective-permute-start.12 = (bf16[128,512]{1,0:T(8,128)(2,1)S(1)}, bf16[128,512]{1,0:T(8,128)(2,1)S(1)}, u32[]{:S(2)}, u32[]{:S(2)}) collective-permute-start(bf16[128,512]{1,0:T(8,128)(2,1)S(1)} %get-tuple-element.23.refs_0_), channel_id=1, source_target_pairs={{0,1},{1,0},{2,3},{3,2},{4,5},{5,4},{6,7},{7,6},{8,9},{9,8},{10,11... | collective-permute-start | bytes 393224 | tf_op jit(solution)/shard_map/ppermute | solution.py:18
  34.8 3.3 %collective-permute-start.18 = (bf16[128,512]{1,0:T(8,128)(2,1)S(1)}, bf16[128,512]{1,0:T(8,128)(2,1)S(1)}, u32[]{:S(2)}, u32[]{:S(2)}) collective-permute-start(bf16[128,512]{1,0:T(8,128)(2,1)S(1)} %collective-permute-done.17.refs_6_), channel_id=1, source_target_pairs={{0,1},{1,0},{2,3},{3,2},{4,5},{5,4},{6,7},{7,6},{8,9},{9,8},{10,11... | collective-permute-start | bytes 393224 | tf_op jit(solution)/shard_map/ppermute | solution.py:18
  36.1 1.9 %collective-permute-start.16 = (bf16[128,512]{1,0:T(8,128)(2,1)S(1)}, bf16[128,512]{1,0:T(8,128)(2,1)S(1)}, u32[]{:S(2)}, u32[]{:S(2)}) collective-permute-start(bf16[128,512]{1,0:T(8,128)(2,1)S(1)} %collective-permute-done.15.refs_4_), channel_id=1, source_target_pairs={{0,1},{1,0},{2,3},{3,2},{4,5},{5,4},{6,7},{7,6},{8,9},{9,8},{10,11... | collective-permute-start | bytes 393224 | tf_op jit(solution)/shard_map/ppermute | solution.py:18
  36.2 1.9 %collective-permute-start.14 = (bf16[128,512]{1,0:T(8,128)(2,1)S(1)}, bf16[128,512]{1,0:T(8,128)(2,1)S(1)}, u32[]{:S(2)}, u32[]{:S(2)}) collective-permute-start(bf16[128,512]{1,0:T(8,128)(2,1)S(1)} %collective-permute-done.13.refs_2_), channel_id=1, source_target_pairs={{0,1},{1,0},{2,3},{3,2},{4,5},{5,4},{6,7},{7,6},{8,9},{9,8},{10,11... | collective-permute-start | bytes 393224 | tf_op jit(solution)/shard_map/ppermute | solution.py:18
  36.6 12.3 %collective-permute-start.19 = (bf16[128,512]{1,0:T(8,128)(2,1)S(1)}, bf16[128,512]{1,0:T(8,128)(2,1)S(1)}, u32[]{:S(2)}, u32[]{:S(2)}) collective-permute-start(bf16[128,512]{1,0:T(8,128)(2,1)S(1)} %collective-permute-done.10.refs_9_), channel_id=1, source_target_pairs={{0,8},{8,0},{16,24},{24,16},{1,9},{9,1},{17,25},{25,17},{2,10},{10... | collective-permute-start | bytes 393224 | tf_op jit(solution)/shard_map/ppermute | solution.py:18

commit v2 on v1

--- a/solution.py
+++ b/solution.py
@@ -103,7 +103,7 @@
 
 def mix_kernel(n_row, n_plane, *refs):
     lines, bundles = refs[:n_row], refs[n_row : n_row + n_plane]
-    half_ref, mixed_ref, both_ref, weight_ref, panel_ref = refs[n_row + n_plane :]
+    half_ref, mixed_ref, both_ref, weight_ref, panel_ref, begun_ref = refs[n_row + n_plane :]
     planes, mu, nu = lines[0].shape
     cut, rest = planes - 1, bundles[0].shape[0] - 1
     row, plane = lax.axis_index("row"), plane_index()
@@ -111,17 +111,25 @@
         panel_ref[pl.ds(pl.multiple_of((plane ^ k) * mu, mu), mu), :] = bundles[k][rest]
     for k in range(n_row):
         weight_ref[:, pl.ds(pl.multiple_of((row ^ k) * nu, nu), nu)] = lines[k][cut]
+    halves = []
     for p in range(cut):
         total = jnp.zeros((mu, nu), jnp.float32)
         for k in range(n_row):
             at = pl.multiple_of((row ^ k) * nu, nu)
             total += dot(lines[k][p], panel_ref[pl.ds(at, nu), :])
         half_ref[:, p * nu : (p + 1) * nu] = total.astype(half_ref.dtype)
+        halves.append(total)
+    lanes = lax.broadcasted_iota(jnp.int32, begun_ref.shape, 1)
+    begun = jnp.zeros(begun_ref.shape, jnp.float32)
     for p in range(rest):
         total = jnp.zeros((mu, nu), jnp.float32)
         for k in range(n_plane):
             at = pl.multiple_of((plane ^ k) * mu, mu)
             total += dot(weight_ref[:, pl.ds(at, mu)], bundles[k][p])
+        for q, value in enumerate(halves):
+            folded = jnp.sum((total * value).reshape(mu // 8, 8, nu), axis=0)
+            own = jnp.sum(jnp.sum(folded, axis=0, keepdims=True), axis=1, keepdims=True)
+            begun = jnp.where(lanes == q * (cut + rest) + cut + p, own, begun)
         mixed_ref[:, p * nu : (p + 1) * nu] = total.astype(mixed_ref.dtype)
         both_ref[:, p * nu : (p + 1) * nu] = total.astype(both_ref.dtype)
         for i, k in enumerate(late(n_row)):
@@ -131,6 +139,7 @@
             )
             place_at = ((i + 1) * rest + p) * nu
             both_ref[:, place_at : place_at + nu] = turned.astype(both_ref.dtype)
+    begun_ref[...] = begun
 
 
 def mix(lines, bundles):
@@ -146,9 +155,10 @@
             jax.ShapeDtypeStruct((mu, (1 + len(late(n_row))) * rest * nu), kind),
             jax.ShapeDtypeStruct((mu, n_row * nu), kind),
             jax.ShapeDtypeStruct((n_plane * mu, nu), kind),
+            jax.ShapeDtypeStruct((1, 128), jnp.float32),
         ),
         in_specs=[VMEM] * (n_row + n_plane),
-        out_specs=[VMEM] * 5,
+        out_specs=[VMEM] * 6,
         compiler_params=pltpu.CompilerParams(vmem_limit_bytes=ROOM),
         cost_estimate=pl.CostEstimate(
             flops=2 * (cut + rest) * mu * nu * nu * n_row,
@@ -159,7 +169,7 @@
     )(*lines, *bundles)
 
 
-def share_kernel(n_row, n_plane, weight_ref, panel_ref, line_ref, bundle_ref, near_ref, *refs):
+def share_kernel(n_row, n_plane, begun_ref, weight_ref, panel_ref, line_ref, bundle_ref, near_ref, *refs):
     halves, far = refs[:n_plane], refs[n_plane : n_plane + n_row // 2]
     first_ref, part_ref, share_ref = refs[n_plane + n_row // 2 :]
     cut, mu, nu = first_ref.shape
@@ -174,7 +184,7 @@
         return sum([folded[:, i : i + 128] for i in range(128, nu, 128)], folded[:, :128])
 
     lanes = lax.broadcasted_iota(jnp.int32, share_ref.shape[1:], 1)
-    shares = [jnp.zeros(share_ref.shape[1:], jnp.float32)]
+    shares = [begun_ref[...]]
 
     def store(p, q, value):
         total = jnp.sum(jnp.sum(value, axis=0, keepdims=True), axis=1, keepdims=True)
@@ -190,8 +200,6 @@
         for p in range(aux):
             value = product(line_ref[p] if p < cut else bundle_ref[p - cut], rounded.astype(jnp.float32))
             store(p, q, value)
-            if p >= cut:
-                store(q, p, value)
     for q in range(rest):
         total = jnp.zeros((mu, nu), jnp.float32)
         for k, ref in known.items():
@@ -209,7 +217,7 @@
         share_ref[i] = shares[0]
 
 
-def share_of(weight, panel, line, bundle, near, halves, far):
+def share_of(begun, weight, panel, line, bundle, near, halves, far):
     planes, mu, nu = line.shape
     cut, rest = planes - 1, bundle.shape[0] - 1
     n_row, n_plane = 2 * len(far), len(halves)
@@ -220,7 +228,7 @@
             jax.ShapeDtypeStruct((rest, mu, nu), jnp.float32),
             jax.ShapeDtypeStruct((n_row * n_plane, 1, 128), jnp.float32),
         ),
-        in_specs=[VMEM] * (5 + n_plane + len(far)),
+        in_specs=[VMEM] * (6 + n_plane + len(far)),
         out_specs=[VMEM] * 3,
         compiler_params=pltpu.CompilerParams(vmem_limit_bytes=ROOM),
         cost_estimate=pl.CostEstimate(
@@ -229,7 +237,7 @@
             transcendentals=0,
         ),
         name="polar_share",
-    )(weight, panel, line, bundle, near, *halves, *far)
+    )(begun, weight, panel, line, bundle, near, *halves, *far)
 
 
 def dress_kernel(n_row, panel_ref, first_ref, part_ref, shares_ref, *refs):
@@ -278,7 +286,7 @@
         return [held for value in values for held in (value, sibling(value))]
 
     line, bundle = place(tile_pairs, tile_counts, tensor_tiles, occupied, virtual)
-    half, mixed, both, weight, panel = mix(gather_row(line, n_row), gather_plane(bundle))
+    half, mixed, both, weight, panel, begun = mix(gather_row(line, n_row), gather_plane(bundle))
     far = {0: mixed}
     step = n_row // 2
     while step > 1:
@@ -288,7 +296,7 @@
     sources, beside = after([far[k ^ 1] for k in late(n_row)], beside)
     blocks = [flip(held, "row", 1, n_row) for held in sources]
     first, part, share = share_of(
-        weight, panel, line, bundle, beside, gather_plane(half), [far[k] for k in range(0, n_row, 2)]
+        begun, weight, panel, line, bundle, beside, gather_plane(half), [far[k] for k in range(0, n_row, 2)]
     )
     dressed, polar = dress(panel, first, part, lax.all_to_all(share, EVERY, 0, 0), blocks, n_row)
     return polar, dressed

time: 50.4 us -> 50.4 us (level)
  no operation moved by 1% of the time
where the time goes in v2:
time: 50.4 us; the launch traced here: 50.3 us
  starting transfers between devices  20.5 us (41%)
  waiting for transfers between devices  14.4 us (29%)
  blocking collectives  10.2 us (20%)
  Pallas kernels  3.85 us (8%)
  between operations  1.33 us (3%)
    ppermute x20, starting transfers between devices, flip(): return lax.ppermute(value, axes, [(i, i ^ mask) for i in range(count)])  20.5 us
    ppermute x20, waiting for transfers between devices, flip(): return lax.ppermute(value, axes, [(i, i ^ mask) for i in range(count)])  14.4 us
    all_to_all x1, blocking collectives, on_device(): lax.all_to_all(share, EVERY, 0, 0)  10.2 us
    pallas_call x1, Pallas kernels, dress(): pl.pallas_call(functools.partial(dress_kernel, n_row), out_shape=(jax.Sha...  1.3 us
    pallas_call x1, Pallas kernels, place(): pl.pallas_call(functools.partial(place_kernel, nu // tile), out_shape=[ja...  1.07 us
  transfers between devices with their start and end apart: 20, of which 8 were waited for; matrix products, arithmetic and copies ran while one was open for 0% of the time, Pallas kernels for 1%

profile of v2, /device:TPU:0, one launch (start us, length us, event | category | flops | bytes accessed | tf_op | source)
XLA Modules:
  0.0 50.3 jit_solution(16734810692284374304)
XLA Ops:
  1.3 1.1 %place.1 = (bf16[3,128,256]{2,1,0:T(8,128)(2,1)S(1)}, bf16[3,128,256]{2,1,0:T(8,128)(2,1)S(1)}) custom-call(s32[1]{0:T(128)S(6)} %copy.7.counts_ref, s32[2]{0:T(128)} %pairs_any.1, bf16[2,4,128,128]{3,2,1,0:T(8,128)(2,1)} %tiles_any.1, bf16[128,256]{1,0:T(8,128)(2,1)} %weight_any.1, bf16[128,256]{1,0:T(8,128)(2,1)} %column_any.1), custom_call_target="tpu_custom_call" | custom-call | bytes 786432 | tf_op jit(solution)/shard_map/place/pallas_call | solution.py:84
  2.4 4.1 %collective-permute-start.1 = (bf16[3,128,256]{2,1,0:T(8,128)(2,1)S(1)}, bf16[3,128,256]{2,1,0:T(8,128)(2,1)S(1)}, u32[]{:S(2)}, u32[]{:S(2)}) collective-permute-start(bf16[3,128,256]{2,1,0:T(8,128)(2,1)S(1)} %get-tuple-element.17.refs_0_.line_ref), channel_id=1, source_target_pairs={{0,16},{8,24},{16,0},{24,8},{1,17},{9,25},{17,1},{25,9},{2,18},{10... | collective-permute-start | bytes 589832 | tf_op jit(solution)/shard_map/ppermute | solution.py:18
  6.5 1.6 %collective-permute-start = (bf16[3,128,256]{2,1,0:T(8,128)(2,1)S(1)}, bf16[3,128,256]{2,1,0:T(8,128)(2,1)S(1)}, u32[]{:S(2)}, u32[]{:S(2)}) collective-permute-start(bf16[3,128,256]{2,1,0:T(8,128)(2,1)S(1)} %get-tuple-element.17.refs_0_.line_ref), channel_id=1, source_target_pairs={{0,8},{8,0},{16,24},{24,16},{1,9},{9,1},{17,25},{25,17},{2,10},{10... | collective-permute-start | bytes 589832 | tf_op jit(solution)/shard_map/ppermute | solution.py:18
  8.0 2.4 %collective-permute-start.8 = (bf16[3,128,256]{2,1,0:T(8,128)(2,1)S(1)}, bf16[3,128,256]{2,1,0:T(8,128)(2,1)S(1)}, u32[]{:S(2)}, u32[]{:S(2)}) collective-permute-start(bf16[3,128,256]{2,1,0:T(8,128)(2,1)S(1)} %get-tuple-element.18.refs_4_.bundle_ref), channel_id=1, source_target_pairs={{0,6},{1,7},{2,4},{3,5},{4,2},{5,3},{6,0},{7,1},{8,14},{9,15},{10,... | collective-permute-start | bytes 589832 | tf_op jit(solution)/shard_map/ppermute | solution.py:18
  10.5 0.5 %collective-permute-start.6 = (bf16[3,128,256]{2,1,0:T(8,128)(2,1)S(1)}, bf16[3,128,256]{2,1,0:T(8,128)(2,1)S(1)}, u32[]{:S(2)}, u32[]{:S(2)}) collective-permute-start(bf16[3,128,256]{2,1,0:T(8,128)(2,1)S(1)} %get-tuple-element.18.refs_4_.bundle_ref), channel_id=1, source_target_pairs={{0,4},{1,5},{2,6},{3,7},{4,0},{5,1},{6,2},{7,3},{8,12},{9,13},{10,... | collective-permute-start | bytes 589832 | tf_op jit(solution)/shard_map/ppermute | solution.py:18
  11.0 0.5 %collective-permute-start.4 = (bf16[3,128,256]{2,1,0:T(8,128)(2,1)S(1)}, bf16[3,128,256]{2,1,0:T(8,128)(2,1)S(1)}, u32[]{:S(2)}, u32[]{:S(2)}) collective-permute-start(bf16[3,128,256]{2,1,0:T(8,128)(2,1)S(1)} %get-tuple-element.18.refs_4_.bundle_ref), channel_id=1, source_target_pairs={{0,2},{1,3},{2,0},{3,1},{4,6},{5,7},{6,4},{7,5},{8,10},{9,11},{10,... | collective-permute-start | bytes 589832 | tf_op jit(solution)/shard_map/ppermute | solution.py:18
  11.5 4.2 %collective-permute-done.1.refs_2_ = bf16[3,128,256]{2,1,0:T(8,128)(2,1)S(1)} collective-permute-done((bf16[3,128,256]{2,1,0:T(8,128)(2,1)S(1)}, bf16[3,128,256]{2,1,0:T(8,128)(2,1)S(1)}, u32[]{:S(2)}, u32[]{:S(2)}) %collective-permute-start.1) | collective-permute-done | bytes 196640 | tf_op jit(solution)/shard_map/ppermute | solution.py:18
  15.9 1.5 %collective-permute-start.2 = (bf16[3,128,256]{2,1,0:T(8,128)(2,1)S(1)}, bf16[3,128,256]{2,1,0:T(8,128)(2,1)S(1)}, u32[]{:S(2)}, u32[]{:S(2)}) collective-permute-start(bf16[3,128,256]{2,1,0:T(8,128)(2,1)S(1)} %collective-permute-done.1.refs_2_), channel_id=1, source_target_pairs={{0,8},{8,0},{16,24},{24,16},{1,9},{9,1},{17,25},{25,17},{2,10},{10... | collective-permute-start | bytes 589832 | tf_op jit(solution)/shard_map/ppermute | solution.py:18
  17.4 2.0 %collective-permute-done.6.refs_8_ = bf16[3,128,256]{2,1,0:T(8,128)(2,1)S(1)} collective-permute-done((bf16[3,128,256]{2,1,0:T(8,128)(2,1)S(1)}, bf16[3,128,256]{2,1,0:T(8,128)(2,1)S(1)}, u32[]{:S(2)}, u32[]{:S(2)}) %collective-permute-start.6) | collective-permute-done | bytes 196640 | tf_op jit(solution)/shard_map/ppermute | solution.py:18
  19.3 0.5 %collective-permute-start.5 = (bf16[3,128,256]{2,1,0:T(8,128)(2,1)S(1)}, bf16[3,128,256]{2,1,0:T(8,128)(2,1)S(1)}, u32[]{:S(2)}, u32[]{:S(2)}) collective-permute-start(bf16[3,128,256]{2,1,0:T(8,128)(2,1)S(1)} %collective-permute-done.4.refs_6_), channel_id=1, source_target_pairs={{0,1},{1,0},{2,3},{3,2},{4,5},{5,4},{6,7},{7,6},{8,9},{9,8},{10,11... | collective-permute-start | bytes 589832 | tf_op jit(solution)/shard_map/ppermute | solution.py:18
  19.8 3.2 %collective-permute-done.2.refs_3_ = bf16[3,128,256]{2,1,0:T(8,128)(2,1)S(1)} collective-permute-done((bf16[3,128,256]{2,1,0:T(8,128)(2,1)S(1)}, bf16[3,128,256]{2,1,0:T(8,128)(2,1)S(1)}, u32[]{:S(2)}, u32[]{:S(2)}) %collective-permute-start.2) | collective-permute-done | bytes 196640 | tf_op jit(solution)/shard_map/ppermute | solution.py:18
  23.0 0.8 %mix.1 = (bf16[128,512]{1,0:T(8,128)(2,1)S(1)}, bf16[128,512]{1,0:T(8,128)(2,1)S(1)}, bf16[128,1024]{1,0:T(8,128)(2,1)S(1)}, bf16[128,1024]{1,0:T(8,128)(2,1)S(1...) custom-call(bf16[3,128,256]{2,1,0:T(8,128)(2,1)S(1)} %get-tuple-element.17.refs_0_.line_ref, ...), custom_call_target="tpu_custom_call" | custom-call | flops 268435456 | bytes 2097152 | tf_op jit(solution)/shard_map/mix/pallas_call | solution.py:150
  23.8 0.6 %collective-permute-start.11 = (bf16[128,1024]{1,0:T(8,128)(2,1)S(1)}, bf16[128,1024]{1,0:T(8,128)(2,1)S(1)}, u32[]{:S(2)}, u32[]{:S(2)}) collective-permute-start(bf16[128,1024]{1,0:T(8,128)(2,1)S(1)} %get-tuple-element.23), channel_id=1, source_target_pairs={{0,8},{8,0},{16,24},{24,16},{1,9},{9,1},{17,25},{25,17},{2,10},{10... | collective-permute-start | bytes 786440 | tf_op jit(solution)/shard_map/ppermute | solution.py:18
  24.4 3.4 %collective-permute-start.10 = (bf16[128,512]{1,0:T(8,128)(2,1)S(1)}, bf16[128,512]{1,0:T(8,128)(2,1)S(1)}, u32[]{:S(2)}, u32[]{:S(2)}) collective-permute-start(bf16[128,512]{1,0:T(8,128)(2,1)S(1)} %get-tuple-element.22.refs_8_), channel_id=1, source_target_pairs={{0,16},{8,24},{16,0},{24,8},{1,17},{9,25},{17,1},{25,9},{2,18},{10... | collective-permute-start | bytes 393224 | tf_op jit(solution)/shard_map/ppermute | solution.py:18
  27.8 2.4 %collective-permute-start.17 = (bf16[128,512]{1,0:T(8,128)(2,1)S(1)}, bf16[128,512]{1,0:T(8,128)(2,1)S(1)}, u32[]{:S(2)}, u32[]{:S(2)}) collective-permute-start(bf16[128,512]{1,0:T(8,128)(2,1)S(1)} %get-tuple-element.25.refs_0_), channel_id=1, source_target_pairs={{0,6},{1,7},{2,4},{3,5},{4,2},{5,3},{6,0},{7,1},{8,14},{9,15},{10,... | collective-permute-start | bytes 393224 | tf_op jit(solution)/shard_map/ppermute | solution.py:18
  30.3 0.5 %collective-permute-start.15 = (bf16[128,512]{1,0:T(8,128)(2,1)S(1)}, bf16[128,512]{1,0:T(8,128)(2,1)S(1)}, u32[]{:S(2)}, u32[]{:S(2)}) collective-permute-start(bf16[128,512]{1,0:T(8,128)(2,1)S(1)} %get-tuple-element.25.refs_0_), channel_id=1, source_target_pairs={{0,4},{1,5},{2,6},{3,7},{4,0},{5,1},{6,2},{7,3},{8,12},{9,13},{10,... | collective-permute-start | bytes 393224 | tf_op jit(solution)/shard_map/ppermute | solution.py:18
  30.8 0.5 %collective-permute-start.13 = (bf16[128,512]{1,0:T(8,128)(2,1)S(1)}, bf16[128,512]{1,0:T(8,128)(2,1)S(1)}, u32[]{:S(2)}, u32[]{:S(2)}) collective-permute-start(bf16[128,512]{1,0:T(8,128)(2,1)S(1)} %get-tuple-element.25.refs_0_), channel_id=1, source_target_pairs={{0,2},{1,3},{2,0},{3,1},{4,6},{5,7},{6,4},{7,5},{8,10},{9,11},{10,... | collective-permute-start | bytes 393224 | tf_op jit(solution)/shard_map/ppermute | solution.py:18
  31.3 0.9 %collective-permute-done.10.refs_9_ = bf16[128,512]{1,0:T(8,128)(2,1)S(1)} collective-permute-done((bf16[128,512]{1,0:T(8,128)(2,1)S(1)}, bf16[128,512]{1,0:T(8,128)(2,1)S(1)}, u32[]{:S(2)}, u32[]{:S(2)}) %collective-permute-start.10) | collective-permute-done | bytes 131104 | tf_op jit(solution)/shard_map/ppermute | solution.py:18
  32.2 2.6 %collective-permute-done.17.refs_6_ = bf16[128,512]{1,0:T(8,128)(2,1)S(1)} collective-permute-done((bf16[128,512]{1,0:T(8,128)(2,1)S(1)}, bf16[128,512]{1,0:T(8,128)(2,1)S(1)}, u32[]{:S(2)}, u32[]{:S(2)}) %collective-permute-start.17) | collective-permute-done | bytes 131104 | tf_op jit(solution)/shard_map/ppermute | solution.py:18
  34.8 1.3 %collective-permute-done.15.refs_4_ = bf16[128,512]{1,0:T(8,128)(2,1)S(1)} collective-permute-done((bf16[128,512]{1,0:T(8,128)(2,1)S(1)}, bf16[128,512]{1,0:T(8,128)(2,1)S(1)}, u32[]{:S(2)}, u32[]{:S(2)}) %collective-permute-start.15) | collective-permute-done | bytes 131104 | tf_op jit(solution)/shard_map/ppermute | solution.py:18
  36.7 1.4 %collective-permute-start.19 = (bf16[128,512]{1,0:T(8,128)(2,1)S(1)}, bf16[128,512]{1,0:T(8,128)(2,1)S(1)}, u32[]{:S(2)}, u32[]{:S(2)}) collective-permute-start(bf16[128,512]{1,0:T(8,128)(2,1)S(1)} %collective-permute-done.10.refs_9_), channel_id=1, source_target_pairs={{0,8},{8,0},{16,24},{24,16},{1,9},{9,1},{17,25},{25,17},{2,10},{10... | collective-permute-start | bytes 393224 | tf_op jit(solution)/shard_map/ppermute | solution.py:18
  38.1 0.7 %polar_share.1 = (bf16[2,128,256]{2,1,0:T(8,128)(2,1)S(1)}, f32[2,128,256]{2,1,0:T(8,128)S(1)}, f32[32,1,128]{2,1,0:T(1,128)S(1)}) custom-call(f32[1,128]{1,0:T(1,128)S(1)} %get-tuple-element.20.begun_ref, bf16[128,1024]{1,0:T(8,128)(2,1)S(1)} %get-tuple-element.21.weight_ref, bf16[1024,256]{1,0:T(8,128)(2,1)S(1)} %get-tuple-element.19.panel_ref, ...), custom_call_target="tpu_custom_call" | custom-call | flops 268435456 | bytes 4194304 | tf_op jit(solution)/shard_map/polar_share/pallas_call | solution.py:224
  38.8 10.2 %all_to_all.5.shares_ref = f32[32,1,128]{2,1,0:T(1,128)S(1)} all-to-all(f32[32,1,128]{2,1,0:T(1,128)S(1)} %get-tuple-element.28), channel_id=1, replica_groups=mesh['row'=4,'col'=2,'rep'=4] {'row','col','rep'}, dimensions={0} | all-to-all | bytes 32768 | tf_op jit(solution)/shard_map/all_to_all | solution.py:301
  49.0 1.3 %dress.1 = (bf16[128,4,256]{2,1,0:T(4,128)(2,1)}, f32[4,4]{1,0:T(4,128)}) custom-call(bf16[1024,256]{1,0:T(8,128)(2,1)S(1)} %get-tuple-element.19.panel_ref, bf16[2,128,256]{2,1,0:T(8,128)(2,1)S(1)} %get-tuple-element.26.first_ref, f32[2,128,256]{2,1,0:T(8,128)S(1)} %get-tuple-element.27.part_ref, f32[32,1,128]{2,1,0:T(1,128)S(1)} %all_to_all.5.shares_ref, ...), custom_call_target="tpu_custom_call" | custom-call | flops 67108864 | bytes 1048576 | tf_op jit(solution)/shard_map/dress/pallas_call | solution.py:264
  (21 shorter events, 0.7 us)
Async XLA Ops:
  2.4 13.3 %collective-permute-start.1 = (bf16[3,128,256]{2,1,0:T(8,128)(2,1)S(1)}, bf16[3,128,256]{2,1,0:T(8,128)(2,1)S(1)}, u32[]{:S(2)}, u32[]{:S(2)}) collective-permute-start(bf16[3,128,256]{2,1,0:T(8,128)(2,1)S(1)} %get-tuple-element.17.refs_0_.line_ref), channel_id=1, source_target_pairs={{0,16},{8,24},{16,0},{24,8},{1,17},{9,25},{17,1},{25,9},{2,18},{10... | collective-permute-start | bytes 589832 | tf_op jit(solution)/shard_map/ppermute | solution.py:18
  6.5 9.4 %collective-permute-start = (bf16[3,128,256]{2,1,0:T(8,128)(2,1)S(1)}, bf16[3,128,256]{2,1,0:T(8,128)(2,1)S(1)}, u32[]{:S(2)}, u32[]{:S(2)}) collective-permute-start(bf16[3,128,256]{2,1,0:T(8,128)(2,1)S(1)} %get-tuple-element.17.refs_0_.line_ref), channel_id=1, source_target_pairs={{0,8},{8,0},{16,24},{24,16},{1,9},{9,1},{17,25},{25,17},{2,10},{10... | collective-permute-start | bytes 589832 | tf_op jit(solution)/shard_map/ppermute | solution.py:18
  8.0 9.3 %collective-permute-start.8 = (bf16[3,128,256]{2,1,0:T(8,128)(2,1)S(1)}, bf16[3,128,256]{2,1,0:T(8,128)(2,1)S(1)}, u32[]{:S(2)}, u32[]{:S(2)}) collective-permute-start(bf16[3,128,256]{2,1,0:T(8,128)(2,1)S(1)} %get-tuple-element.18.refs_4_.bundle_ref), channel_id=1, source_target_pairs={{0,6},{1,7},{2,4},{3,5},{4,2},{5,3},{6,0},{7,1},{8,14},{9,15},{10,... | collective-permute-start | bytes 589832 | tf_op jit(solution)/shard_map/ppermute | solution.py:18
  10.5 8.8 %collective-permute-start.6 = (bf16[3,128,256]{2,1,0:T(8,128)(2,1)S(1)}, bf16[3,128,256]{2,1,0:T(8,128)(2,1)S(1)}, u32[]{:S(2)}, u32[]{:S(2)}) collective-permute-start(bf16[3,128,256]{2,1,0:T(8,128)(2,1)S(1)} %get-tuple-element.18.refs_4_.bundle_ref), channel_id=1, source_target_pairs={{0,4},{1,5},{2,6},{3,7},{4,0},{5,1},{6,2},{7,3},{8,12},{9,13},{10,... | collective-permute-start | bytes 589832 | tf_op jit(solution)/shard_map/ppermute | solution.py:18
  11.0 8.3 %collective-permute-start.4 = (bf16[3,128,256]{2,1,0:T(8,128)(2,1)S(1)}, bf16[3,128,256]{2,1,0:T(8,128)(2,1)S(1)}, u32[]{:S(2)}, u32[]{:S(2)}) collective-permute-start(bf16[3,128,256]{2,1,0:T(8,128)(2,1)S(1)} %get-tuple-element.18.refs_4_.bundle_ref), channel_id=1, source_target_pairs={{0,2},{1,3},{2,0},{3,1},{4,6},{5,7},{6,4},{7,5},{8,10},{9,11},{10,... | collective-permute-start | bytes 589832 | tf_op jit(solution)/shard_map/ppermute | solution.py:18
  15.7 4.2 %collective-permute-start.3 = (bf16[3,128,256]{2,1,0:T(8,128)(2,1)S(1)}, bf16[3,128,256]{2,1,0:T(8,128)(2,1)S(1)}, u32[]{:S(2)}, u32[]{:S(2)}) collective-permute-start(bf16[3,128,256]{2,1,0:T(8,128)(2,1)S(1)} %get-tuple-element.18.refs_4_.bundle_ref), channel_id=1, source_target_pairs={{0,1},{1,0},{2,3},{3,2},{4,5},{5,4},{6,7},{7,6},{8,9},{9,8},{10,11... | collective-permute-start | bytes 589832 | tf_op jit(solution)/shard_map/ppermute | solution.py:18
  15.9 7.1 %collective-permute-start.2 = (bf16[3,128,256]{2,1,0:T(8,128)(2,1)S(1)}, bf16[3,128,256]{2,1,0:T(8,128)(2,1)S(1)}, u32[]{:S(2)}, u32[]{:S(2)}) collective-permute-start(bf16[3,128,256]{2,1,0:T(8,128)(2,1)S(1)} %collective-permute-done.1.refs_2_), channel_id=1, source_target_pairs={{0,8},{8,0},{16,24},{24,16},{1,9},{9,1},{17,25},{25,17},{2,10},{10... | collective-permute-start | bytes 589832 | tf_op jit(solution)/shard_map/ppermute | solution.py:18
  17.4 5.6 %collective-permute-start.9 = (bf16[3,128,256]{2,1,0:T(8,128)(2,1)S(1)}, bf16[3,128,256]{2,1,0:T(8,128)(2,1)S(1)}, u32[]{:S(2)}, u32[]{:S(2)}) collective-permute-start(bf16[3,128,256]{2,1,0:T(8,128)(2,1)S(1)} %collective-permute-done.8.refs_10_), channel_id=1, source_target_pairs={{0,1},{1,0},{2,3},{3,2},{4,5},{5,4},{6,7},{7,6},{8,9},{9,8},{10,11... | collective-permute-start | bytes 589832 | tf_op jit(solution)/shard_map/ppermute | solution.py:18
  19.3 3.7 %collective-permute-start.7 = (bf16[3,128,256]{2,1,0:T(8,128)(2,1)S(1)}, bf16[3,128,256]{2,1,0:T(8,128)(2,1)S(1)}, u32[]{:S(2)}, u32[]{:S(2)}) collective-permute-start(bf16[3,128,256]{2,1,0:T(8,128)(2,1)S(1)} %collective-permute-done.6.refs_8_), channel_id=1, source_target_pairs={{0,1},{1,0},{2,3},{3,2},{4,5},{5,4},{6,7},{7,6},{8,9},{9,8},{10,11... | collective-permute-start | bytes 589832 | tf_op jit(solution)/shard_map/ppermute | solution.py:18
  19.3 3.7 %collective-permute-start.5 = (bf16[3,128,256]{2,1,0:T(8,128)(2,1)S(1)}, bf16[3,128,256]{2,1,0:T(8,128)(2,1)S(1)}, u32[]{:S(2)}, u32[]{:S(2)}) collective-permute-start(bf16[3,128,256]{2,1,0:T(8,128)(2,1)S(1)} %collective-permute-done.4.refs_6_), channel_id=1, source_target_pairs={{0,1},{1,0},{2,3},{3,2},{4,5},{5,4},{6,7},{7,6},{8,9},{9,8},{10,11... | collective-permute-start | bytes 589832 | tf_op jit(solution)/shard_map/ppermute | solution.py:18
  23.8 12.8 %collective-permute-start.11 = (bf16[128,1024]{1,0:T(8,128)(2,1)S(1)}, bf16[128,1024]{1,0:T(8,128)(2,1)S(1)}, u32[]{:S(2)}, u32[]{:S(2)}) collective-permute-start(bf16[128,1024]{1,0:T(8,128)(2,1)S(1)} %get-tuple-element.23), channel_id=1, source_target_pairs={{0,8},{8,0},{16,24},{24,16},{1,9},{9,1},{17,25},{25,17},{2,10},{10... | collective-permute-start | bytes 786440 | tf_op jit(solution)/shard_map/ppermute | solution.py:18
  24.4 7.7 %collective-permute-start.10 = (bf16[128,512]{1,0:T(8,128)(2,1)S(1)}, bf16[128,512]{1,0:T(8,128)(2,1)S(1)}, u32[]{:S(2)}, u32[]{:S(2)}) collective-permute-start(bf16[128,512]{1,0:T(8,128)(2,1)S(1)} %get-tuple-element.22.refs_8_), channel_id=1, source_target_pairs={{0,16},{8,24},{16,0},{24,8},{1,17},{9,25},{17,1},{25,9},{2,18},{10... | collective-permute-start | bytes 393224 | tf_op jit(solution)/shard_map/ppermute | solution.py:18
  27.8 7.0 %collective-permute-start.17 = (bf16[128,512]{1,0:T(8,128)(2,1)S(1)}, bf16[128,512]{1,0:T(8,128)(2,1)S(1)}, u32[]{:S(2)}, u32[]{:S(2)}) collective-permute-start(bf16[128,512]{1,0:T(8,128)(2,1)S(1)} %get-tuple-element.25.refs_0_), channel_id=1, source_target_pairs={{0,6},{1,7},{2,4},{3,5},{4,2},{5,3},{6,0},{7,1},{8,14},{9,15},{10,... | collective-permute-start | bytes 393224 | tf_op jit(solution)/shard_map/ppermute | solution.py:18
  30.3 5.9 %collective-permute-start.15 = (bf16[128,512]{1,0:T(8,128)(2,1)S(1)}, bf16[128,512]{1,0:T(8,128)(2,1)S(1)}, u32[]{:S(2)}, u32[]{:S(2)}) collective-permute-start(bf16[128,512]{1,0:T(8,128)(2,1)S(1)} %get-tuple-element.25.refs_0_), channel_id=1, source_target_pairs={{0,4},{1,5},{2,6},{3,7},{4,0},{5,1},{6,2},{7,3},{8,12},{9,13},{10,... | collective-permute-start | bytes 393224 | tf_op jit(solution)/shard_map/ppermute | solution.py:18
  30.8 5.4 %collective-permute-start.13 = (bf16[128,512]{1,0:T(8,128)(2,1)S(1)}, bf16[128,512]{1,0:T(8,128)(2,1)S(1)}, u32[]{:S(2)}, u32[]{:S(2)}) collective-permute-start(bf16[128,512]{1,0:T(8,128)(2,1)S(1)} %get-tuple-element.25.refs_0_), channel_id=1, source_target_pairs={{0,2},{1,3},{2,0},{3,1},{4,6},{5,7},{6,4},{7,5},{8,10},{9,11},{10,... | collective-permute-start | bytes 393224 | tf_op jit(solution)/shard_map/ppermute | solution.py:18
  32.2 5.9 %collective-permute-start.12 = (bf16[128,512]{1,0:T(8,128)(2,1)S(1)}, bf16[128,512]{1,0:T(8,128)(2,1)S(1)}, u32[]{:S(2)}, u32[]{:S(2)}) collective-permute-start(bf16[128,512]{1,0:T(8,128)(2,1)S(1)} %get-tuple-element.25.refs_0_), channel_id=1, source_target_pairs={{0,1},{1,0},{2,3},{3,2},{4,5},{5,4},{6,7},{7,6},{8,9},{9,8},{10,11... | collective-permute-start | bytes 393224 | tf_op jit(solution)/shard_map/ppermute | solution.py:18
  34.8 3.3 %collective-permute-start.18 = (bf16[128,512]{1,0:T(8,128)(2,1)S(1)}, bf16[128,512]{1,0:T(8,128)(2,1)S(1)}, u32[]{:S(2)}, u32[]{:S(2)}) collective-permute-start(bf16[128,512]{1,0:T(8,128)(2,1)S(1)} %collective-permute-done.17.refs_6_), channel_id=1, source_target_pairs={{0,1},{1,0},{2,3},{3,2},{4,5},{5,4},{6,7},{7,6},{8,9},{9,8},{10,11... | collective-permute-start | bytes 393224 | tf_op jit(solution)/shard_map/ppermute | solution.py:18
  36.1 1.9 %collective-permute-start.16 = (bf16[128,512]{1,0:T(8,128)(2,1)S(1)}, bf16[128,512]{1,0:T(8,128)(2,1)S(1)}, u32[]{:S(2)}, u32[]{:S(2)}) collective-permute-start(bf16[128,512]{1,0:T(8,128)(2,1)S(1)} %collective-permute-done.15.refs_4_), channel_id=1, source_target_pairs={{0,1},{1,0},{2,3},{3,2},{4,5},{5,4},{6,7},{7,6},{8,9},{9,8},{10,11... | collective-permute-start | bytes 393224 | tf_op jit(solution)/shard_map/ppermute | solution.py:18
  36.2 1.9 %collective-permute-start.14 = (bf16[128,512]{1,0:T(8,128)(2,1)S(1)}, bf16[128,512]{1,0:T(8,128)(2,1)S(1)}, u32[]{:S(2)}, u32[]{:S(2)}) collective-permute-start(bf16[128,512]{1,0:T(8,128)(2,1)S(1)} %collective-permute-done.13.refs_2_), channel_id=1, source_target_pairs={{0,1},{1,0},{2,3},{3,2},{4,5},{5,4},{6,7},{7,6},{8,9},{9,8},{10,11... | collective-permute-start | bytes 393224 | tf_op jit(solution)/shard_map/ppermute | solution.py:18
  36.7 12.3 %collective-permute-start.19 = (bf16[128,512]{1,0:T(8,128)(2,1)S(1)}, bf16[128,512]{1,0:T(8,128)(2,1)S(1)}, u32[]{:S(2)}, u32[]{:S(2)}) collective-permute-start(bf16[128,512]{1,0:T(8,128)(2,1)S(1)} %collective-permute-done.10.refs_9_), channel_id=1, source_target_pairs={{0,8},{8,0},{16,24},{24,16},{1,9},{9,1},{17,25},{25,17},{2,10},{10... | collective-permute-start | bytes 393224 | tf_op jit(solution)/shard_map/ppermute | solution.py:18

commit v3 on v2

--- a/solution.py
+++ b/solution.py
@@ -244,14 +244,15 @@
     blocks, (out_ref, polar_ref) = refs[:-2], refs[-2:]
     cut, _, nu = first_ref.shape
     row = lax.axis_index("row")
-    for q in range(cut):
-        out_ref[:, q, :] = first_ref[q]
+    values = [first_ref[q] for q in range(cut)]
     for q in range(part_ref.shape[0]):
         total = part_ref[q]
         for k, ref in zip(late(n_row), blocks):
             at = pl.multiple_of((row ^ k) * nu, nu)
             total += dot(ref[:, q * nu : (q + 1) * nu], panel_ref[pl.ds(at, nu), :])
-        out_ref[:, cut + q, :] = total.astype(out_ref.dtype)
+        values.append(total.astype(out_ref.dtype))
+    for q in range(0, len(values), 2):
+        out_ref[:, q : q + 2, :] = jnp.stack(values[q : q + 2], axis=1)
     aux = polar_ref.shape[0]
     polar = jnp.sum(shares_ref[...], axis=0) / panel_ref.shape[0]
     for p in range(aux):

time: 50.4 us -> 50.6 us (level)
  no operation moved by 1% of the time
where the time goes in v3:
time: 50.6 us; the launch traced here: 50.4 us
  starting transfers between devices  20.5 us (41%)
  waiting for transfers between devices  14.4 us (28%)
  blocking collectives  10.2 us (20%)
  Pallas kernels  4.01 us (8%)
  between operations  1.33 us (3%)
    ppermute x20, starting transfers between devices, flip(): return lax.ppermute(value, axes, [(i, i ^ mask) for i in range(count)])  20.5 us
    ppermute x20, waiting for transfers between devices, flip(): return lax.ppermute(value, axes, [(i, i ^ mask) for i in range(count)])  14.4 us
    all_to_all x1, blocking collectives, on_device(): lax.all_to_all(share, EVERY, 0, 0)  10.2 us
    pallas_call x1, Pallas kernels, dress(): pl.pallas_call(functools.partial(dress_kernel, n_row), out_shape=(jax.Sha...  1.46 us
    pallas_call x1, Pallas kernels, place(): pl.pallas_call(functools.partial(place_kernel, nu // tile), out_shape=[ja...  1.07 us
  transfers between devices with their start and end apart: 20, of which 8 were waited for; matrix products, arithmetic and copies ran while one was open for 0% of the time, Pallas kernels for 1%

profile of v3, /device:TPU:0, one launch (start us, length us, event | category | flops | bytes accessed | tf_op | source)
XLA Modules:
  0.0 50.4 jit_solution(13579250986378919007)
XLA Ops:
  1.3 1.1 %place.1 = (bf16[3,128,256]{2,1,0:T(8,128)(2,1)S(1)}, bf16[3,128,256]{2,1,0:T(8,128)(2,1)S(1)}) custom-call(s32[1]{0:T(128)S(6)} %copy.7.counts_ref, s32[2]{0:T(128)} %pairs_any.1, bf16[2,4,128,128]{3,2,1,0:T(8,128)(2,1)} %tiles_any.1, bf16[128,256]{1,0:T(8,128)(2,1)} %weight_any.1, bf16[128,256]{1,0:T(8,128)(2,1)} %column_any.1), custom_call_target="tpu_custom_call" | custom-call | bytes 786432 | tf_op jit(solution)/shard_map/place/pallas_call | solution.py:84
  2.4 4.1 %collective-permute-start.1 = (bf16[3,128,256]{2,1,0:T(8,128)(2,1)S(1)}, bf16[3,128,256]{2,1,0:T(8,128)(2,1)S(1)}, u32[]{:S(2)}, u32[]{:S(2)}) collective-permute-start(bf16[3,128,256]{2,1,0:T(8,128)(2,1)S(1)} %get-tuple-element.17.refs_0_.line_ref), channel_id=1, source_target_pairs={{0,16},{8,24},{16,0},{24,8},{1,17},{9,25},{17,1},{25,9},{2,18},{10... | collective-permute-start | bytes 589832 | tf_op jit(solution)/shard_map/ppermute | solution.py:18
  6.5 1.6 %collective-permute-start = (bf16[3,128,256]{2,1,0:T(8,128)(2,1)S(1)}, bf16[3,128,256]{2,1,0:T(8,128)(2,1)S(1)}, u32[]{:S(2)}, u32[]{:S(2)}) collective-permute-start(bf16[3,128,256]{2,1,0:T(8,128)(2,1)S(1)} %get-tuple-element.17.refs_0_.line_ref), channel_id=1, source_target_pairs={{0,8},{8,0},{16,24},{24,16},{1,9},{9,1},{17,25},{25,17},{2,10},{10... | collective-permute-start | bytes 589832 | tf_op jit(solution)/shard_map/ppermute | solution.py:18
  8.0 2.4 %collective-permute-start.8 = (bf16[3,128,256]{2,1,0:T(8,128)(2,1)S(1)}, bf16[3,128,256]{2,1,0:T(8,128)(2,1)S(1)}, u32[]{:S(2)}, u32[]{:S(2)}) collective-permute-start(bf16[3,128,256]{2,1,0:T(8,128)(2,1)S(1)} %get-tuple-element.18.refs_4_.bundle_ref), channel_id=1, source_target_pairs={{0,6},{1,7},{2,4},{3,5},{4,2},{5,3},{6,0},{7,1},{8,14},{9,15},{10,... | collective-permute-start | bytes 589832 | tf_op jit(solution)/shard_map/ppermute | solution.py:18
  10.5 0.5 %collective-permute-start.6 = (bf16[3,128,256]{2,1,0:T(8,128)(2,1)S(1)}, bf16[3,128,256]{2,1,0:T(8,128)(2,1)S(1)}, u32[]{:S(2)}, u32[]{:S(2)}) collective-permute-start(bf16[3,128,256]{2,1,0:T(8,128)(2,1)S(1)} %get-tuple-element.18.refs_4_.bundle_ref), channel_id=1, source_target_pairs={{0,4},{1,5},{2,6},{3,7},{4,0},{5,1},{6,2},{7,3},{8,12},{9,13},{10,... | collective-permute-start | bytes 589832 | tf_op jit(solution)/shard_map/ppermute | solution.py:18
  11.0 0.5 %collective-permute-start.4 = (bf16[3,128,256]{2,1,0:T(8,128)(2,1)S(1)}, bf16[3,128,256]{2,1,0:T(8,128)(2,1)S(1)}, u32[]{:S(2)}, u32[]{:S(2)}) collective-permute-start(bf16[3,128,256]{2,1,0:T(8,128)(2,1)S(1)} %get-tuple-element.18.refs_4_.bundle_ref), channel_id=1, source_target_pairs={{0,2},{1,3},{2,0},{3,1},{4,6},{5,7},{6,4},{7,5},{8,10},{9,11},{10,... | collective-permute-start | bytes 589832 | tf_op jit(solution)/shard_map/ppermute | solution.py:18
  11.5 4.1 %collective-permute-done.1.refs_2_ = bf16[3,128,256]{2,1,0:T(8,128)(2,1)S(1)} collective-permute-done((bf16[3,128,256]{2,1,0:T(8,128)(2,1)S(1)}, bf16[3,128,256]{2,1,0:T(8,128)(2,1)S(1)}, u32[]{:S(2)}, u32[]{:S(2)}) %collective-permute-start.1) | collective-permute-done | bytes 196640 | tf_op jit(solution)/shard_map/ppermute | solution.py:18
  15.9 1.5 %collective-permute-start.2 = (bf16[3,128,256]{2,1,0:T(8,128)(2,1)S(1)}, bf16[3,128,256]{2,1,0:T(8,128)(2,1)S(1)}, u32[]{:S(2)}, u32[]{:S(2)}) collective-permute-start(bf16[3,128,256]{2,1,0:T(8,128)(2,1)S(1)} %collective-permute-done.1.refs_2_), channel_id=1, source_target_pairs={{0,8},{8,0},{16,24},{24,16},{1,9},{9,1},{17,25},{25,17},{2,10},{10... | collective-permute-start | bytes 589832 | tf_op jit(solution)/shard_map/ppermute | solution.py:18
  17.4 2.0 %collective-permute-done.6.refs_8_ = bf16[3,128,256]{2,1,0:T(8,128)(2,1)S(1)} collective-permute-done((bf16[3,128,256]{2,1,0:T(8,128)(2,1)S(1)}, bf16[3,128,256]{2,1,0:T(8,128)(2,1)S(1)}, u32[]{:S(2)}, u32[]{:S(2)}) %collective-permute-start.6) | collective-permute-done | bytes 196640 | tf_op jit(solution)/shard_map/ppermute | solution.py:18
  19.3 0.5 %collective-permute-start.5 = (bf16[3,128,256]{2,1,0:T(8,128)(2,1)S(1)}, bf16[3,128,256]{2,1,0:T(8,128)(2,1)S(1)}, u32[]{:S(2)}, u32[]{:S(2)}) collective-permute-start(bf16[3,128,256]{2,1,0:T(8,128)(2,1)S(1)} %collective-permute-done.4.refs_6_), channel_id=1, source_target_pairs={{0,1},{1,0},{2,3},{3,2},{4,5},{5,4},{6,7},{7,6},{8,9},{9,8},{10,11... | collective-permute-start | bytes 589832 | tf_op jit(solution)/shard_map/ppermute | solution.py:18
  19.8 3.2 %collective-permute-done.2.refs_3_ = bf16[3,128,256]{2,1,0:T(8,128)(2,1)S(1)} collective-permute-done((bf16[3,128,256]{2,1,0:T(8,128)(2,1)S(1)}, bf16[3,128,256]{2,1,0:T(8,128)(2,1)S(1)}, u32[]{:S(2)}, u32[]{:S(2)}) %collective-permute-start.2) | collective-permute-done | bytes 196640 | tf_op jit(solution)/shard_map/ppermute | solution.py:18
  23.0 0.8 %mix.1 = (bf16[128,512]{1,0:T(8,128)(2,1)S(1)}, bf16[128,512]{1,0:T(8,128)(2,1)S(1)}, bf16[128,1024]{1,0:T(8,128)(2,1)S(1)}, bf16[128,1024]{1,0:T(8,128)(2,1)S(1...) custom-call(bf16[3,128,256]{2,1,0:T(8,128)(2,1)S(1)} %get-tuple-element.17.refs_0_.line_ref, ...), custom_call_target="tpu_custom_call" | custom-call | flops 268435456 | bytes 2097152 | tf_op jit(solution)/shard_map/mix/pallas_call | solution.py:150
  23.8 0.6 %collective-permute-start.11 = (bf16[128,1024]{1,0:T(8,128)(2,1)S(1)}, bf16[128,1024]{1,0:T(8,128)(2,1)S(1)}, u32[]{:S(2)}, u32[]{:S(2)}) collective-permute-start(bf16[128,1024]{1,0:T(8,128)(2,1)S(1)} %get-tuple-element.23), channel_id=1, source_target_pairs={{0,8},{8,0},{16,24},{24,16},{1,9},{9,1},{17,25},{25,17},{2,10},{10... | collective-permute-start | bytes 786440 | tf_op jit(solution)/shard_map/ppermute | solution.py:18
  24.4 3.4 %collective-permute-start.10 = (bf16[128,512]{1,0:T(8,128)(2,1)S(1)}, bf16[128,512]{1,0:T(8,128)(2,1)S(1)}, u32[]{:S(2)}, u32[]{:S(2)}) collective-permute-start(bf16[128,512]{1,0:T(8,128)(2,1)S(1)} %get-tuple-element.22.refs_8_), channel_id=1, source_target_pairs={{0,16},{8,24},{16,0},{24,8},{1,17},{9,25},{17,1},{25,9},{2,18},{10... | collective-permute-start | bytes 393224 | tf_op jit(solution)/shard_map/ppermute | solution.py:18
  27.8 2.4 %collective-permute-start.17 = (bf16[128,512]{1,0:T(8,128)(2,1)S(1)}, bf16[128,512]{1,0:T(8,128)(2,1)S(1)}, u32[]{:S(2)}, u32[]{:S(2)}) collective-permute-start(bf16[128,512]{1,0:T(8,128)(2,1)S(1)} %get-tuple-element.25.refs_0_), channel_id=1, source_target_pairs={{0,6},{1,7},{2,4},{3,5},{4,2},{5,3},{6,0},{7,1},{8,14},{9,15},{10,... | collective-permute-start | bytes 393224 | tf_op jit(solution)/shard_map/ppermute | solution.py:18
  30.3 0.5 %collective-permute-start.15 = (bf16[128,512]{1,0:T(8,128)(2,1)S(1)}, bf16[128,512]{1,0:T(8,128)(2,1)S(1)}, u32[]{:S(2)}, u32[]{:S(2)}) collective-permute-start(bf16[128,512]{1,0:T(8,128)(2,1)S(1)} %get-tuple-element.25.refs_0_), channel_id=1, source_target_pairs={{0,4},{1,5},{2,6},{3,7},{4,0},{5,1},{6,2},{7,3},{8,12},{9,13},{10,... | collective-permute-start | bytes 393224 | tf_op jit(solution)/shard_map/ppermute | solution.py:18
  30.8 0.5 %collective-permute-start.13 = (bf16[128,512]{1,0:T(8,128)(2,1)S(1)}, bf16[128,512]{1,0:T(8,128)(2,1)S(1)}, u32[]{:S(2)}, u32[]{:S(2)}) collective-permute-start(bf16[128,512]{1,0:T(8,128)(2,1)S(1)} %get-tuple-element.25.refs_0_), channel_id=1, source_target_pairs={{0,2},{1,3},{2,0},{3,1},{4,6},{5,7},{6,4},{7,5},{8,10},{9,11},{10,... | collective-permute-start | bytes 393224 | tf_op jit(solution)/shard_map/ppermute | solution.py:18
  31.3 0.8 %collective-permute-done.10.refs_9_ = bf16[128,512]{1,0:T(8,128)(2,1)S(1)} collective-permute-done((bf16[128,512]{1,0:T(8,128)(2,1)S(1)}, bf16[128,512]{1,0:T(8,128)(2,1)S(1)}, u32[]{:S(2)}, u32[]{:S(2)}) %collective-permute-start.10) | collective-permute-done | bytes 131104 | tf_op jit(solution)/shard_map/ppermute | solution.py:18
  32.2 2.6 %collective-permute-done.17.refs_6_ = bf16[128,512]{1,0:T(8,128)(2,1)S(1)} collective-permute-done((bf16[128,512]{1,0:T(8,128)(2,1)S(1)}, bf16[128,512]{1,0:T(8,128)(2,1)S(1)}, u32[]{:S(2)}, u32[]{:S(2)}) %collective-permute-start.17) | collective-permute-done | bytes 131104 | tf_op jit(solution)/shard_map/ppermute | solution.py:18
  34.8 1.3 %collective-permute-done.15.refs_4_ = bf16[128,512]{1,0:T(8,128)(2,1)S(1)} collective-permute-done((bf16[128,512]{1,0:T(8,128)(2,1)S(1)}, bf16[128,512]{1,0:T(8,128)(2,1)S(1)}, u32[]{:S(2)}, u32[]{:S(2)}) %collective-permute-start.15) | collective-permute-done | bytes 131104 | tf_op jit(solution)/shard_map/ppermute | solution.py:18
  36.7 1.4 %collective-permute-start.19 = (bf16[128,512]{1,0:T(8,128)(2,1)S(1)}, bf16[128,512]{1,0:T(8,128)(2,1)S(1)}, u32[]{:S(2)}, u32[]{:S(2)}) collective-permute-start(bf16[128,512]{1,0:T(8,128)(2,1)S(1)} %collective-permute-done.10.refs_9_), channel_id=1, source_target_pairs={{0,8},{8,0},{16,24},{24,16},{1,9},{9,1},{17,25},{25,17},{2,10},{10... | collective-permute-start | bytes 393224 | tf_op jit(solution)/shard_map/ppermute | solution.py:18
  38.1 0.7 %polar_share.1 = (bf16[2,128,256]{2,1,0:T(8,128)(2,1)S(1)}, f32[2,128,256]{2,1,0:T(8,128)S(1)}, f32[32,1,128]{2,1,0:T(1,128)S(1)}) custom-call(f32[1,128]{1,0:T(1,128)S(1)} %get-tuple-element.20.begun_ref, bf16[128,1024]{1,0:T(8,128)(2,1)S(1)} %get-tuple-element.21.weight_ref, bf16[1024,256]{1,0:T(8,128)(2,1)S(1)} %get-tuple-element.19.panel_ref, ...), custom_call_target="tpu_custom_call" | custom-call | flops 268435456 | bytes 4194304 | tf_op jit(solution)/shard_map/polar_share/pallas_call | solution.py:224
  38.8 10.2 %all_to_all.5.shares_ref = f32[32,1,128]{2,1,0:T(1,128)S(1)} all-to-all(f32[32,1,128]{2,1,0:T(1,128)S(1)} %get-tuple-element.28), channel_id=1, replica_groups=mesh['row'=4,'col'=2,'rep'=4] {'row','col','rep'}, dimensions={0} | all-to-all | bytes 32768 | tf_op jit(solution)/shard_map/all_to_all | solution.py:302
  49.0 1.5 %dress.1 = (bf16[128,4,256]{2,1,0:T(4,128)(2,1)}, f32[4,4]{1,0:T(4,128)}) custom-call(bf16[1024,256]{1,0:T(8,128)(2,1)S(1)} %get-tuple-element.19.panel_ref, bf16[2,128,256]{2,1,0:T(8,128)(2,1)S(1)} %get-tuple-element.26.first_ref, f32[2,128,256]{2,1,0:T(8,128)S(1)} %get-tuple-element.27.part_ref, f32[32,1,128]{2,1,0:T(1,128)S(1)} %all_to_all.5.shares_ref, ...), custom_call_target="tpu_custom_call" | custom-call | flops 67108864 | bytes 1048576 | tf_op jit(solution)/shard_map/dress/pallas_call | solution.py:265
  (21 shorter events, 0.7 us)
Async XLA Ops:
  2.4 13.3 %collective-permute-start.1 = (bf16[3,128,256]{2,1,0:T(8,128)(2,1)S(1)}, bf16[3,128,256]{2,1,0:T(8,128)(2,1)S(1)}, u32[]{:S(2)}, u32[]{:S(2)}) collective-permute-start(bf16[3,128,256]{2,1,0:T(8,128)(2,1)S(1)} %get-tuple-element.17.refs_0_.line_ref), channel_id=1, source_target_pairs={{0,16},{8,24},{16,0},{24,8},{1,17},{9,25},{17,1},{25,9},{2,18},{10... | collective-permute-start | bytes 589832 | tf_op jit(solution)/shard_map/ppermute | solution.py:18
  6.5 9.4 %collective-permute-start = (bf16[3,128,256]{2,1,0:T(8,128)(2,1)S(1)}, bf16[3,128,256]{2,1,0:T(8,128)(2,1)S(1)}, u32[]{:S(2)}, u32[]{:S(2)}) collective-permute-start(bf16[3,128,256]{2,1,0:T(8,128)(2,1)S(1)} %get-tuple-element.17.refs_0_.line_ref), channel_id=1, source_target_pairs={{0,8},{8,0},{16,24},{24,16},{1,9},{9,1},{17,25},{25,17},{2,10},{10... | collective-permute-start | bytes 589832 | tf_op jit(solution)/shard_map/ppermute | solution.py:18
  8.0 9.3 %collective-permute-start.8 = (bf16[3,128,256]{2,1,0:T(8,128)(2,1)S(1)}, bf16[3,128,256]{2,1,0:T(8,128)(2,1)S(1)}, u32[]{:S(2)}, u32[]{:S(2)}) collective-permute-start(bf16[3,128,256]{2,1,0:T(8,128)(2,1)S(1)} %get-tuple-element.18.refs_4_.bundle_ref), channel_id=1, source_target_pairs={{0,6},{1,7},{2,4},{3,5},{4,2},{5,3},{6,0},{7,1},{8,14},{9,15},{10,... | collective-permute-start | bytes 589832 | tf_op jit(solution)/shard_map/ppermute | solution.py:18
  10.5 8.8 %collective-permute-start.6 = (bf16[3,128,256]{2,1,0:T(8,128)(2,1)S(1)}, bf16[3,128,256]{2,1,0:T(8,128)(2,1)S(1)}, u32[]{:S(2)}, u32[]{:S(2)}) collective-permute-start(bf16[3,128,256]{2,1,0:T(8,128)(2,1)S(1)} %get-tuple-element.18.refs_4_.bundle_ref), channel_id=1, source_target_pairs={{0,4},{1,5},{2,6},{3,7},{4,0},{5,1},{6,2},{7,3},{8,12},{9,13},{10,... | collective-permute-start | bytes 589832 | tf_op jit(solution)/shard_map/ppermute | solution.py:18
  11.0 8.3 %collective-permute-start.4 = (bf16[3,128,256]{2,1,0:T(8,128)(2,1)S(1)}, bf16[3,128,256]{2,1,0:T(8,128)(2,1)S(1)}, u32[]{:S(2)}, u32[]{:S(2)}) collective-permute-start(bf16[3,128,256]{2,1,0:T(8,128)(2,1)S(1)} %get-tuple-element.18.refs_4_.bundle_ref), channel_id=1, source_target_pairs={{0,2},{1,3},{2,0},{3,1},{4,6},{5,7},{6,4},{7,5},{8,10},{9,11},{10,... | collective-permute-start | bytes 589832 | tf_op jit(solution)/shard_map/ppermute | solution.py:18
  15.7 4.2 %collective-permute-start.3 = (bf16[3,128,256]{2,1,0:T(8,128)(2,1)S(1)}, bf16[3,128,256]{2,1,0:T(8,128)(2,1)S(1)}, u32[]{:S(2)}, u32[]{:S(2)}) collective-permute-start(bf16[3,128,256]{2,1,0:T(8,128)(2,1)S(1)} %get-tuple-element.18.refs_4_.bundle_ref), channel_id=1, source_target_pairs={{0,1},{1,0},{2,3},{3,2},{4,5},{5,4},{6,7},{7,6},{8,9},{9,8},{10,11... | collective-permute-start | bytes 589832 | tf_op jit(solution)/shard_map/ppermute | solution.py:18
  15.9 7.1 %collective-permute-start.2 = (bf16[3,128,256]{2,1,0:T(8,128)(2,1)S(1)}, bf16[3,128,256]{2,1,0:T(8,128)(2,1)S(1)}, u32[]{:S(2)}, u32[]{:S(2)}) collective-permute-start(bf16[3,128,256]{2,1,0:T(8,128)(2,1)S(1)} %collective-permute-done.1.refs_2_), channel_id=1, source_target_pairs={{0,8},{8,0},{16,24},{24,16},{1,9},{9,1},{17,25},{25,17},{2,10},{10... | collective-permute-start | bytes 589832 | tf_op jit(solution)/shard_map/ppermute | solution.py:18
  17.4 5.6 %collective-permute-start.9 = (bf16[3,128,256]{2,1,0:T(8,128)(2,1)S(1)}, bf16[3,128,256]{2,1,0:T(8,128)(2,1)S(1)}, u32[]{:S(2)}, u32[]{:S(2)}) collective-permute-start(bf16[3,128,256]{2,1,0:T(8,128)(2,1)S(1)} %collective-permute-done.8.refs_10_), channel_id=1, source_target_pairs={{0,1},{1,0},{2,3},{3,2},{4,5},{5,4},{6,7},{7,6},{8,9},{9,8},{10,11... | collective-permute-start | bytes 589832 | tf_op jit(solution)/shard_map/ppermute | solution.py:18
  19.3 3.7 %collective-permute-start.7 = (bf16[3,128,256]{2,1,0:T(8,128)(2,1)S(1)}, bf16[3,128,256]{2,1,0:T(8,128)(2,1)S(1)}, u32[]{:S(2)}, u32[]{:S(2)}) collective-permute-start(bf16[3,128,256]{2,1,0:T(8,128)(2,1)S(1)} %collective-permute-done.6.refs_8_), channel_id=1, source_target_pairs={{0,1},{1,0},{2,3},{3,2},{4,5},{5,4},{6,7},{7,6},{8,9},{9,8},{10,11... | collective-permute-start | bytes 589832 | tf_op jit(solution)/shard_map/ppermute | solution.py:18
  19.3 3.7 %collective-permute-start.5 = (bf16[3,128,256]{2,1,0:T(8,128)(2,1)S(1)}, bf16[3,128,256]{2,1,0:T(8,128)(2,1)S(1)}, u32[]{:S(2)}, u32[]{:S(2)}) collective-permute-start(bf16[3,128,256]{2,1,0:T(8,128)(2,1)S(1)} %collective-permute-done.4.refs_6_), channel_id=1, source_target_pairs={{0,1},{1,0},{2,3},{3,2},{4,5},{5,4},{6,7},{7,6},{8,9},{9,8},{10,11... | collective-permute-start | bytes 589832 | tf_op jit(solution)/shard_map/ppermute | solution.py:18
  23.8 12.8 %collective-permute-start.11 = (bf16[128,1024]{1,0:T(8,128)(2,1)S(1)}, bf16[128,1024]{1,0:T(8,128)(2,1)S(1)}, u32[]{:S(2)}, u32[]{:S(2)}) collective-permute-start(bf16[128,1024]{1,0:T(8,128)(2,1)S(1)} %get-tuple-element.23), channel_id=1, source_target_pairs={{0,8},{8,0},{16,24},{24,16},{1,9},{9,1},{17,25},{25,17},{2,10},{10... | collective-permute-start | bytes 786440 | tf_op jit(solution)/shard_map/ppermute | solution.py:18
  24.4 7.7 %collective-permute-start.10 = (bf16[128,512]{1,0:T(8,128)(2,1)S(1)}, bf16[128,512]{1,0:T(8,128)(2,1)S(1)}, u32[]{:S(2)}, u32[]{:S(2)}) collective-permute-start(bf16[128,512]{1,0:T(8,128)(2,1)S(1)} %get-tuple-element.22.refs_8_), channel_id=1, source_target_pairs={{0,16},{8,24},{16,0},{24,8},{1,17},{9,25},{17,1},{25,9},{2,18},{10... | collective-permute-start | bytes 393224 | tf_op jit(solution)/shard_map/ppermute | solution.py:18
  27.8 7.0 %collective-permute-start.17 = (bf16[128,512]{1,0:T(8,128)(2,1)S(1)}, bf16[128,512]{1,0:T(8,128)(2,1)S(1)}, u32[]{:S(2)}, u32[]{:S(2)}) collective-permute-start(bf16[128,512]{1,0:T(8,128)(2,1)S(1)} %get-tuple-element.25.refs_0_), channel_id=1, source_target_pairs={{0,6},{1,7},{2,4},{3,5},{4,2},{5,3},{6,0},{7,1},{8,14},{9,15},{10,... | collective-permute-start | bytes 393224 | tf_op jit(solution)/shard_map/ppermute | solution.py:18
  30.3 5.9 %collective-permute-start.15 = (bf16[128,512]{1,0:T(8,128)(2,1)S(1)}, bf16[128,512]{1,0:T(8,128)(2,1)S(1)}, u32[]{:S(2)}, u32[]{:S(2)}) collective-permute-start(bf16[128,512]{1,0:T(8,128)(2,1)S(1)} %get-tuple-element.25.refs_0_), channel_id=1, source_target_pairs={{0,4},{1,5},{2,6},{3,7},{4,0},{5,1},{6,2},{7,3},{8,12},{9,13},{10,... | collective-permute-start | bytes 393224 | tf_op jit(solution)/shard_map/ppermute | solution.py:18
  30.8 5.4 %collective-permute-start.13 = (bf16[128,512]{1,0:T(8,128)(2,1)S(1)}, bf16[128,512]{1,0:T(8,128)(2,1)S(1)}, u32[]{:S(2)}, u32[]{:S(2)}) collective-permute-start(bf16[128,512]{1,0:T(8,128)(2,1)S(1)} %get-tuple-element.25.refs_0_), channel_id=1, source_target_pairs={{0,2},{1,3},{2,0},{3,1},{4,6},{5,7},{6,4},{7,5},{8,10},{9,11},{10,... | collective-permute-start | bytes 393224 | tf_op jit(solution)/shard_map/ppermute | solution.py:18
  32.2 5.9 %collective-permute-start.12 = (bf16[128,512]{1,0:T(8,128)(2,1)S(1)}, bf16[128,512]{1,0:T(8,128)(2,1)S(1)}, u32[]{:S(2)}, u32[]{:S(2)}) collective-permute-start(bf16[128,512]{1,0:T(8,128)(2,1)S(1)} %get-tuple-element.25.refs_0_), channel_id=1, source_target_pairs={{0,1},{1,0},{2,3},{3,2},{4,5},{5,4},{6,7},{7,6},{8,9},{9,8},{10,11... | collective-permute-start | bytes 393224 | tf_op jit(solution)/shard_map/ppermute | solution.py:18
  34.8 3.3 %collective-permute-start.18 = (bf16[128,512]{1,0:T(8,128)(2,1)S(1)}, bf16[128,512]{1,0:T(8,128)(2,1)S(1)}, u32[]{:S(2)}, u32[]{:S(2)}) collective-permute-start(bf16[128,512]{1,0:T(8,128)(2,1)S(1)} %collective-permute-done.17.refs_6_), channel_id=1, source_target_pairs={{0,1},{1,0},{2,3},{3,2},{4,5},{5,4},{6,7},{7,6},{8,9},{9,8},{10,11... | collective-permute-start | bytes 393224 | tf_op jit(solution)/shard_map/ppermute | solution.py:18
  36.1 1.9 %collective-permute-start.16 = (bf16[128,512]{1,0:T(8,128)(2,1)S(1)}, bf16[128,512]{1,0:T(8,128)(2,1)S(1)}, u32[]{:S(2)}, u32[]{:S(2)}) collective-permute-start(bf16[128,512]{1,0:T(8,128)(2,1)S(1)} %collective-permute-done.15.refs_4_), channel_id=1, source_target_pairs={{0,1},{1,0},{2,3},{3,2},{4,5},{5,4},{6,7},{7,6},{8,9},{9,8},{10,11... | collective-permute-start | bytes 393224 | tf_op jit(solution)/shard_map/ppermute | solution.py:18
  36.2 1.9 %collective-permute-start.14 = (bf16[128,512]{1,0:T(8,128)(2,1)S(1)}, bf16[128,512]{1,0:T(8,128)(2,1)S(1)}, u32[]{:S(2)}, u32[]{:S(2)}) collective-permute-start(bf16[128,512]{1,0:T(8,128)(2,1)S(1)} %collective-permute-done.13.refs_2_), channel_id=1, source_target_pairs={{0,1},{1,0},{2,3},{3,2},{4,5},{5,4},{6,7},{7,6},{8,9},{9,8},{10,11... | collective-permute-start | bytes 393224 | tf_op jit(solution)/shard_map/ppermute | solution.py:18
  36.7 12.3 %collective-permute-start.19 = (bf16[128,512]{1,0:T(8,128)(2,1)S(1)}, bf16[128,512]{1,0:T(8,128)(2,1)S(1)}, u32[]{:S(2)}, u32[]{:S(2)}) collective-permute-start(bf16[128,512]{1,0:T(8,128)(2,1)S(1)} %collective-permute-done.10.refs_9_), channel_id=1, source_target_pairs={{0,8},{8,0},{16,24},{24,16},{1,9},{9,1},{17,25},{25,17},{2,10},{10... | collective-permute-start | bytes 393224 | tf_op jit(solution)/shard_map/ppermute | solution.py:18

commit v4 on v2

--- a/solution.py
+++ b/solution.py
@@ -33,6 +33,15 @@
 
 def late(n_row):
     return list(range(3, n_row, 2))
+
+
+def chip_order(n_plane):
+    return [2 * (i ^ (i >> 1)) for i in range(1, n_plane // 2)]
+
+
+def by_distance(refs):
+    places = [k for chip in [0] + chip_order(len(refs)) for k in (chip, chip ^ 1)]
+    return [refs[places.index(k)] for k in range(len(refs))]
 
 
 def plane_index():
@@ -102,7 +111,7 @@
 
 
 def mix_kernel(n_row, n_plane, *refs):
-    lines, bundles = refs[:n_row], refs[n_row : n_row + n_plane]
+    lines, bundles = refs[:n_row], by_distance(refs[n_row : n_row + n_plane])
     half_ref, mixed_ref, both_ref, weight_ref, panel_ref, begun_ref = refs[n_row + n_plane :]
     planes, mu, nu = lines[0].shape
     cut, rest = planes - 1, bundles[0].shape[0] - 1
@@ -170,7 +179,7 @@
 
 
 def share_kernel(n_row, n_plane, begun_ref, weight_ref, panel_ref, line_ref, bundle_ref, near_ref, *refs):
-    halves, far = refs[:n_plane], refs[n_plane : n_plane + n_row // 2]
+    halves, far = by_distance(refs[:n_plane]), refs[n_plane : n_plane + n_row // 2]
     first_ref, part_ref, share_ref = refs[n_plane + n_row // 2 :]
     cut, mu, nu = first_ref.shape
     rest = part_ref.shape[0]
@@ -278,11 +287,10 @@
 def on_device(tensor_tiles, tile_pairs, tile_counts, occupied, virtual):
     aux = tensor_tiles.shape[1]
     n_row, n_plane = lax.axis_size("row"), lax.axis_size("col") * lax.axis_size("rep")
-    near = list(range(2, n_plane, 2))
     sibling = lambda value: flip(value, PLANE, 1, n_plane)
 
     def gather_plane(value):
-        values = [value] + [flip(value, PLANE, k, n_plane) for k in near]
+        values = [value] + [flip(value, PLANE, k, n_plane) for k in chip_order(n_plane)]
         return [held for value in values for held in (value, sibling(value))]
 
     line, bundle = place(tile_pairs, tile_counts, tensor_tiles, occupied, virtual)

time: 50.4 us -> 50.4 us (level)
  waiting for transfers between devices: 14.4 us -> 17 us
  starting transfers between devices: 20.5 us -> 18.7 us
  blocking collectives: 10.2 us -> 9.38 us
    ppermute x20, waiting for transfers between devices: 14.4 us -> 17 us  [flip(): return lax.ppermute(value, axes, [(i, i ^ mask) for i in range(count)])]
    ppermute x20, starting transfers between devices: 20.5 us -> 18.7 us  [flip(): return lax.ppermute(value, axes, [(i, i ^ mask) for i in range(count)])]
    all_to_all x1, blocking collectives: 10.2 us -> 9.38 us  [on_device(): lax.all_to_all(share, EVERY, 0, 0)]
  transfers between devices with their start and end apart: 20 -> 20, of which waited for: 8 -> 10; matrix products, arithmetic and copies ran while one was open for 0% -> 0% of each run, Pallas kernels for 1% -> 1%
where the time goes in v4:
time: 50.4 us; the launch traced here: 50.3 us
  starting transfers between devices  18.7 us (37%)
  waiting for transfers between devices  17 us (34%)
  blocking collectives  9.38 us (19%)
  Pallas kernels  3.85 us (8%)
  between operations  1.32 us (3%)
    ppermute x20, starting transfers between devices, flip(): return lax.ppermute(value, axes, [(i, i ^ mask) for i in range(count)])  18.7 us
    ppermute x20, waiting for transfers between devices, flip(): return lax.ppermute(value, axes, [(i, i ^ mask) for i in range(count)])  17 us
    all_to_all x1, blocking collectives, on_device(): lax.all_to_all(share, EVERY, 0, 0)  9.38 us
    pallas_call x1, Pallas kernels, dress(): pl.pallas_call(functools.partial(dress_kernel, n_row), out_shape=(jax.Sha...  1.3 us
    pallas_call x1, Pallas kernels, place(): pl.pallas_call(functools.partial(place_kernel, nu // tile), out_shape=[ja...  1.08 us
  transfers between devices with their start and end apart: 20, of which 10 were waited for; matrix products, arithmetic and copies ran while one was open for 0% of the time, Pallas kernels for 1%

profile of v4, /device:TPU:0, one launch (start us, length us, event | category | flops | bytes accessed | tf_op | source)
XLA Modules:
  0.0 50.3 jit_solution(2630572418452594199)
XLA Ops:
  1.3 1.1 %place.1 = (bf16[3,128,256]{2,1,0:T(8,128)(2,1)S(1)}, bf16[3,128,256]{2,1,0:T(8,128)(2,1)S(1)}) custom-call(s32[1]{0:T(128)S(6)} %copy.7.counts_ref, s32[2]{0:T(128)} %pairs_any.1, bf16[2,4,128,128]{3,2,1,0:T(8,128)(2,1)} %tiles_any.1, bf16[128,256]{1,0:T(8,128)(2,1)} %weight_any.1, bf16[128,256]{1,0:T(8,128)(2,1)} %column_any.1), custom_call_target="tpu_custom_call" | custom-call | bytes 786432 | tf_op jit(solution)/shard_map/place/pallas_call | solution.py:93
  2.4 4.1 %collective-permute-start.1 = (bf16[3,128,256]{2,1,0:T(8,128)(2,1)S(1)}, bf16[3,128,256]{2,1,0:T(8,128)(2,1)S(1)}, u32[]{:S(2)}, u32[]{:S(2)}) collective-permute-start(bf16[3,128,256]{2,1,0:T(8,128)(2,1)S(1)} %get-tuple-element.17.refs_0_.line_ref), channel_id=1, source_target_pairs={{0,16},{8,24},{16,0},{24,8},{1,17},{9,25},{17,1},{25,9},{2,18},{10... | collective-permute-start | bytes 589832 | tf_op jit(solution)/shard_map/ppermute | solution.py:18
  6.5 1.6 %collective-permute-start = (bf16[3,128,256]{2,1,0:T(8,128)(2,1)S(1)}, bf16[3,128,256]{2,1,0:T(8,128)(2,1)S(1)}, u32[]{:S(2)}, u32[]{:S(2)}) collective-permute-start(bf16[3,128,256]{2,1,0:T(8,128)(2,1)S(1)} %get-tuple-element.17.refs_0_.line_ref), channel_id=1, source_target_pairs={{0,8},{8,0},{16,24},{24,16},{1,9},{9,1},{17,25},{25,17},{2,10},{10... | collective-permute-start | bytes 589832 | tf_op jit(solution)/shard_map/ppermute | solution.py:18
  8.0 1.5 %collective-permute-start.8 = (bf16[3,128,256]{2,1,0:T(8,128)(2,1)S(1)}, bf16[3,128,256]{2,1,0:T(8,128)(2,1)S(1)}, u32[]{:S(2)}, u32[]{:S(2)}) collective-permute-start(bf16[3,128,256]{2,1,0:T(8,128)(2,1)S(1)} %get-tuple-element.18.refs_4_.bundle_ref), channel_id=1, source_target_pairs={{0,4},{1,5},{2,6},{3,7},{4,0},{5,1},{6,2},{7,3},{8,12},{9,13},{10,... | collective-permute-start | bytes 589832 | tf_op jit(solution)/shard_map/ppermute | solution.py:18
  9.5 1.5 %collective-permute-start.6 = (bf16[3,128,256]{2,1,0:T(8,128)(2,1)S(1)}, bf16[3,128,256]{2,1,0:T(8,128)(2,1)S(1)}, u32[]{:S(2)}, u32[]{:S(2)}) collective-permute-start(bf16[3,128,256]{2,1,0:T(8,128)(2,1)S(1)} %get-tuple-element.18.refs_4_.bundle_ref), channel_id=1, source_target_pairs={{0,6},{1,7},{2,4},{3,5},{4,2},{5,3},{6,0},{7,1},{8,14},{9,15},{10,... | collective-permute-start | bytes 589832 | tf_op jit(solution)/shard_map/ppermute | solution.py:18
  11.5 4.2 %collective-permute-done.1.refs_2_ = bf16[3,128,256]{2,1,0:T(8,128)(2,1)S(1)} collective-permute-done((bf16[3,128,256]{2,1,0:T(8,128)(2,1)S(1)}, bf16[3,128,256]{2,1,0:T(8,128)(2,1)S(1)}, u32[]{:S(2)}, u32[]{:S(2)}) %collective-permute-start.1) | collective-permute-done | bytes 196640 | tf_op jit(solution)/shard_map/ppermute | solution.py:18
  15.9 1.5 %collective-permute-start.2 = (bf16[3,128,256]{2,1,0:T(8,128)(2,1)S(1)}, bf16[3,128,256]{2,1,0:T(8,128)(2,1)S(1)}, u32[]{:S(2)}, u32[]{:S(2)}) collective-permute-start(bf16[3,128,256]{2,1,0:T(8,128)(2,1)S(1)} %collective-permute-done.1.refs_2_), channel_id=1, source_target_pairs={{0,8},{8,0},{16,24},{24,16},{1,9},{9,1},{17,25},{25,17},{2,10},{10... | collective-permute-start | bytes 589832 | tf_op jit(solution)/shard_map/ppermute | solution.py:18
  17.4 2.0 %collective-permute-done.6.refs_8_ = bf16[3,128,256]{2,1,0:T(8,128)(2,1)S(1)} collective-permute-done((bf16[3,128,256]{2,1,0:T(8,128)(2,1)S(1)}, bf16[3,128,256]{2,1,0:T(8,128)(2,1)S(1)}, u32[]{:S(2)}, u32[]{:S(2)}) %collective-permute-start.6) | collective-permute-done | bytes 196640 | tf_op jit(solution)/shard_map/ppermute | solution.py:18
  19.4 1.4 %collective-permute-done.4.refs_6_ = bf16[3,128,256]{2,1,0:T(8,128)(2,1)S(1)} collective-permute-done((bf16[3,128,256]{2,1,0:T(8,128)(2,1)S(1)}, bf16[3,128,256]{2,1,0:T(8,128)(2,1)S(1)}, u32[]{:S(2)}, u32[]{:S(2)}) %collective-permute-start.4) | collective-permute-done | bytes 196640 | tf_op jit(solution)/shard_map/ppermute | solution.py:18
  20.8 2.2 %collective-permute-done.2.refs_3_ = bf16[3,128,256]{2,1,0:T(8,128)(2,1)S(1)} collective-permute-done((bf16[3,128,256]{2,1,0:T(8,128)(2,1)S(1)}, bf16[3,128,256]{2,1,0:T(8,128)(2,1)S(1)}, u32[]{:S(2)}, u32[]{:S(2)}) %collective-permute-start.2) | collective-permute-done | bytes 196640 | tf_op jit(solution)/shard_map/ppermute | solution.py:18
  23.0 0.8 %mix.1 = (bf16[128,512]{1,0:T(8,128)(2,1)S(1)}, bf16[128,512]{1,0:T(8,128)(2,1)S(1)}, bf16[128,1024]{1,0:T(8,128)(2,1)S(1)}, bf16[128,1024]{1,0:T(8,128)(2,1)S(1...) custom-call(bf16[3,128,256]{2,1,0:T(8,128)(2,1)S(1)} %get-tuple-element.17.refs_0_.line_ref, ...), custom_call_target="tpu_custom_call" | custom-call | flops 268435456 | bytes 2097152 | tf_op jit(solution)/shard_map/mix/pallas_call | solution.py:159
  23.8 0.6 %collective-permute-start.11 = (bf16[128,1024]{1,0:T(8,128)(2,1)S(1)}, bf16[128,1024]{1,0:T(8,128)(2,1)S(1)}, u32[]{:S(2)}, u32[]{:S(2)}) collective-permute-start(bf16[128,1024]{1,0:T(8,128)(2,1)S(1)} %get-tuple-element.23), channel_id=1, source_target_pairs={{0,8},{8,0},{16,24},{24,16},{1,9},{9,1},{17,25},{25,17},{2,10},{10... | collective-permute-start | bytes 786440 | tf_op jit(solution)/shard_map/ppermute | solution.py:18
  24.4 3.4 %collective-permute-start.10 = (bf16[128,512]{1,0:T(8,128)(2,1)S(1)}, bf16[128,512]{1,0:T(8,128)(2,1)S(1)}, u32[]{:S(2)}, u32[]{:S(2)}) collective-permute-start(bf16[128,512]{1,0:T(8,128)(2,1)S(1)} %get-tuple-element.22.refs_8_), channel_id=1, source_target_pairs={{0,16},{8,24},{16,0},{24,8},{1,17},{9,25},{17,1},{25,9},{2,18},{10... | collective-permute-start | bytes 393224 | tf_op jit(solution)/shard_map/ppermute | solution.py:18
  27.8 1.5 %collective-permute-start.17 = (bf16[128,512]{1,0:T(8,128)(2,1)S(1)}, bf16[128,512]{1,0:T(8,128)(2,1)S(1)}, u32[]{:S(2)}, u32[]{:S(2)}) collective-permute-start(bf16[128,512]{1,0:T(8,128)(2,1)S(1)} %get-tuple-element.25.refs_0_), channel_id=1, source_target_pairs={{0,4},{1,5},{2,6},{3,7},{4,0},{5,1},{6,2},{7,3},{8,12},{9,13},{10,... | collective-permute-start | bytes 393224 | tf_op jit(solution)/shard_map/ppermute | solution.py:18
  29.3 1.5 %collective-permute-start.15 = (bf16[128,512]{1,0:T(8,128)(2,1)S(1)}, bf16[128,512]{1,0:T(8,128)(2,1)S(1)}, u32[]{:S(2)}, u32[]{:S(2)}) collective-permute-start(bf16[128,512]{1,0:T(8,128)(2,1)S(1)} %get-tuple-element.25.refs_0_), channel_id=1, source_target_pairs={{0,6},{1,7},{2,4},{3,5},{4,2},{5,3},{6,0},{7,1},{8,14},{9,15},{10,... | collective-permute-start | bytes 393224 | tf_op jit(solution)/shard_map/ppermute | solution.py:18
  30.8 0.5 %collective-permute-start.13 = (bf16[128,512]{1,0:T(8,128)(2,1)S(1)}, bf16[128,512]{1,0:T(8,128)(2,1)S(1)}, u32[]{:S(2)}, u32[]{:S(2)}) collective-permute-start(bf16[128,512]{1,0:T(8,128)(2,1)S(1)} %get-tuple-element.25.refs_0_), channel_id=1, source_target_pairs={{0,2},{1,3},{2,0},{3,1},{4,6},{5,7},{6,4},{7,5},{8,10},{9,11},{10,... | collective-permute-start | bytes 393224 | tf_op jit(solution)/shard_map/ppermute | solution.py:18
  31.3 0.9 %collective-permute-done.10.refs_9_ = bf16[128,512]{1,0:T(8,128)(2,1)S(1)} collective-permute-done((bf16[128,512]{1,0:T(8,128)(2,1)S(1)}, bf16[128,512]{1,0:T(8,128)(2,1)S(1)}, u32[]{:S(2)}, u32[]{:S(2)}) %collective-permute-start.10) | collective-permute-done | bytes 131104 | tf_op jit(solution)/shard_map/ppermute | solution.py:18
  32.2 1.8 %collective-permute-done.17.refs_6_ = bf16[128,512]{1,0:T(8,128)(2,1)S(1)} collective-permute-done((bf16[128,512]{1,0:T(8,128)(2,1)S(1)}, bf16[128,512]{1,0:T(8,128)(2,1)S(1)}, u32[]{:S(2)}, u32[]{:S(2)}) %collective-permute-start.17) | collective-permute-done | bytes 131104 | tf_op jit(solution)/shard_map/ppermute | solution.py:18
  33.9 2.3 %collective-permute-done.15.refs_4_ = bf16[128,512]{1,0:T(8,128)(2,1)S(1)} collective-permute-done((bf16[128,512]{1,0:T(8,128)(2,1)S(1)}, bf16[128,512]{1,0:T(8,128)(2,1)S(1)}, u32[]{:S(2)}, u32[]{:S(2)}) %collective-permute-start.15) | collective-permute-done | bytes 131104 | tf_op jit(solution)/shard_map/ppermute | solution.py:18
  36.2 1.3 %collective-permute-done.13.refs_2_ = bf16[128,512]{1,0:T(8,128)(2,1)S(1)} collective-permute-done((bf16[128,512]{1,0:T(8,128)(2,1)S(1)}, bf16[128,512]{1,0:T(8,128)(2,1)S(1)}, u32[]{:S(2)}, u32[]{:S(2)}) %collective-permute-start.13) | collective-permute-done | bytes 131104 | tf_op jit(solution)/shard_map/ppermute | solution.py:18
  38.1 0.8 %collective-permute-done.14.refs_3_ = bf16[128,512]{1,0:T(8,128)(2,1)S(1)} collective-permute-done((bf16[128,512]{1,0:T(8,128)(2,1)S(1)}, bf16[128,512]{1,0:T(8,128)(2,1)S(1)}, u32[]{:S(2)}, u32[]{:S(2)}) %collective-permute-start.14) | collective-permute-done | bytes 131104 | tf_op jit(solution)/shard_map/ppermute | solution.py:18
  38.9 0.7 %polar_share.1 = (bf16[2,128,256]{2,1,0:T(8,128)(2,1)S(1)}, f32[2,128,256]{2,1,0:T(8,128)S(1)}, f32[32,1,128]{2,1,0:T(1,128)S(1)}) custom-call(f32[1,128]{1,0:T(1,128)S(1)} %get-tuple-element.20.begun_ref, bf16[128,1024]{1,0:T(8,128)(2,1)S(1)} %get-tuple-element.21.weight_ref, bf16[1024,256]{1,0:T(8,128)(2,1)S(1)} %get-tuple-element.19.panel_ref, ...), custom_call_target="tpu_custom_call" | custom-call | flops 268435456 | bytes 4194304 | tf_op jit(solution)/shard_map/polar_share/pallas_call | solution.py:233
  39.6 9.4 %all_to_all.5.shares_ref = f32[32,1,128]{2,1,0:T(1,128)S(1)} all-to-all(f32[32,1,128]{2,1,0:T(1,128)S(1)} %get-tuple-element.28), channel_id=1, replica_groups=mesh['row'=4,'col'=2,'rep'=4] {'row','col','rep'}, dimensions={0} | all-to-all | bytes 32768 | tf_op jit(solution)/shard_map/all_to_all | solution.py:309
  49.0 1.3 %dress.1 = (bf16[128,4,256]{2,1,0:T(4,128)(2,1)}, f32[4,4]{1,0:T(4,128)}) custom-call(bf16[1024,256]{1,0:T(8,128)(2,1)S(1)} %get-tuple-element.19.panel_ref, bf16[2,128,256]{2,1,0:T(8,128)(2,1)S(1)} %get-tuple-element.26.first_ref, f32[2,128,256]{2,1,0:T(8,128)S(1)} %get-tuple-element.27.part_ref, f32[32,1,128]{2,1,0:T(1,128)S(1)} %all_to_all.5.shares_ref, ...), custom_call_target="tpu_custom_call" | custom-call | flops 67108864 | bytes 1048576 | tf_op jit(solution)/shard_map/dress/pallas_call | solution.py:273
  (21 shorter events, 1.2 us)
Async XLA Ops:
  2.4 13.3 %collective-permute-start.1 = (bf16[3,128,256]{2,1,0:T(8,128)(2,1)S(1)}, bf16[3,128,256]{2,1,0:T(8,128)(2,1)S(1)}, u32[]{:S(2)}, u32[]{:S(2)}) collective-permute-start(bf16[3,128,256]{2,1,0:T(8,128)(2,1)S(1)} %get-tuple-element.17.refs_0_.line_ref), channel_id=1, source_target_pairs={{0,16},{8,24},{16,0},{24,8},{1,17},{9,25},{17,1},{25,9},{2,18},{10... | collective-permute-start | bytes 589832 | tf_op jit(solution)/shard_map/ppermute | solution.py:18
  6.5 9.4 %collective-permute-start = (bf16[3,128,256]{2,1,0:T(8,128)(2,1)S(1)}, bf16[3,128,256]{2,1,0:T(8,128)(2,1)S(1)}, u32[]{:S(2)}, u32[]{:S(2)}) collective-permute-start(bf16[3,128,256]{2,1,0:T(8,128)(2,1)S(1)} %get-tuple-element.17.refs_0_.line_ref), channel_id=1, source_target_pairs={{0,8},{8,0},{16,24},{24,16},{1,9},{9,1},{17,25},{25,17},{2,10},{10... | collective-permute-start | bytes 589832 | tf_op jit(solution)/shard_map/ppermute | solution.py:18
  8.0 9.3 %collective-permute-start.8 = (bf16[3,128,256]{2,1,0:T(8,128)(2,1)S(1)}, bf16[3,128,256]{2,1,0:T(8,128)(2,1)S(1)}, u32[]{:S(2)}, u32[]{:S(2)}) collective-permute-start(bf16[3,128,256]{2,1,0:T(8,128)(2,1)S(1)} %get-tuple-element.18.refs_4_.bundle_ref), channel_id=1, source_target_pairs={{0,4},{1,5},{2,6},{3,7},{4,0},{5,1},{6,2},{7,3},{8,12},{9,13},{10,... | collective-permute-start | bytes 589832 | tf_op jit(solution)/shard_map/ppermute | solution.py:18
  9.5 9.9 %collective-permute-start.6 = (bf16[3,128,256]{2,1,0:T(8,128)(2,1)S(1)}, bf16[3,128,256]{2,1,0:T(8,128)(2,1)S(1)}, u32[]{:S(2)}, u32[]{:S(2)}) collective-permute-start(bf16[3,128,256]{2,1,0:T(8,128)(2,1)S(1)} %get-tuple-element.18.refs_4_.bundle_ref), channel_id=1, source_target_pairs={{0,6},{1,7},{2,4},{3,5},{4,2},{5,3},{6,0},{7,1},{8,14},{9,15},{10,... | collective-permute-start | bytes 589832 | tf_op jit(solution)/shard_map/ppermute | solution.py:18
  11.0 9.7 %collective-permute-start.4 = (bf16[3,128,256]{2,1,0:T(8,128)(2,1)S(1)}, bf16[3,128,256]{2,1,0:T(8,128)(2,1)S(1)}, u32[]{:S(2)}, u32[]{:S(2)}) collective-permute-start(bf16[3,128,256]{2,1,0:T(8,128)(2,1)S(1)} %get-tuple-element.18.refs_4_.bundle_ref), channel_id=1, source_target_pairs={{0,2},{1,3},{2,0},{3,1},{4,6},{5,7},{6,4},{7,5},{8,10},{9,11},{10,... | collective-permute-start | bytes 589832 | tf_op jit(solution)/shard_map/ppermute | solution.py:18
  15.7 5.1 %collective-permute-start.3 = (bf16[3,128,256]{2,1,0:T(8,128)(2,1)S(1)}, bf16[3,128,256]{2,1,0:T(8,128)(2,1)S(1)}, u32[]{:S(2)}, u32[]{:S(2)}) collective-permute-start(bf16[3,128,256]{2,1,0:T(8,128)(2,1)S(1)} %get-tuple-element.18.refs_4_.bundle_ref), channel_id=1, source_target_pairs={{0,1},{1,0},{2,3},{3,2},{4,5},{5,4},{6,7},{7,6},{8,9},{9,8},{10,11... | collective-permute-start | bytes 589832 | tf_op jit(solution)/shard_map/ppermute | solution.py:18
  15.9 7.1 %collective-permute-start.2 = (bf16[3,128,256]{2,1,0:T(8,128)(2,1)S(1)}, bf16[3,128,256]{2,1,0:T(8,128)(2,1)S(1)}, u32[]{:S(2)}, u32[]{:S(2)}) collective-permute-start(bf16[3,128,256]{2,1,0:T(8,128)(2,1)S(1)} %collective-permute-done.1.refs_2_), channel_id=1, source_target_pairs={{0,8},{8,0},{16,24},{24,16},{1,9},{9,1},{17,25},{25,17},{2,10},{10... | collective-permute-start | bytes 589832 | tf_op jit(solution)/shard_map/ppermute | solution.py:18
  17.4 5.6 %collective-permute-start.9 = (bf16[3,128,256]{2,1,0:T(8,128)(2,1)S(1)}, bf16[3,128,256]{2,1,0:T(8,128)(2,1)S(1)}, u32[]{:S(2)}, u32[]{:S(2)}) collective-permute-start(bf16[3,128,256]{2,1,0:T(8,128)(2,1)S(1)} %collective-permute-done.8.refs_10_), channel_id=1, source_target_pairs={{0,1},{1,0},{2,3},{3,2},{4,5},{5,4},{6,7},{7,6},{8,9},{9,8},{10,11... | collective-permute-start | bytes 589832 | tf_op jit(solution)/shard_map/ppermute | solution.py:18
  19.4 3.6 %collective-permute-start.7 = (bf16[3,128,256]{2,1,0:T(8,128)(2,1)S(1)}, bf16[3,128,256]{2,1,0:T(8,128)(2,1)S(1)}, u32[]{:S(2)}, u32[]{:S(2)}) collective-permute-start(bf16[3,128,256]{2,1,0:T(8,128)(2,1)S(1)} %collective-permute-done.6.refs_8_), channel_id=1, source_target_pairs={{0,1},{1,0},{2,3},{3,2},{4,5},{5,4},{6,7},{7,6},{8,9},{9,8},{10,11... | collective-permute-start | bytes 589832 | tf_op jit(solution)/shard_map/ppermute | solution.py:18
  20.8 2.3 %collective-permute-start.5 = (bf16[3,128,256]{2,1,0:T(8,128)(2,1)S(1)}, bf16[3,128,256]{2,1,0:T(8,128)(2,1)S(1)}, u32[]{:S(2)}, u32[]{:S(2)}) collective-permute-start(bf16[3,128,256]{2,1,0:T(8,128)(2,1)S(1)} %collective-permute-done.4.refs_6_), channel_id=1, source_target_pairs={{0,1},{1,0},{2,3},{3,2},{4,5},{5,4},{6,7},{7,6},{8,9},{9,8},{10,11... | collective-permute-start | bytes 589832 | tf_op jit(solution)/shard_map/ppermute | solution.py:18
  23.8 13.7 %collective-permute-start.11 = (bf16[128,1024]{1,0:T(8,128)(2,1)S(1)}, bf16[128,1024]{1,0:T(8,128)(2,1)S(1)}, u32[]{:S(2)}, u32[]{:S(2)}) collective-permute-start(bf16[128,1024]{1,0:T(8,128)(2,1)S(1)} %get-tuple-element.23), channel_id=1, source_target_pairs={{0,8},{8,0},{16,24},{24,16},{1,9},{9,1},{17,25},{25,17},{2,10},{10... | collective-permute-start | bytes 786440 | tf_op jit(solution)/shard_map/ppermute | solution.py:18
  24.4 7.7 %collective-permute-start.10 = (bf16[128,512]{1,0:T(8,128)(2,1)S(1)}, bf16[128,512]{1,0:T(8,128)(2,1)S(1)}, u32[]{:S(2)}, u32[]{:S(2)}) collective-permute-start(bf16[128,512]{1,0:T(8,128)(2,1)S(1)} %get-tuple-element.22.refs_8_), channel_id=1, source_target_pairs={{0,16},{8,24},{16,0},{24,8},{1,17},{9,25},{17,1},{25,9},{2,18},{10... | collective-permute-start | bytes 393224 | tf_op jit(solution)/shard_map/ppermute | solution.py:18
  27.8 6.1 %collective-permute-start.17 = (bf16[128,512]{1,0:T(8,128)(2,1)S(1)}, bf16[128,512]{1,0:T(8,128)(2,1)S(1)}, u32[]{:S(2)}, u32[]{:S(2)}) collective-permute-start(bf16[128,512]{1,0:T(8,128)(2,1)S(1)} %get-tuple-element.25.refs_0_), channel_id=1, source_target_pairs={{0,4},{1,5},{2,6},{3,7},{4,0},{5,1},{6,2},{7,3},{8,12},{9,13},{10,... | collective-permute-start | bytes 393224 | tf_op jit(solution)/shard_map/ppermute | solution.py:18
  29.3 6.9 %collective-permute-start.15 = (bf16[128,512]{1,0:T(8,128)(2,1)S(1)}, bf16[128,512]{1,0:T(8,128)(2,1)S(1)}, u32[]{:S(2)}, u32[]{:S(2)}) collective-permute-start(bf16[128,512]{1,0:T(8,128)(2,1)S(1)} %get-tuple-element.25.refs_0_), channel_id=1, source_target_pairs={{0,6},{1,7},{2,4},{3,5},{4,2},{5,3},{6,0},{7,1},{8,14},{9,15},{10,... | collective-permute-start | bytes 393224 | tf_op jit(solution)/shard_map/ppermute | solution.py:18
  30.8 6.7 %collective-permute-start.13 = (bf16[128,512]{1,0:T(8,128)(2,1)S(1)}, bf16[128,512]{1,0:T(8,128)(2,1)S(1)}, u32[]{:S(2)}, u32[]{:S(2)}) collective-permute-start(bf16[128,512]{1,0:T(8,128)(2,1)S(1)} %get-tuple-element.25.refs_0_), channel_id=1, source_target_pairs={{0,2},{1,3},{2,0},{3,1},{4,6},{5,7},{6,4},{7,5},{8,10},{9,11},{10,... | collective-permute-start | bytes 393224 | tf_op jit(solution)/shard_map/ppermute | solution.py:18
  32.2 5.9 %collective-permute-start.12 = (bf16[128,512]{1,0:T(8,128)(2,1)S(1)}, bf16[128,512]{1,0:T(8,128)(2,1)S(1)}, u32[]{:S(2)}, u32[]{:S(2)}) collective-permute-start(bf16[128,512]{1,0:T(8,128)(2,1)S(1)} %get-tuple-element.25.refs_0_), channel_id=1, source_target_pairs={{0,1},{1,0},{2,3},{3,2},{4,5},{5,4},{6,7},{7,6},{8,9},{9,8},{10,11... | collective-permute-start | bytes 393224 | tf_op jit(solution)/shard_map/ppermute | solution.py:18
  33.9 4.1 %collective-permute-start.18 = (bf16[128,512]{1,0:T(8,128)(2,1)S(1)}, bf16[128,512]{1,0:T(8,128)(2,1)S(1)}, u32[]{:S(2)}, u32[]{:S(2)}) collective-permute-start(bf16[128,512]{1,0:T(8,128)(2,1)S(1)} %collective-permute-done.17.refs_6_), channel_id=1, source_target_pairs={{0,1},{1,0},{2,3},{3,2},{4,5},{5,4},{6,7},{7,6},{8,9},{9,8},{10,11... | collective-permute-start | bytes 393224 | tf_op jit(solution)/shard_map/ppermute | solution.py:18
  36.2 1.8 %collective-permute-start.16 = (bf16[128,512]{1,0:T(8,128)(2,1)S(1)}, bf16[128,512]{1,0:T(8,128)(2,1)S(1)}, u32[]{:S(2)}, u32[]{:S(2)}) collective-permute-start(bf16[128,512]{1,0:T(8,128)(2,1)S(1)} %collective-permute-done.15.refs_4_), channel_id=1, source_target_pairs={{0,1},{1,0},{2,3},{3,2},{4,5},{5,4},{6,7},{7,6},{8,9},{9,8},{10,11... | collective-permute-start | bytes 393224 | tf_op jit(solution)/shard_map/ppermute | solution.py:18
  37.5 1.3 %collective-permute-start.14 = (bf16[128,512]{1,0:T(8,128)(2,1)S(1)}, bf16[128,512]{1,0:T(8,128)(2,1)S(1)}, u32[]{:S(2)}, u32[]{:S(2)}) collective-permute-start(bf16[128,512]{1,0:T(8,128)(2,1)S(1)} %collective-permute-done.13.refs_2_), channel_id=1, source_target_pairs={{0,1},{1,0},{2,3},{3,2},{4,5},{5,4},{6,7},{7,6},{8,9},{9,8},{10,11... | collective-permute-start | bytes 393224 | tf_op jit(solution)/shard_map/ppermute | solution.py:18
  37.5 11.4 %collective-permute-start.19 = (bf16[128,512]{1,0:T(8,128)(2,1)S(1)}, bf16[128,512]{1,0:T(8,128)(2,1)S(1)}, u32[]{:S(2)}, u32[]{:S(2)}) collective-permute-start(bf16[128,512]{1,0:T(8,128)(2,1)S(1)} %collective-permute-done.10.refs_9_), channel_id=1, source_target_pairs={{0,8},{8,0},{16,24},{24,16},{1,9},{9,1},{17,25},{25,17},{2,10},{10... | collective-permute-start | bytes 393224 | tf_op jit(solution)/shard_map/ppermute | solution.py:18

commit v5 on v4

--- a/solution.py
+++ b/solution.py
@@ -110,6 +110,11 @@
     return jnp.dot(left, right, preferred_element_type=jnp.float32)
 
 
+def pair(weight_ref, plane, k, mu):
+    spots = [pl.ds(pl.multiple_of((plane ^ i) * mu, mu), mu) for i in (k, k + 1)]
+    return jnp.concatenate([weight_ref[:, spot] for spot in spots], axis=1)
+
+
 def mix_kernel(n_row, n_plane, *refs):
     lines, bundles = refs[:n_row], by_distance(refs[n_row : n_row + n_plane])
     half_ref, mixed_ref, both_ref, weight_ref, panel_ref, begun_ref = refs[n_row + n_plane :]
@@ -132,9 +137,8 @@
     begun = jnp.zeros(begun_ref.shape, jnp.float32)
     for p in range(rest):
         total = jnp.zeros((mu, nu), jnp.float32)
-        for k in range(n_plane):
-            at = pl.multiple_of((plane ^ k) * mu, mu)
-            total += dot(weight_ref[:, pl.ds(at, mu)], bundles[k][p])
+        for k in range(0, n_plane, 2):
+            total += dot(pair(weight_ref, plane, k, mu), jnp.concatenate([bundles[k][p], bundles[k + 1][p]], axis=0))
         for q, value in enumerate(halves):
             folded = jnp.sum((total * value).reshape(mu // 8, 8, nu), axis=0)
             own = jnp.sum(jnp.sum(folded, axis=0, keepdims=True), axis=1, keepdims=True)
@@ -201,9 +205,10 @@
 
     for q in range(cut):
         total = jnp.zeros((mu, nu), jnp.float32)
-        for k in range(n_plane):
-            at = pl.multiple_of((plane ^ k) * mu, mu)
-            total += dot(weight_ref[:, pl.ds(at, mu)], halves[k][:, q * nu : (q + 1) * nu])
+        columns = slice(q * nu, (q + 1) * nu)
+        for k in range(0, n_plane, 2):
+            both = jnp.concatenate([halves[k][:, columns], halves[k + 1][:, columns]], axis=0)
+            total += dot(pair(weight_ref, plane, k, mu), both)
         rounded = total.astype(first_ref.dtype)
         first_ref[q] = rounded
         for p in range(aux):

time: 50.4 us -> 50.2 us (level)
  no operation moved by 1% of the time
where the time goes in v5:
time: 50.2 us; the launch traced here: 50 us
  starting transfers between devices  18.7 us (37%)
  waiting for transfers between devices  17 us (34%)
  blocking collectives  9.38 us (19%)
  Pallas kernels  3.62 us (7%)
  between operations  1.32 us (3%)
    ppermute x20, starting transfers between devices, flip(): return lax.ppermute(value, axes, [(i, i ^ mask) for i in range(count)])  18.7 us
    ppermute x20, waiting for transfers between devices, flip(): return lax.ppermute(value, axes, [(i, i ^ mask) for i in range(count)])  17 us
    all_to_all x1, blocking collectives, on_device(): lax.all_to_all(share, EVERY, 0, 0)  9.38 us
    pallas_call x1, Pallas kernels, dress(): pl.pallas_call(functools.partial(dress_kernel, n_row), out_shape=(jax.Sha...  1.3 us
    pallas_call x1, Pallas kernels, place(): pl.pallas_call(functools.partial(place_kernel, nu // tile), out_shape=[ja...  1.07 us
  transfers between devices with their start and end apart: 20, of which 10 were waited for; matrix products, arithmetic and copies ran while one was open for 0% of the time, Pallas kernels for 1%

profile of v5, /device:TPU:0, one launch (start us, length us, event | category | flops | bytes accessed | tf_op | source)
XLA Modules:
  0.0 50.0 jit_solution(2096969755884058405)
XLA Ops:
  1.3 1.1 %place.1 = (bf16[3,128,256]{2,1,0:T(8,128)(2,1)S(1)}, bf16[3,128,256]{2,1,0:T(8,128)(2,1)S(1)}) custom-call(s32[1]{0:T(128)S(6)} %copy.7.counts_ref, s32[2]{0:T(128)} %pairs_any.1, bf16[2,4,128,128]{3,2,1,0:T(8,128)(2,1)} %tiles_any.1, bf16[128,256]{1,0:T(8,128)(2,1)} %weight_any.1, bf16[128,256]{1,0:T(8,128)(2,1)} %column_any.1), custom_call_target="tpu_custom_call" | custom-call | bytes 786432 | tf_op jit(solution)/shard_map/place/pallas_call | solution.py:93
  2.4 4.1 %collective-permute-start.1 = (bf16[3,128,256]{2,1,0:T(8,128)(2,1)S(1)}, bf16[3,128,256]{2,1,0:T(8,128)(2,1)S(1)}, u32[]{:S(2)}, u32[]{:S(2)}) collective-permute-start(bf16[3,128,256]{2,1,0:T(8,128)(2,1)S(1)} %get-tuple-element.17.refs_0_.line_ref), channel_id=1, source_target_pairs={{0,16},{8,24},{16,0},{24,8},{1,17},{9,25},{17,1},{25,9},{2,18},{10... | collective-permute-start | bytes 589832 | tf_op jit(solution)/shard_map/ppermute | solution.py:18
  6.5 1.6 %collective-permute-start = (bf16[3,128,256]{2,1,0:T(8,128)(2,1)S(1)}, bf16[3,128,256]{2,1,0:T(8,128)(2,1)S(1)}, u32[]{:S(2)}, u32[]{:S(2)}) collective-permute-start(bf16[3,128,256]{2,1,0:T(8,128)(2,1)S(1)} %get-tuple-element.17.refs_0_.line_ref), channel_id=1, source_target_pairs={{0,8},{8,0},{16,24},{24,16},{1,9},{9,1},{17,25},{25,17},{2,10},{10... | collective-permute-start | bytes 589832 | tf_op jit(solution)/shard_map/ppermute | solution.py:18
  8.0 1.5 %collective-permute-start.8 = (bf16[3,128,256]{2,1,0:T(8,128)(2,1)S(1)}, bf16[3,128,256]{2,1,0:T(8,128)(2,1)S(1)}, u32[]{:S(2)}, u32[]{:S(2)}) collective-permute-start(bf16[3,128,256]{2,1,0:T(8,128)(2,1)S(1)} %get-tuple-element.18.refs_4_.bundle_ref), channel_id=1, source_target_pairs={{0,4},{1,5},{2,6},{3,7},{4,0},{5,1},{6,2},{7,3},{8,12},{9,13},{10,... | collective-permute-start | bytes 589832 | tf_op jit(solution)/shard_map/ppermute | solution.py:18
  9.5 1.5 %collective-permute-start.6 = (bf16[3,128,256]{2,1,0:T(8,128)(2,1)S(1)}, bf16[3,128,256]{2,1,0:T(8,128)(2,1)S(1)}, u32[]{:S(2)}, u32[]{:S(2)}) collective-permute-start(bf16[3,128,256]{2,1,0:T(8,128)(2,1)S(1)} %get-tuple-element.18.refs_4_.bundle_ref), channel_id=1, source_target_pairs={{0,6},{1,7},{2,4},{3,5},{4,2},{5,3},{6,0},{7,1},{8,14},{9,15},{10,... | collective-permute-start | bytes 589832 | tf_op jit(solution)/shard_map/ppermute | solution.py:18
  11.5 4.2 %collective-permute-done.1.refs_2_ = bf16[3,128,256]{2,1,0:T(8,128)(2,1)S(1)} collective-permute-done((bf16[3,128,256]{2,1,0:T(8,128)(2,1)S(1)}, bf16[3,128,256]{2,1,0:T(8,128)(2,1)S(1)}, u32[]{:S(2)}, u32[]{:S(2)}) %collective-permute-start.1) | collective-permute-done | bytes 196640 | tf_op jit(solution)/shard_map/ppermute | solution.py:18
  15.9 1.5 %collective-permute-start.2 = (bf16[3,128,256]{2,1,0:T(8,128)(2,1)S(1)}, bf16[3,128,256]{2,1,0:T(8,128)(2,1)S(1)}, u32[]{:S(2)}, u32[]{:S(2)}) collective-permute-start(bf16[3,128,256]{2,1,0:T(8,128)(2,1)S(1)} %collective-permute-done.1.refs_2_), channel_id=1, source_target_pairs={{0,8},{8,0},{16,24},{24,16},{1,9},{9,1},{17,25},{25,17},{2,10},{10... | collective-permute-start | bytes 589832 | tf_op jit(solution)/shard_map/ppermute | solution.py:18
  17.4 2.0 %collective-permute-done.6.refs_8_ = bf16[3,128,256]{2,1,0:T(8,128)(2,1)S(1)} collective-permute-done((bf16[3,128,256]{2,1,0:T(8,128)(2,1)S(1)}, bf16[3,128,256]{2,1,0:T(8,128)(2,1)S(1)}, u32[]{:S(2)}, u32[]{:S(2)}) %collective-permute-start.6) | collective-permute-done | bytes 196640 | tf_op jit(solution)/shard_map/ppermute | solution.py:18
  19.4 1.4 %collective-permute-done.4.refs_6_ = bf16[3,128,256]{2,1,0:T(8,128)(2,1)S(1)} collective-permute-done((bf16[3,128,256]{2,1,0:T(8,128)(2,1)S(1)}, bf16[3,128,256]{2,1,0:T(8,128)(2,1)S(1)}, u32[]{:S(2)}, u32[]{:S(2)}) %collective-permute-start.4) | collective-permute-done | bytes 196640 | tf_op jit(solution)/shard_map/ppermute | solution.py:18
  20.8 2.2 %collective-permute-done.2.refs_3_ = bf16[3,128,256]{2,1,0:T(8,128)(2,1)S(1)} collective-permute-done((bf16[3,128,256]{2,1,0:T(8,128)(2,1)S(1)}, bf16[3,128,256]{2,1,0:T(8,128)(2,1)S(1)}, u32[]{:S(2)}, u32[]{:S(2)}) %collective-permute-start.2) | collective-permute-done | bytes 196640 | tf_op jit(solution)/shard_map/ppermute | solution.py:18
  23.0 0.7 %mix.1 = (bf16[128,512]{1,0:T(8,128)(2,1)S(1)}, bf16[128,512]{1,0:T(8,128)(2,1)S(1)}, bf16[128,1024]{1,0:T(8,128)(2,1)S(1)}, bf16[128,1024]{1,0:T(8,128)(2,1)S(1...) custom-call(bf16[3,128,256]{2,1,0:T(8,128)(2,1)S(1)} %get-tuple-element.17.refs_0_.line_ref, ...), custom_call_target="tpu_custom_call" | custom-call | flops 268435456 | bytes 2097152 | tf_op jit(solution)/shard_map/mix/pallas_call | solution.py:163
  23.7 0.6 %collective-permute-start.11 = (bf16[128,1024]{1,0:T(8,128)(2,1)S(1)}, bf16[128,1024]{1,0:T(8,128)(2,1)S(1)}, u32[]{:S(2)}, u32[]{:S(2)}) collective-permute-start(bf16[128,1024]{1,0:T(8,128)(2,1)S(1)} %get-tuple-element.23), channel_id=1, source_target_pairs={{0,8},{8,0},{16,24},{24,16},{1,9},{9,1},{17,25},{25,17},{2,10},{10... | collective-permute-start | bytes 786440 | tf_op jit(solution)/shard_map/ppermute | solution.py:18
  24.3 3.4 %collective-permute-start.10 = (bf16[128,512]{1,0:T(8,128)(2,1)S(1)}, bf16[128,512]{1,0:T(8,128)(2,1)S(1)}, u32[]{:S(2)}, u32[]{:S(2)}) collective-permute-start(bf16[128,512]{1,0:T(8,128)(2,1)S(1)} %get-tuple-element.22.refs_8_), channel_id=1, source_target_pairs={{0,16},{8,24},{16,0},{24,8},{1,17},{9,25},{17,1},{25,9},{2,18},{10... | collective-permute-start | bytes 393224 | tf_op jit(solution)/shard_map/ppermute | solution.py:18
  27.7 1.5 %collective-permute-start.17 = (bf16[128,512]{1,0:T(8,128)(2,1)S(1)}, bf16[128,512]{1,0:T(8,128)(2,1)S(1)}, u32[]{:S(2)}, u32[]{:S(2)}) collective-permute-start(bf16[128,512]{1,0:T(8,128)(2,1)S(1)} %get-tuple-element.25.refs_0_), channel_id=1, source_target_pairs={{0,4},{1,5},{2,6},{3,7},{4,0},{5,1},{6,2},{7,3},{8,12},{9,13},{10,... | collective-permute-start | bytes 393224 | tf_op jit(solution)/shard_map/ppermute | solution.py:18
  29.2 1.5 %collective-permute-start.15 = (bf16[128,512]{1,0:T(8,128)(2,1)S(1)}, bf16[128,512]{1,0:T(8,128)(2,1)S(1)}, u32[]{:S(2)}, u32[]{:S(2)}) collective-permute-start(bf16[128,512]{1,0:T(8,128)(2,1)S(1)} %get-tuple-element.25.refs_0_), channel_id=1, source_target_pairs={{0,6},{1,7},{2,4},{3,5},{4,2},{5,3},{6,0},{7,1},{8,14},{9,15},{10,... | collective-permute-start | bytes 393224 | tf_op jit(solution)/shard_map/ppermute | solution.py:18
  30.7 0.5 %collective-permute-start.13 = (bf16[128,512]{1,0:T(8,128)(2,1)S(1)}, bf16[128,512]{1,0:T(8,128)(2,1)S(1)}, u32[]{:S(2)}, u32[]{:S(2)}) collective-permute-start(bf16[128,512]{1,0:T(8,128)(2,1)S(1)} %get-tuple-element.25.refs_0_), channel_id=1, source_target_pairs={{0,2},{1,3},{2,0},{3,1},{4,6},{5,7},{6,4},{7,5},{8,10},{9,11},{10,... | collective-permute-start | bytes 393224 | tf_op jit(solution)/shard_map/ppermute | solution.py:18
  31.2 0.8 %collective-permute-done.10.refs_9_ = bf16[128,512]{1,0:T(8,128)(2,1)S(1)} collective-permute-done((bf16[128,512]{1,0:T(8,128)(2,1)S(1)}, bf16[128,512]{1,0:T(8,128)(2,1)S(1)}, u32[]{:S(2)}, u32[]{:S(2)}) %collective-permute-start.10) | collective-permute-done | bytes 131104 | tf_op jit(solution)/shard_map/ppermute | solution.py:18
  32.0 1.8 %collective-permute-done.17.refs_6_ = bf16[128,512]{1,0:T(8,128)(2,1)S(1)} collective-permute-done((bf16[128,512]{1,0:T(8,128)(2,1)S(1)}, bf16[128,512]{1,0:T(8,128)(2,1)S(1)}, u32[]{:S(2)}, u32[]{:S(2)}) %collective-permute-start.17) | collective-permute-done | bytes 131104 | tf_op jit(solution)/shard_map/ppermute | solution.py:18
  33.8 2.3 %collective-permute-done.15.refs_4_ = bf16[128,512]{1,0:T(8,128)(2,1)S(1)} collective-permute-done((bf16[128,512]{1,0:T(8,128)(2,1)S(1)}, bf16[128,512]{1,0:T(8,128)(2,1)S(1)}, u32[]{:S(2)}, u32[]{:S(2)}) %collective-permute-start.15) | collective-permute-done | bytes 131104 | tf_op jit(solution)/shard_map/ppermute | solution.py:18
  36.1 1.3 %collective-permute-done.13.refs_2_ = bf16[128,512]{1,0:T(8,128)(2,1)S(1)} collective-permute-done((bf16[128,512]{1,0:T(8,128)(2,1)S(1)}, bf16[128,512]{1,0:T(8,128)(2,1)S(1)}, u32[]{:S(2)}, u32[]{:S(2)}) %collective-permute-start.13) | collective-permute-done | bytes 131104 | tf_op jit(solution)/shard_map/ppermute | solution.py:18
  37.9 0.8 %collective-permute-done.14.refs_3_ = bf16[128,512]{1,0:T(8,128)(2,1)S(1)} collective-permute-done((bf16[128,512]{1,0:T(8,128)(2,1)S(1)}, bf16[128,512]{1,0:T(8,128)(2,1)S(1)}, u32[]{:S(2)}, u32[]{:S(2)}) %collective-permute-start.14) | collective-permute-done | bytes 131104 | tf_op jit(solution)/shard_map/ppermute | solution.py:18
  38.8 0.6 %polar_share.1 = (bf16[2,128,256]{2,1,0:T(8,128)(2,1)S(1)}, f32[2,128,256]{2,1,0:T(8,128)S(1)}, f32[32,1,128]{2,1,0:T(1,128)S(1)}) custom-call(f32[1,128]{1,0:T(1,128)S(1)} %get-tuple-element.20.begun_ref, bf16[128,1024]{1,0:T(8,128)(2,1)S(1)} %get-tuple-element.21.weight_ref, bf16[1024,256]{1,0:T(8,128)(2,1)S(1)} %get-tuple-element.19.panel_ref, ...), custom_call_target="tpu_custom_call" | custom-call | flops 268435456 | bytes 4194304 | tf_op jit(solution)/shard_map/polar_share/pallas_call | solution.py:238
  39.3 9.4 %all_to_all.5.shares_ref = f32[32,1,128]{2,1,0:T(1,128)S(1)} all-to-all(f32[32,1,128]{2,1,0:T(1,128)S(1)} %get-tuple-element.28), channel_id=1, replica_groups=mesh['row'=4,'col'=2,'rep'=4] {'row','col','rep'}, dimensions={0} | all-to-all | bytes 32768 | tf_op jit(solution)/shard_map/all_to_all | solution.py:314
  48.7 1.3 %dress.1 = (bf16[128,4,256]{2,1,0:T(4,128)(2,1)}, f32[4,4]{1,0:T(4,128)}) custom-call(bf16[1024,256]{1,0:T(8,128)(2,1)S(1)} %get-tuple-element.19.panel_ref, bf16[2,128,256]{2,1,0:T(8,128)(2,1)S(1)} %get-tuple-element.26.first_ref, f32[2,128,256]{2,1,0:T(8,128)S(1)} %get-tuple-element.27.part_ref, f32[32,1,128]{2,1,0:T(1,128)S(1)} %all_to_all.5.shares_ref, ...), custom_call_target="tpu_custom_call" | custom-call | flops 67108864 | bytes 1048576 | tf_op jit(solution)/shard_map/dress/pallas_call | solution.py:278
  (21 shorter events, 1.2 us)
Async XLA Ops:
  2.4 13.3 %collective-permute-start.1 = (bf16[3,128,256]{2,1,0:T(8,128)(2,1)S(1)}, bf16[3,128,256]{2,1,0:T(8,128)(2,1)S(1)}, u32[]{:S(2)}, u32[]{:S(2)}) collective-permute-start(bf16[3,128,256]{2,1,0:T(8,128)(2,1)S(1)} %get-tuple-element.17.refs_0_.line_ref), channel_id=1, source_target_pairs={{0,16},{8,24},{16,0},{24,8},{1,17},{9,25},{17,1},{25,9},{2,18},{10... | collective-permute-start | bytes 589832 | tf_op jit(solution)/shard_map/ppermute | solution.py:18
  6.5 9.4 %collective-permute-start = (bf16[3,128,256]{2,1,0:T(8,128)(2,1)S(1)}, bf16[3,128,256]{2,1,0:T(8,128)(2,1)S(1)}, u32[]{:S(2)}, u32[]{:S(2)}) collective-permute-start(bf16[3,128,256]{2,1,0:T(8,128)(2,1)S(1)} %get-tuple-element.17.refs_0_.line_ref), channel_id=1, source_target_pairs={{0,8},{8,0},{16,24},{24,16},{1,9},{9,1},{17,25},{25,17},{2,10},{10... | collective-permute-start | bytes 589832 | tf_op jit(solution)/shard_map/ppermute | solution.py:18
  8.0 9.3 %collective-permute-start.8 = (bf16[3,128,256]{2,1,0:T(8,128)(2,1)S(1)}, bf16[3,128,256]{2,1,0:T(8,128)(2,1)S(1)}, u32[]{:S(2)}, u32[]{:S(2)}) collective-permute-start(bf16[3,128,256]{2,1,0:T(8,128)(2,1)S(1)} %get-tuple-element.18.refs_4_.bundle_ref), channel_id=1, source_target_pairs={{0,4},{1,5},{2,6},{3,7},{4,0},{5,1},{6,2},{7,3},{8,12},{9,13},{10,... | collective-permute-start | bytes 589832 | tf_op jit(solution)/shard_map/ppermute | solution.py:18
  9.5 9.9 %collective-permute-start.6 = (bf16[3,128,256]{2,1,0:T(8,128)(2,1)S(1)}, bf16[3,128,256]{2,1,0:T(8,128)(2,1)S(1)}, u32[]{:S(2)}, u32[]{:S(2)}) collective-permute-start(bf16[3,128,256]{2,1,0:T(8,128)(2,1)S(1)} %get-tuple-element.18.refs_4_.bundle_ref), channel_id=1, source_target_pairs={{0,6},{1,7},{2,4},{3,5},{4,2},{5,3},{6,0},{7,1},{8,14},{9,15},{10,... | collective-permute-start | bytes 589832 | tf_op jit(solution)/shard_map/ppermute | solution.py:18
  11.0 9.7 %collective-permute-start.4 = (bf16[3,128,256]{2,1,0:T(8,128)(2,1)S(1)}, bf16[3,128,256]{2,1,0:T(8,128)(2,1)S(1)}, u32[]{:S(2)}, u32[]{:S(2)}) collective-permute-start(bf16[3,128,256]{2,1,0:T(8,128)(2,1)S(1)} %get-tuple-element.18.refs_4_.bundle_ref), channel_id=1, source_target_pairs={{0,2},{1,3},{2,0},{3,1},{4,6},{5,7},{6,4},{7,5},{8,10},{9,11},{10,... | collective-permute-start | bytes 589832 | tf_op jit(solution)/shard_map/ppermute | solution.py:18
  15.7 5.1 %collective-permute-start.3 = (bf16[3,128,256]{2,1,0:T(8,128)(2,1)S(1)}, bf16[3,128,256]{2,1,0:T(8,128)(2,1)S(1)}, u32[]{:S(2)}, u32[]{:S(2)}) collective-permute-start(bf16[3,128,256]{2,1,0:T(8,128)(2,1)S(1)} %get-tuple-element.18.refs_4_.bundle_ref), channel_id=1, source_target_pairs={{0,1},{1,0},{2,3},{3,2},{4,5},{5,4},{6,7},{7,6},{8,9},{9,8},{10,11... | collective-permute-start | bytes 589832 | tf_op jit(solution)/shard_map/ppermute | solution.py:18
  15.9 7.1 %collective-permute-start.2 = (bf16[3,128,256]{2,1,0:T(8,128)(2,1)S(1)}, bf16[3,128,256]{2,1,0:T(8,128)(2,1)S(1)}, u32[]{:S(2)}, u32[]{:S(2)}) collective-permute-start(bf16[3,128,256]{2,1,0:T(8,128)(2,1)S(1)} %collective-permute-done.1.refs_2_), channel_id=1, source_target_pairs={{0,8},{8,0},{16,24},{24,16},{1,9},{9,1},{17,25},{25,17},{2,10},{10... | collective-permute-start | bytes 589832 | tf_op jit(solution)/shard_map/ppermute | solution.py:18
  17.4 5.6 %collective-permute-start.9 = (bf16[3,128,256]{2,1,0:T(8,128)(2,1)S(1)}, bf16[3,128,256]{2,1,0:T(8,128)(2,1)S(1)}, u32[]{:S(2)}, u32[]{:S(2)}) collective-permute-start(bf16[3,128,256]{2,1,0:T(8,128)(2,1)S(1)} %collective-permute-done.8.refs_10_), channel_id=1, source_target_pairs={{0,1},{1,0},{2,3},{3,2},{4,5},{5,4},{6,7},{7,6},{8,9},{9,8},{10,11... | collective-permute-start | bytes 589832 | tf_op jit(solution)/shard_map/ppermute | solution.py:18
  19.4 3.6 %collective-permute-start.7 = (bf16[3,128,256]{2,1,0:T(8,128)(2,1)S(1)}, bf16[3,128,256]{2,1,0:T(8,128)(2,1)S(1)}, u32[]{:S(2)}, u32[]{:S(2)}) collective-permute-start(bf16[3,128,256]{2,1,0:T(8,128)(2,1)S(1)} %collective-permute-done.6.refs_8_), channel_id=1, source_target_pairs={{0,1},{1,0},{2,3},{3,2},{4,5},{5,4},{6,7},{7,6},{8,9},{9,8},{10,11... | collective-permute-start | bytes 589832 | tf_op jit(solution)/shard_map/ppermute | solution.py:18
  20.8 2.3 %collective-permute-start.5 = (bf16[3,128,256]{2,1,0:T(8,128)(2,1)S(1)}, bf16[3,128,256]{2,1,0:T(8,128)(2,1)S(1)}, u32[]{:S(2)}, u32[]{:S(2)}) collective-permute-start(bf16[3,128,256]{2,1,0:T(8,128)(2,1)S(1)} %collective-permute-done.4.refs_6_), channel_id=1, source_target_pairs={{0,1},{1,0},{2,3},{3,2},{4,5},{5,4},{6,7},{7,6},{8,9},{9,8},{10,11... | collective-permute-start | bytes 589832 | tf_op jit(solution)/shard_map/ppermute | solution.py:18
  23.7 13.7 %collective-permute-start.11 = (bf16[128,1024]{1,0:T(8,128)(2,1)S(1)}, bf16[128,1024]{1,0:T(8,128)(2,1)S(1)}, u32[]{:S(2)}, u32[]{:S(2)}) collective-permute-start(bf16[128,1024]{1,0:T(8,128)(2,1)S(1)} %get-tuple-element.23), channel_id=1, source_target_pairs={{0,8},{8,0},{16,24},{24,16},{1,9},{9,1},{17,25},{25,17},{2,10},{10... | collective-permute-start | bytes 786440 | tf_op jit(solution)/shard_map/ppermute | solution.py:18
  24.3 7.7 %collective-permute-start.10 = (bf16[128,512]{1,0:T(8,128)(2,1)S(1)}, bf16[128,512]{1,0:T(8,128)(2,1)S(1)}, u32[]{:S(2)}, u32[]{:S(2)}) collective-permute-start(bf16[128,512]{1,0:T(8,128)(2,1)S(1)} %get-tuple-element.22.refs_8_), channel_id=1, source_target_pairs={{0,16},{8,24},{16,0},{24,8},{1,17},{9,25},{17,1},{25,9},{2,18},{10... | collective-permute-start | bytes 393224 | tf_op jit(solution)/shard_map/ppermute | solution.py:18
  27.7 6.1 %collective-permute-start.17 = (bf16[128,512]{1,0:T(8,128)(2,1)S(1)}, bf16[128,512]{1,0:T(8,128)(2,1)S(1)}, u32[]{:S(2)}, u32[]{:S(2)}) collective-permute-start(bf16[128,512]{1,0:T(8,128)(2,1)S(1)} %get-tuple-element.25.refs_0_), channel_id=1, source_target_pairs={{0,4},{1,5},{2,6},{3,7},{4,0},{5,1},{6,2},{7,3},{8,12},{9,13},{10,... | collective-permute-start | bytes 393224 | tf_op jit(solution)/shard_map/ppermute | solution.py:18
  29.2 6.9 %collective-permute-start.15 = (bf16[128,512]{1,0:T(8,128)(2,1)S(1)}, bf16[128,512]{1,0:T(8,128)(2,1)S(1)}, u32[]{:S(2)}, u32[]{:S(2)}) collective-permute-start(bf16[128,512]{1,0:T(8,128)(2,1)S(1)} %get-tuple-element.25.refs_0_), channel_id=1, source_target_pairs={{0,6},{1,7},{2,4},{3,5},{4,2},{5,3},{6,0},{7,1},{8,14},{9,15},{10,... | collective-permute-start | bytes 393224 | tf_op jit(solution)/shard_map/ppermute | solution.py:18
  30.7 6.7 %collective-permute-start.13 = (bf16[128,512]{1,0:T(8,128)(2,1)S(1)}, bf16[128,512]{1,0:T(8,128)(2,1)S(1)}, u32[]{:S(2)}, u32[]{:S(2)}) collective-permute-start(bf16[128,512]{1,0:T(8,128)(2,1)S(1)} %get-tuple-element.25.refs_0_), channel_id=1, source_target_pairs={{0,2},{1,3},{2,0},{3,1},{4,6},{5,7},{6,4},{7,5},{8,10},{9,11},{10,... | collective-permute-start | bytes 393224 | tf_op jit(solution)/shard_map/ppermute | solution.py:18
  32.0 5.9 %collective-permute-start.12 = (bf16[128,512]{1,0:T(8,128)(2,1)S(1)}, bf16[128,512]{1,0:T(8,128)(2,1)S(1)}, u32[]{:S(2)}, u32[]{:S(2)}) collective-permute-start(bf16[128,512]{1,0:T(8,128)(2,1)S(1)} %get-tuple-element.25.refs_0_), channel_id=1, source_target_pairs={{0,1},{1,0},{2,3},{3,2},{4,5},{5,4},{6,7},{7,6},{8,9},{9,8},{10,11... | collective-permute-start | bytes 393224 | tf_op jit(solution)/shard_map/ppermute | solution.py:18
  33.8 4.1 %collective-permute-start.18 = (bf16[128,512]{1,0:T(8,128)(2,1)S(1)}, bf16[128,512]{1,0:T(8,128)(2,1)S(1)}, u32[]{:S(2)}, u32[]{:S(2)}) collective-permute-start(bf16[128,512]{1,0:T(8,128)(2,1)S(1)} %collective-permute-done.17.refs_6_), channel_id=1, source_target_pairs={{0,1},{1,0},{2,3},{3,2},{4,5},{5,4},{6,7},{7,6},{8,9},{9,8},{10,11... | collective-permute-start | bytes 393224 | tf_op jit(solution)/shard_map/ppermute | solution.py:18
  36.1 1.8 %collective-permute-start.16 = (bf16[128,512]{1,0:T(8,128)(2,1)S(1)}, bf16[128,512]{1,0:T(8,128)(2,1)S(1)}, u32[]{:S(2)}, u32[]{:S(2)}) collective-permute-start(bf16[128,512]{1,0:T(8,128)(2,1)S(1)} %collective-permute-done.15.refs_4_), channel_id=1, source_target_pairs={{0,1},{1,0},{2,3},{3,2},{4,5},{5,4},{6,7},{7,6},{8,9},{9,8},{10,11... | collective-permute-start | bytes 393224 | tf_op jit(solution)/shard_map/ppermute | solution.py:18
  37.4 1.3 %collective-permute-start.14 = (bf16[128,512]{1,0:T(8,128)(2,1)S(1)}, bf16[128,512]{1,0:T(8,128)(2,1)S(1)}, u32[]{:S(2)}, u32[]{:S(2)}) collective-permute-start(bf16[128,512]{1,0:T(8,128)(2,1)S(1)} %collective-permute-done.13.refs_2_), channel_id=1, source_target_pairs={{0,1},{1,0},{2,3},{3,2},{4,5},{5,4},{6,7},{7,6},{8,9},{9,8},{10,11... | collective-permute-start | bytes 393224 | tf_op jit(solution)/shard_map/ppermute | solution.py:18
  37.4 11.3 %collective-permute-start.19 = (bf16[128,512]{1,0:T(8,128)(2,1)S(1)}, bf16[128,512]{1,0:T(8,128)(2,1)S(1)}, u32[]{:S(2)}, u32[]{:S(2)}) collective-permute-start(bf16[128,512]{1,0:T(8,128)(2,1)S(1)} %collective-permute-done.10.refs_9_), channel_id=1, source_target_pairs={{0,8},{8,0},{16,24},{24,16},{1,9},{9,1},{17,25},{25,17},{2,10},{10... | collective-permute-start | bytes 393224 | tf_op jit(solution)/shard_map/ppermute | solution.py:18

commit v6 on v5

--- a/solution.py
+++ b/solution.py
@@ -110,8 +110,8 @@
     return jnp.dot(left, right, preferred_element_type=jnp.float32)
 
 
-def pair(weight_ref, plane, k, mu):
-    spots = [pl.ds(pl.multiple_of((plane ^ i) * mu, mu), mu) for i in (k, k + 1)]
+def in_plane(weight_ref, plane, mu):
+    spots = [pl.ds(pl.multiple_of((plane ^ k) * mu, mu), mu) for k in range(weight_ref.shape[1] // mu)]
     return jnp.concatenate([weight_ref[:, spot] for spot in spots], axis=1)
 
 
@@ -137,8 +137,7 @@
     begun = jnp.zeros(begun_ref.shape, jnp.float32)
     for p in range(rest):
         total = jnp.zeros((mu, nu), jnp.float32)
-        for k in range(0, n_plane, 2):
-            total += dot(pair(weight_ref, plane, k, mu), jnp.concatenate([bundles[k][p], bundles[k + 1][p]], axis=0))
+        total += dot(in_plane(weight_ref, plane, mu), jnp.concatenate([ref[p] for ref in bundles], axis=0))
         for q, value in enumerate(halves):
             folded = jnp.sum((total * value).reshape(mu // 8, 8, nu), axis=0)
             own = jnp.sum(jnp.sum(folded, axis=0, keepdims=True), axis=1, keepdims=True)
@@ -206,9 +205,7 @@
     for q in range(cut):
         total = jnp.zeros((mu, nu), jnp.float32)
         columns = slice(q * nu, (q + 1) * nu)
-        for k in range(0, n_plane, 2):
-            both = jnp.concatenate([halves[k][:, columns], halves[k + 1][:, columns]], axis=0)
-            total += dot(pair(weight_ref, plane, k, mu), both)
+        total += dot(in_plane(weight_ref, plane, mu), jnp.concatenate([ref[:, columns] for ref in halves], axis=0))
         rounded = total.astype(first_ref.dtype)
         first_ref[q] = rounded
         for p in range(aux):

time: 50.2 us -> 50.2 us (level)
  no operation moved by 1% of the time
where the time goes in v6:
time: 50.2 us; the launch traced here: 50 us
  starting transfers between devices  18.7 us (37%)
  waiting for transfers between devices  17.1 us (34%)
  blocking collectives  9.37 us (19%)
  Pallas kernels  3.63 us (7%)
  between operations  1.32 us (3%)
    ppermute x20, starting transfers between devices, flip(): return lax.ppermute(value, axes, [(i, i ^ mask) for i in range(count)])  18.7 us
    ppermute x20, waiting for transfers between devices, flip(): return lax.ppermute(value, axes, [(i, i ^ mask) for i in range(count)])  17.1 us
    all_to_all x1, blocking collectives, on_device(): lax.all_to_all(share, EVERY, 0, 0)  9.37 us
    pallas_call x1, Pallas kernels, dress(): pl.pallas_call(functools.partial(dress_kernel, n_row), out_shape=(jax.Sha...  1.3 us
    pallas_call x1, Pallas kernels, place(): pl.pallas_call(functools.partial(place_kernel, nu // tile), out_shape=[ja...  1.07 us
  transfers between devices with their start and end apart: 20, of which 10 were waited for; matrix products, arithmetic and copies ran while one was open for 0% of the time, Pallas kernels for 1%

profile of v6, /device:TPU:0, one launch (start us, length us, event | category | flops | bytes accessed | tf_op | source)
XLA Modules:
  0.0 50.0 jit_solution(8273313511679506873)
XLA Ops:
  1.3 1.1 %place.1 = (bf16[3,128,256]{2,1,0:T(8,128)(2,1)S(1)}, bf16[3,128,256]{2,1,0:T(8,128)(2,1)S(1)}) custom-call(s32[1]{0:T(128)S(6)} %copy.7.counts_ref, s32[2]{0:T(128)} %pairs_any.1, bf16[2,4,128,128]{3,2,1,0:T(8,128)(2,1)} %tiles_any.1, bf16[128,256]{1,0:T(8,128)(2,1)} %weight_any.1, bf16[128,256]{1,0:T(8,128)(2,1)} %column_any.1), custom_call_target="tpu_custom_call" | custom-call | bytes 786432 | tf_op jit(solution)/shard_map/place/pallas_call | solution.py:93
  2.4 4.1 %collective-permute-start.1 = (bf16[3,128,256]{2,1,0:T(8,128)(2,1)S(1)}, bf16[3,128,256]{2,1,0:T(8,128)(2,1)S(1)}, u32[]{:S(2)}, u32[]{:S(2)}) collective-permute-start(bf16[3,128,256]{2,1,0:T(8,128)(2,1)S(1)} %get-tuple-element.17.refs_0_.line_ref), channel_id=1, source_target_pairs={{0,16},{8,24},{16,0},{24,8},{1,17},{9,25},{17,1},{25,9},{2,18},{10... | collective-permute-start | bytes 589832 | tf_op jit(solution)/shard_map/ppermute | solution.py:18
  6.5 1.6 %collective-permute-start = (bf16[3,128,256]{2,1,0:T(8,128)(2,1)S(1)}, bf16[3,128,256]{2,1,0:T(8,128)(2,1)S(1)}, u32[]{:S(2)}, u32[]{:S(2)}) collective-permute-start(bf16[3,128,256]{2,1,0:T(8,128)(2,1)S(1)} %get-tuple-element.17.refs_0_.line_ref), channel_id=1, source_target_pairs={{0,8},{8,0},{16,24},{24,16},{1,9},{9,1},{17,25},{25,17},{2,10},{10... | collective-permute-start | bytes 589832 | tf_op jit(solution)/shard_map/ppermute | solution.py:18
  8.0 1.5 %collective-permute-start.8 = (bf16[3,128,256]{2,1,0:T(8,128)(2,1)S(1)}, bf16[3,128,256]{2,1,0:T(8,128)(2,1)S(1)}, u32[]{:S(2)}, u32[]{:S(2)}) collective-permute-start(bf16[3,128,256]{2,1,0:T(8,128)(2,1)S(1)} %get-tuple-element.18.refs_4_.bundle_ref), channel_id=1, source_target_pairs={{0,4},{1,5},{2,6},{3,7},{4,0},{5,1},{6,2},{7,3},{8,12},{9,13},{10,... | collective-permute-start | bytes 589832 | tf_op jit(solution)/shard_map/ppermute | solution.py:18
  9.5 1.5 %collective-permute-start.6 = (bf16[3,128,256]{2,1,0:T(8,128)(2,1)S(1)}, bf16[3,128,256]{2,1,0:T(8,128)(2,1)S(1)}, u32[]{:S(2)}, u32[]{:S(2)}) collective-permute-start(bf16[3,128,256]{2,1,0:T(8,128)(2,1)S(1)} %get-tuple-element.18.refs_4_.bundle_ref), channel_id=1, source_target_pairs={{0,6},{1,7},{2,4},{3,5},{4,2},{5,3},{6,0},{7,1},{8,14},{9,15},{10,... | collective-permute-start | bytes 589832 | tf_op jit(solution)/shard_map/ppermute | solution.py:18
  11.5 4.2 %collective-permute-done.1.refs_2_ = bf16[3,128,256]{2,1,0:T(8,128)(2,1)S(1)} collective-permute-done((bf16[3,128,256]{2,1,0:T(8,128)(2,1)S(1)}, bf16[3,128,256]{2,1,0:T(8,128)(2,1)S(1)}, u32[]{:S(2)}, u32[]{:S(2)}) %collective-permute-start.1) | collective-permute-done | bytes 196640 | tf_op jit(solution)/shard_map/ppermute | solution.py:18
  15.9 1.5 %collective-permute-start.2 = (bf16[3,128,256]{2,1,0:T(8,128)(2,1)S(1)}, bf16[3,128,256]{2,1,0:T(8,128)(2,1)S(1)}, u32[]{:S(2)}, u32[]{:S(2)}) collective-permute-start(bf16[3,128,256]{2,1,0:T(8,128)(2,1)S(1)} %collective-permute-done.1.refs_2_), channel_id=1, source_target_pairs={{0,8},{8,0},{16,24},{24,16},{1,9},{9,1},{17,25},{25,17},{2,10},{10... | collective-permute-start | bytes 589832 | tf_op jit(solution)/shard_map/ppermute | solution.py:18
  17.4 2.0 %collective-permute-done.6.refs_8_ = bf16[3,128,256]{2,1,0:T(8,128)(2,1)S(1)} collective-permute-done((bf16[3,128,256]{2,1,0:T(8,128)(2,1)S(1)}, bf16[3,128,256]{2,1,0:T(8,128)(2,1)S(1)}, u32[]{:S(2)}, u32[]{:S(2)}) %collective-permute-start.6) | collective-permute-done | bytes 196640 | tf_op jit(solution)/shard_map/ppermute | solution.py:18
  19.4 1.4 %collective-permute-done.4.refs_6_ = bf16[3,128,256]{2,1,0:T(8,128)(2,1)S(1)} collective-permute-done((bf16[3,128,256]{2,1,0:T(8,128)(2,1)S(1)}, bf16[3,128,256]{2,1,0:T(8,128)(2,1)S(1)}, u32[]{:S(2)}, u32[]{:S(2)}) %collective-permute-start.4) | collective-permute-done | bytes 196640 | tf_op jit(solution)/shard_map/ppermute | solution.py:18
  20.8 2.2 %collective-permute-done.2.refs_3_ = bf16[3,128,256]{2,1,0:T(8,128)(2,1)S(1)} collective-permute-done((bf16[3,128,256]{2,1,0:T(8,128)(2,1)S(1)}, bf16[3,128,256]{2,1,0:T(8,128)(2,1)S(1)}, u32[]{:S(2)}, u32[]{:S(2)}) %collective-permute-start.2) | collective-permute-done | bytes 196640 | tf_op jit(solution)/shard_map/ppermute | solution.py:18
  23.0 0.7 %mix.1 = (bf16[128,512]{1,0:T(8,128)(2,1)S(1)}, bf16[128,512]{1,0:T(8,128)(2,1)S(1)}, bf16[128,1024]{1,0:T(8,128)(2,1)S(1)}, bf16[128,1024]{1,0:T(8,128)(2,1)S(1...) custom-call(bf16[3,128,256]{2,1,0:T(8,128)(2,1)S(1)} %get-tuple-element.17.refs_0_.line_ref, ...), custom_call_target="tpu_custom_call" | custom-call | flops 268435456 | bytes 2097152 | tf_op jit(solution)/shard_map/mix/pallas_call | solution.py:162
  23.7 0.6 %collective-permute-start.11 = (bf16[128,1024]{1,0:T(8,128)(2,1)S(1)}, bf16[128,1024]{1,0:T(8,128)(2,1)S(1)}, u32[]{:S(2)}, u32[]{:S(2)}) collective-permute-start(bf16[128,1024]{1,0:T(8,128)(2,1)S(1)} %get-tuple-element.23), channel_id=1, source_target_pairs={{0,8},{8,0},{16,24},{24,16},{1,9},{9,1},{17,25},{25,17},{2,10},{10... | collective-permute-start | bytes 786440 | tf_op jit(solution)/shard_map/ppermute | solution.py:18
  24.3 3.4 %collective-permute-start.10 = (bf16[128,512]{1,0:T(8,128)(2,1)S(1)}, bf16[128,512]{1,0:T(8,128)(2,1)S(1)}, u32[]{:S(2)}, u32[]{:S(2)}) collective-permute-start(bf16[128,512]{1,0:T(8,128)(2,1)S(1)} %get-tuple-element.22.refs_8_), channel_id=1, source_target_pairs={{0,16},{8,24},{16,0},{24,8},{1,17},{9,25},{17,1},{25,9},{2,18},{10... | collective-permute-start | bytes 393224 | tf_op jit(solution)/shard_map/ppermute | solution.py:18
  27.7 1.5 %collective-permute-start.17 = (bf16[128,512]{1,0:T(8,128)(2,1)S(1)}, bf16[128,512]{1,0:T(8,128)(2,1)S(1)}, u32[]{:S(2)}, u32[]{:S(2)}) collective-permute-start(bf16[128,512]{1,0:T(8,128)(2,1)S(1)} %get-tuple-element.25.refs_0_), channel_id=1, source_target_pairs={{0,4},{1,5},{2,6},{3,7},{4,0},{5,1},{6,2},{7,3},{8,12},{9,13},{10,... | collective-permute-start | bytes 393224 | tf_op jit(solution)/shard_map/ppermute | solution.py:18
  29.2 1.5 %collective-permute-start.15 = (bf16[128,512]{1,0:T(8,128)(2,1)S(1)}, bf16[128,512]{1,0:T(8,128)(2,1)S(1)}, u32[]{:S(2)}, u32[]{:S(2)}) collective-permute-start(bf16[128,512]{1,0:T(8,128)(2,1)S(1)} %get-tuple-element.25.refs_0_), channel_id=1, source_target_pairs={{0,6},{1,7},{2,4},{3,5},{4,2},{5,3},{6,0},{7,1},{8,14},{9,15},{10,... | collective-permute-start | bytes 393224 | tf_op jit(solution)/shard_map/ppermute | solution.py:18
  30.7 0.5 %collective-permute-start.13 = (bf16[128,512]{1,0:T(8,128)(2,1)S(1)}, bf16[128,512]{1,0:T(8,128)(2,1)S(1)}, u32[]{:S(2)}, u32[]{:S(2)}) collective-permute-start(bf16[128,512]{1,0:T(8,128)(2,1)S(1)} %get-tuple-element.25.refs_0_), channel_id=1, source_target_pairs={{0,2},{1,3},{2,0},{3,1},{4,6},{5,7},{6,4},{7,5},{8,10},{9,11},{10,... | collective-permute-start | bytes 393224 | tf_op jit(solution)/shard_map/ppermute | solution.py:18
  31.2 0.8 %collective-permute-done.10.refs_9_ = bf16[128,512]{1,0:T(8,128)(2,1)S(1)} collective-permute-done((bf16[128,512]{1,0:T(8,128)(2,1)S(1)}, bf16[128,512]{1,0:T(8,128)(2,1)S(1)}, u32[]{:S(2)}, u32[]{:S(2)}) %collective-permute-start.10) | collective-permute-done | bytes 131104 | tf_op jit(solution)/shard_map/ppermute | solution.py:18
  32.0 1.7 %collective-permute-done.17.refs_6_ = bf16[128,512]{1,0:T(8,128)(2,1)S(1)} collective-permute-done((bf16[128,512]{1,0:T(8,128)(2,1)S(1)}, bf16[128,512]{1,0:T(8,128)(2,1)S(1)}, u32[]{:S(2)}, u32[]{:S(2)}) %collective-permute-start.17) | collective-permute-done | bytes 131104 | tf_op jit(solution)/shard_map/ppermute | solution.py:18
  33.7 2.4 %collective-permute-done.15.refs_4_ = bf16[128,512]{1,0:T(8,128)(2,1)S(1)} collective-permute-done((bf16[128,512]{1,0:T(8,128)(2,1)S(1)}, bf16[128,512]{1,0:T(8,128)(2,1)S(1)}, u32[]{:S(2)}, u32[]{:S(2)}) %collective-permute-start.15) | collective-permute-done | bytes 131104 | tf_op jit(solution)/shard_map/ppermute | solution.py:18
  36.1 1.3 %collective-permute-done.13.refs_2_ = bf16[128,512]{1,0:T(8,128)(2,1)S(1)} collective-permute-done((bf16[128,512]{1,0:T(8,128)(2,1)S(1)}, bf16[128,512]{1,0:T(8,128)(2,1)S(1)}, u32[]{:S(2)}, u32[]{:S(2)}) %collective-permute-start.13) | collective-permute-done | bytes 131104 | tf_op jit(solution)/shard_map/ppermute | solution.py:18
  37.9 0.8 %collective-permute-done.14.refs_3_ = bf16[128,512]{1,0:T(8,128)(2,1)S(1)} collective-permute-done((bf16[128,512]{1,0:T(8,128)(2,1)S(1)}, bf16[128,512]{1,0:T(8,128)(2,1)S(1)}, u32[]{:S(2)}, u32[]{:S(2)}) %collective-permute-start.14) | collective-permute-done | bytes 131104 | tf_op jit(solution)/shard_map/ppermute | solution.py:18
  38.8 0.6 %polar_share.1 = (bf16[2,128,256]{2,1,0:T(8,128)(2,1)S(1)}, f32[2,128,256]{2,1,0:T(8,128)S(1)}, f32[32,1,128]{2,1,0:T(1,128)S(1)}) custom-call(f32[1,128]{1,0:T(1,128)S(1)} %get-tuple-element.20.begun_ref, bf16[128,1024]{1,0:T(8,128)(2,1)S(1)} %get-tuple-element.21.weight_ref, bf16[1024,256]{1,0:T(8,128)(2,1)S(1)} %get-tuple-element.19.panel_ref, ...), custom_call_target="tpu_custom_call" | custom-call | flops 268435456 | bytes 4194304 | tf_op jit(solution)/shard_map/polar_share/pallas_call | solution.py:235
  39.4 9.4 %all_to_all.5.shares_ref = f32[32,1,128]{2,1,0:T(1,128)S(1)} all-to-all(f32[32,1,128]{2,1,0:T(1,128)S(1)} %get-tuple-element.28), channel_id=1, replica_groups=mesh['row'=4,'col'=2,'rep'=4] {'row','col','rep'}, dimensions={0} | all-to-all | bytes 32768 | tf_op jit(solution)/shard_map/all_to_all | solution.py:311
  48.7 1.3 %dress.1 = (bf16[128,4,256]{2,1,0:T(4,128)(2,1)}, f32[4,4]{1,0:T(4,128)}) custom-call(bf16[1024,256]{1,0:T(8,128)(2,1)S(1)} %get-tuple-element.19.panel_ref, bf16[2,128,256]{2,1,0:T(8,128)(2,1)S(1)} %get-tuple-element.26.first_ref, f32[2,128,256]{2,1,0:T(8,128)S(1)} %get-tuple-element.27.part_ref, f32[32,1,128]{2,1,0:T(1,128)S(1)} %all_to_all.5.shares_ref, ...), custom_call_target="tpu_custom_call" | custom-call | flops 67108864 | bytes 1048576 | tf_op jit(solution)/shard_map/dress/pallas_call | solution.py:275
  (21 shorter events, 1.2 us)
Async XLA Ops:
  2.4 13.3 %collective-permute-start.1 = (bf16[3,128,256]{2,1,0:T(8,128)(2,1)S(1)}, bf16[3,128,256]{2,1,0:T(8,128)(2,1)S(1)}, u32[]{:S(2)}, u32[]{:S(2)}) collective-permute-start(bf16[3,128,256]{2,1,0:T(8,128)(2,1)S(1)} %get-tuple-element.17.refs_0_.line_ref), channel_id=1, source_target_pairs={{0,16},{8,24},{16,0},{24,8},{1,17},{9,25},{17,1},{25,9},{2,18},{10... | collective-permute-start | bytes 589832 | tf_op jit(solution)/shard_map/ppermute | solution.py:18
  6.5 9.4 %collective-permute-start = (bf16[3,128,256]{2,1,0:T(8,128)(2,1)S(1)}, bf16[3,128,256]{2,1,0:T(8,128)(2,1)S(1)}, u32[]{:S(2)}, u32[]{:S(2)}) collective-permute-start(bf16[3,128,256]{2,1,0:T(8,128)(2,1)S(1)} %get-tuple-element.17.refs_0_.line_ref), channel_id=1, source_target_pairs={{0,8},{8,0},{16,24},{24,16},{1,9},{9,1},{17,25},{25,17},{2,10},{10... | collective-permute-start | bytes 589832 | tf_op jit(solution)/shard_map/ppermute | solution.py:18
  8.0 9.3 %collective-permute-start.8 = (bf16[3,128,256]{2,1,0:T(8,128)(2,1)S(1)}, bf16[3,128,256]{2,1,0:T(8,128)(2,1)S(1)}, u32[]{:S(2)}, u32[]{:S(2)}) collective-permute-start(bf16[3,128,256]{2,1,0:T(8,128)(2,1)S(1)} %get-tuple-element.18.refs_4_.bundle_ref), channel_id=1, source_target_pairs={{0,4},{1,5},{2,6},{3,7},{4,0},{5,1},{6,2},{7,3},{8,12},{9,13},{10,... | collective-permute-start | bytes 589832 | tf_op jit(solution)/shard_map/ppermute | solution.py:18
  9.5 9.9 %collective-permute-start.6 = (bf16[3,128,256]{2,1,0:T(8,128)(2,1)S(1)}, bf16[3,128,256]{2,1,0:T(8,128)(2,1)S(1)}, u32[]{:S(2)}, u32[]{:S(2)}) collective-permute-start(bf16[3,128,256]{2,1,0:T(8,128)(2,1)S(1)} %get-tuple-element.18.refs_4_.bundle_ref), channel_id=1, source_target_pairs={{0,6},{1,7},{2,4},{3,5},{4,2},{5,3},{6,0},{7,1},{8,14},{9,15},{10,... | collective-permute-start | bytes 589832 | tf_op jit(solution)/shard_map/ppermute | solution.py:18
  11.0 9.7 %collective-permute-start.4 = (bf16[3,128,256]{2,1,0:T(8,128)(2,1)S(1)}, bf16[3,128,256]{2,1,0:T(8,128)(2,1)S(1)}, u32[]{:S(2)}, u32[]{:S(2)}) collective-permute-start(bf16[3,128,256]{2,1,0:T(8,128)(2,1)S(1)} %get-tuple-element.18.refs_4_.bundle_ref), channel_id=1, source_target_pairs={{0,2},{1,3},{2,0},{3,1},{4,6},{5,7},{6,4},{7,5},{8,10},{9,11},{10,... | collective-permute-start | bytes 589832 | tf_op jit(solution)/shard_map/ppermute | solution.py:18
  15.7 5.1 %collective-permute-start.3 = (bf16[3,128,256]{2,1,0:T(8,128)(2,1)S(1)}, bf16[3,128,256]{2,1,0:T(8,128)(2,1)S(1)}, u32[]{:S(2)}, u32[]{:S(2)}) collective-permute-start(bf16[3,128,256]{2,1,0:T(8,128)(2,1)S(1)} %get-tuple-element.18.refs_4_.bundle_ref), channel_id=1, source_target_pairs={{0,1},{1,0},{2,3},{3,2},{4,5},{5,4},{6,7},{7,6},{8,9},{9,8},{10,11... | collective-permute-start | bytes 589832 | tf_op jit(solution)/shard_map/ppermute | solution.py:18
  15.9 7.1 %collective-permute-start.2 = (bf16[3,128,256]{2,1,0:T(8,128)(2,1)S(1)}, bf16[3,128,256]{2,1,0:T(8,128)(2,1)S(1)}, u32[]{:S(2)}, u32[]{:S(2)}) collective-permute-start(bf16[3,128,256]{2,1,0:T(8,128)(2,1)S(1)} %collective-permute-done.1.refs_2_), channel_id=1, source_target_pairs={{0,8},{8,0},{16,24},{24,16},{1,9},{9,1},{17,25},{25,17},{2,10},{10... | collective-permute-start | bytes 589832 | tf_op jit(solution)/shard_map/ppermute | solution.py:18
  17.4 5.6 %collective-permute-start.9 = (bf16[3,128,256]{2,1,0:T(8,128)(2,1)S(1)}, bf16[3,128,256]{2,1,0:T(8,128)(2,1)S(1)}, u32[]{:S(2)}, u32[]{:S(2)}) collective-permute-start(bf16[3,128,256]{2,1,0:T(8,128)(2,1)S(1)} %collective-permute-done.8.refs_10_), channel_id=1, source_target_pairs={{0,1},{1,0},{2,3},{3,2},{4,5},{5,4},{6,7},{7,6},{8,9},{9,8},{10,11... | collective-permute-start | bytes 589832 | tf_op jit(solution)/shard_map/ppermute | solution.py:18
  19.4 3.6 %collective-permute-start.7 = (bf16[3,128,256]{2,1,0:T(8,128)(2,1)S(1)}, bf16[3,128,256]{2,1,0:T(8,128)(2,1)S(1)}, u32[]{:S(2)}, u32[]{:S(2)}) collective-permute-start(bf16[3,128,256]{2,1,0:T(8,128)(2,1)S(1)} %collective-permute-done.6.refs_8_), channel_id=1, source_target_pairs={{0,1},{1,0},{2,3},{3,2},{4,5},{5,4},{6,7},{7,6},{8,9},{9,8},{10,11... | collective-permute-start | bytes 589832 | tf_op jit(solution)/shard_map/ppermute | solution.py:18
  20.8 2.3 %collective-permute-start.5 = (bf16[3,128,256]{2,1,0:T(8,128)(2,1)S(1)}, bf16[3,128,256]{2,1,0:T(8,128)(2,1)S(1)}, u32[]{:S(2)}, u32[]{:S(2)}) collective-permute-start(bf16[3,128,256]{2,1,0:T(8,128)(2,1)S(1)} %collective-permute-done.4.refs_6_), channel_id=1, source_target_pairs={{0,1},{1,0},{2,3},{3,2},{4,5},{5,4},{6,7},{7,6},{8,9},{9,8},{10,11... | collective-permute-start | bytes 589832 | tf_op jit(solution)/shard_map/ppermute | solution.py:18
  23.7 13.7 %collective-permute-start.11 = (bf16[128,1024]{1,0:T(8,128)(2,1)S(1)}, bf16[128,1024]{1,0:T(8,128)(2,1)S(1)}, u32[]{:S(2)}, u32[]{:S(2)}) collective-permute-start(bf16[128,1024]{1,0:T(8,128)(2,1)S(1)} %get-tuple-element.23), channel_id=1, source_target_pairs={{0,8},{8,0},{16,24},{24,16},{1,9},{9,1},{17,25},{25,17},{2,10},{10... | collective-permute-start | bytes 786440 | tf_op jit(solution)/shard_map/ppermute | solution.py:18
  24.3 7.7 %collective-permute-start.10 = (bf16[128,512]{1,0:T(8,128)(2,1)S(1)}, bf16[128,512]{1,0:T(8,128)(2,1)S(1)}, u32[]{:S(2)}, u32[]{:S(2)}) collective-permute-start(bf16[128,512]{1,0:T(8,128)(2,1)S(1)} %get-tuple-element.22.refs_8_), channel_id=1, source_target_pairs={{0,16},{8,24},{16,0},{24,8},{1,17},{9,25},{17,1},{25,9},{2,18},{10... | collective-permute-start | bytes 393224 | tf_op jit(solution)/shard_map/ppermute | solution.py:18
  27.7 6.0 %collective-permute-start.17 = (bf16[128,512]{1,0:T(8,128)(2,1)S(1)}, bf16[128,512]{1,0:T(8,128)(2,1)S(1)}, u32[]{:S(2)}, u32[]{:S(2)}) collective-permute-start(bf16[128,512]{1,0:T(8,128)(2,1)S(1)} %get-tuple-element.25.refs_0_), channel_id=1, source_target_pairs={{0,4},{1,5},{2,6},{3,7},{4,0},{5,1},{6,2},{7,3},{8,12},{9,13},{10,... | collective-permute-start | bytes 393224 | tf_op jit(solution)/shard_map/ppermute | solution.py:18
  29.2 6.9 %collective-permute-start.15 = (bf16[128,512]{1,0:T(8,128)(2,1)S(1)}, bf16[128,512]{1,0:T(8,128)(2,1)S(1)}, u32[]{:S(2)}, u32[]{:S(2)}) collective-permute-start(bf16[128,512]{1,0:T(8,128)(2,1)S(1)} %get-tuple-element.25.refs_0_), channel_id=1, source_target_pairs={{0,6},{1,7},{2,4},{3,5},{4,2},{5,3},{6,0},{7,1},{8,14},{9,15},{10,... | collective-permute-start | bytes 393224 | tf_op jit(solution)/shard_map/ppermute | solution.py:18
  30.7 6.7 %collective-permute-start.13 = (bf16[128,512]{1,0:T(8,128)(2,1)S(1)}, bf16[128,512]{1,0:T(8,128)(2,1)S(1)}, u32[]{:S(2)}, u32[]{:S(2)}) collective-permute-start(bf16[128,512]{1,0:T(8,128)(2,1)S(1)} %get-tuple-element.25.refs_0_), channel_id=1, source_target_pairs={{0,2},{1,3},{2,0},{3,1},{4,6},{5,7},{6,4},{7,5},{8,10},{9,11},{10,... | collective-permute-start | bytes 393224 | tf_op jit(solution)/shard_map/ppermute | solution.py:18
  32.0 5.9 %collective-permute-start.12 = (bf16[128,512]{1,0:T(8,128)(2,1)S(1)}, bf16[128,512]{1,0:T(8,128)(2,1)S(1)}, u32[]{:S(2)}, u32[]{:S(2)}) collective-permute-start(bf16[128,512]{1,0:T(8,128)(2,1)S(1)} %get-tuple-element.25.refs_0_), channel_id=1, source_target_pairs={{0,1},{1,0},{2,3},{3,2},{4,5},{5,4},{6,7},{7,6},{8,9},{9,8},{10,11... | collective-permute-start | bytes 393224 | tf_op jit(solution)/shard_map/ppermute | solution.py:18
  33.7 4.2 %collective-permute-start.18 = (bf16[128,512]{1,0:T(8,128)(2,1)S(1)}, bf16[128,512]{1,0:T(8,128)(2,1)S(1)}, u32[]{:S(2)}, u32[]{:S(2)}) collective-permute-start(bf16[128,512]{1,0:T(8,128)(2,1)S(1)} %collective-permute-done.17.refs_6_), channel_id=1, source_target_pairs={{0,1},{1,0},{2,3},{3,2},{4,5},{5,4},{6,7},{7,6},{8,9},{9,8},{10,11... | collective-permute-start | bytes 393224 | tf_op jit(solution)/shard_map/ppermute | solution.py:18
  36.1 1.8 %collective-permute-start.16 = (bf16[128,512]{1,0:T(8,128)(2,1)S(1)}, bf16[128,512]{1,0:T(8,128)(2,1)S(1)}, u32[]{:S(2)}, u32[]{:S(2)}) collective-permute-start(bf16[128,512]{1,0:T(8,128)(2,1)S(1)} %collective-permute-done.15.refs_4_), channel_id=1, source_target_pairs={{0,1},{1,0},{2,3},{3,2},{4,5},{5,4},{6,7},{7,6},{8,9},{9,8},{10,11... | collective-permute-start | bytes 393224 | tf_op jit(solution)/shard_map/ppermute | solution.py:18
  37.4 1.3 %collective-permute-start.14 = (bf16[128,512]{1,0:T(8,128)(2,1)S(1)}, bf16[128,512]{1,0:T(8,128)(2,1)S(1)}, u32[]{:S(2)}, u32[]{:S(2)}) collective-permute-start(bf16[128,512]{1,0:T(8,128)(2,1)S(1)} %collective-permute-done.13.refs_2_), channel_id=1, source_target_pairs={{0,1},{1,0},{2,3},{3,2},{4,5},{5,4},{6,7},{7,6},{8,9},{9,8},{10,11... | collective-permute-start | bytes 393224 | tf_op jit(solution)/shard_map/ppermute | solution.py:18
  37.4 11.3 %collective-permute-start.19 = (bf16[128,512]{1,0:T(8,128)(2,1)S(1)}, bf16[128,512]{1,0:T(8,128)(2,1)S(1)}, u32[]{:S(2)}, u32[]{:S(2)}) collective-permute-start(bf16[128,512]{1,0:T(8,128)(2,1)S(1)} %collective-permute-done.10.refs_9_), channel_id=1, source_target_pairs={{0,8},{8,0},{16,24},{24,16},{1,9},{9,1},{17,25},{25,17},{2,10},{10... | collective-permute-start | bytes 393224 | tf_op jit(solution)/shard_map/ppermute | solution.py:18
